TPU v7x, 32 devices: a whole 2x2x4 slice. The times are simulated.
32 devices in a mesh: expert: 2 (over x), tensor: 4 (over y, core), dp: 4 (over z).
Axes of the slice: x: 2, y: 2, z: 4, core: 2. Of those that a mesh axis runs over, the one named last changes fastest.
Arguments:
- tokens: bfloat16 [4096, 1024], P(('expert', 'dp')), may hold values from -6 to 6
- cotangent: bfloat16 [4096, 1024], P(('expert', 'dp')), may hold values from -6 to 6
- seq_lengths: int32 [2, 4], P('expert'), may hold values from 1 to 512, 1536 in all within a row
- deal_order: int32 [2, 4], P('expert'), may hold values from 0 to 3, each once within a row
- routes: int32 [4096, 8], P(('expert', 'dp')), may hold values from 0 to 31, all different within a row
- slot_order: int32 [8, 4096], P(('expert', 'dp')), may hold values from 0 to 4095, each once within a row
- first_gain: bfloat16 [1024], replicated, may hold values from 0.5 to 1.5
- w_query: bfloat16 [1024, 1024], P(None, 'tensor'), may hold values from -0.1875 to 0.1875
- w_key: bfloat16 [1024, 512], P(None, 'tensor'), may hold values from -0.1875 to 0.1875
- w_value: bfloat16 [1024, 512], P(None, 'tensor'), may hold values from -0.1875 to 0.1875
- w_out: bfloat16 [1024, 1024], P('tensor'), may hold values from -3 to 3
- second_gain: bfloat16 [1024], replicated, may hold values from 0.5 to 1.5
- w_router: bfloat16 [1024, 32], replicated, may hold values from -0.09375 to 0.09375
- w_gate: bfloat16 [32, 1024, 512], P('expert', None, 'tensor'), may hold values from -0.1875 to 0.1875
- w_up: bfloat16 [32, 1024, 512], P('expert', None, 'tensor'), may hold values from -0.1875 to 0.1875
- w_down: bfloat16 [32, 512, 1024], P('expert', 'tensor'), may hold values from -1 to 1
Outputs:
- block_out: bfloat16 [4096, 1024], P(('expert', 'dp'), 'tensor')
- input_grad: bfloat16 [4096, 1024], P(('expert', 'dp'), 'tensor')
- first_gain_grad: float32 [1024], replicated
- query_grad: float32 [1024, 1024], P(None, 'tensor')
- key_grad: float32 [1024, 512], P(None, 'tensor')
- value_grad: float32 [1024, 512], P(None, 'tensor')
- out_grad: float32 [1024, 1024], P('tensor')
- second_gain_grad: float32 [1024], replicated
- router_grad: float32 [1024, 32], replicated
- gate_grad: float32 [32, 1024, 512], P('expert', None, 'tensor')
- up_grad: float32 [32, 1024, 512], P('expert', None, 'tensor')
- down_grad: float32 [32, 512, 1024], P('expert', 'tensor')
Inputs may be any that keep to these rules, and one draw needn't show every extreme that they name: `seq_lengths`: in each row the lengths sum to 1536. `deal_order`: each row is a permutation of the 4 sequences of one group. `routes`: a row's 8 experts are distinct. `slot_order`: each row is a permutation of the 4096 entries of one unit.
All inputs are finite; a program needn't handle non-finite values.
Results may differ from a plain program's by a relative error of at most 0.018.
Values may be sent and summed in bfloat16 or wider, within the bound.
A program may use at most 192 MiB of HBM per device.

v0:
```python
import math

import jax
import jax.numpy as jnp
from jax import lax
from jax.sharding import PartitionSpec as P

HEADS = 16
KV_HEADS = 8
HEAD_DIM = 64
EXPERTS = 32
TOP = 8
SLOT = 512


EPS = 1e-06
THETA = 10000.0
NEG = -1e30


def rms_scale(values):
    return lax.rsqrt(jnp.mean(values * values, axis=-1, keepdims=True) + EPS)


def rotate(values, direction):
    row_count, head_count, head_width = values.shape
    halfway = head_width // 2
    places = (jnp.arange(row_count, dtype=jnp.int32) % SLOT).astype(jnp.float32)
    spread = THETA ** (-2.0 * jnp.arange(halfway, dtype=jnp.float32) / head_width)
    angles = places[:, None] * spread[None, :]
    cosine = jnp.cos(angles)[:, None, :]
    sine_part = direction * jnp.sin(angles)[:, None, :]
    lower_half = values[..., :halfway]
    upper_half = values[..., halfway:]
    return jnp.concatenate(
        [
            lower_half * cosine - upper_half * sine_part,
            upper_half * cosine + lower_half * sine_part,
        ],
        axis=-1,
    )


def route_tables(routes, entry_order, live_rows, capacity):
    token_count, route_count = routes.shape
    entry_count = token_count * route_count
    slot_count = EXPERTS * capacity
    experts_flat = routes.reshape(entry_count)
    entry_live = jnp.repeat(live_rows, route_count, total_repeat_length=entry_count)
    ordered = experts_flat[entry_order]
    ordered_live = entry_live[entry_order]
    onehot = (
        (ordered[:, None] == jnp.arange(EXPERTS, dtype=jnp.int32)[None, :]) & ordered_live[:, None]
    ).astype(jnp.int32)
    before = jnp.cumsum(onehot, axis=0) - onehot
    ranked = jnp.sum(before * onehot, axis=1)
    placing = jnp.zeros((entry_count,), jnp.int32).at[entry_order].set(ranked)
    kept_entry = entry_live & (placing < capacity)
    target = jnp.where(kept_entry, experts_flat * capacity + placing, slot_count)
    filler = (
        jnp.full((slot_count,), -1, jnp.int32)
        .at[target]
        .set(jnp.arange(entry_count, dtype=jnp.int32), mode="drop")
    )
    filled = filler >= 0
    source_entry = jnp.maximum(filler, 0)
    return (
        kept_entry.reshape(token_count, route_count),
        jnp.minimum(target, slot_count - 1).reshape(token_count, route_count),
        filled,
        source_entry // route_count,
        source_entry,
    )


def slot_scores(queries, key_rows, length):
    score_scale = 1.0 / math.sqrt(HEAD_DIM)
    scaled = (
        jnp.einsum("qkgd,jkd->kgqj", queries, key_rows, preferred_element_type=jnp.float32)
        * score_scale
    )
    places = jnp.arange(SLOT, dtype=jnp.int32)
    allowed = (places[None, :] <= places[:, None]) & (places[None, :] < length)
    return jnp.where(allowed[None, None], scaled, NEG)


def forward_slot(packed):
    queries, key_rows, value_rows, length = packed
    scores = slot_scores(queries, key_rows, length)
    highest = jnp.max(scores, axis=-1, keepdims=True)
    weights = jnp.exp(scores - highest)
    totals = jnp.sum(weights, axis=-1, keepdims=True)
    probability = (weights / totals).astype(jnp.bfloat16)
    mixed_rows = jnp.einsum(
        "kgqj,jkd->qkgd", probability, value_rows, preferred_element_type=jnp.float32
    )
    return (mixed_rows, highest + jnp.log(totals))


def backward_slot(packed):
    queries, key_rows, value_rows, grad_rows, logsum, length = packed
    score_scale = 1.0 / math.sqrt(HEAD_DIM)
    scores = slot_scores(queries, key_rows, length)
    probability = jnp.exp(scores - logsum)
    grad_prob = jnp.einsum(
        "qkgd,jkd->kgqj", grad_rows, value_rows, preferred_element_type=jnp.float32
    )
    center = jnp.sum(probability * grad_prob, axis=-1, keepdims=True)
    grad_score = (probability * (grad_prob - center)).astype(jnp.bfloat16)
    grad_query = (
        jnp.einsum("kgqj,jkd->qkgd", grad_score, key_rows, preferred_element_type=jnp.float32)
        * score_scale
    )
    grad_key = (
        jnp.einsum("kgqj,qkgd->jkd", grad_score, queries, preferred_element_type=jnp.float32)
        * score_scale
    )
    grad_value = jnp.einsum(
        "kgqj,qkgd->jkd",
        probability.astype(jnp.bfloat16),
        grad_rows,
        preferred_element_type=jnp.float32,
    )
    return (grad_query, grad_key, grad_value)


def on_device(
    tokens,
    cotangent,
    seq_lengths,
    deal_order,
    routes,
    slot_order,
    first_gain,
    w_query,
    w_key,
    w_value,
    w_out,
    second_gain,
    w_router,
    w_gate,
    w_up,
    w_down,
):
    dp_count = lax.axis_size("dp")
    dp_index = lax.axis_index("dp")
    tensor_index = lax.axis_index("tensor")
    expert_count = lax.axis_size("expert")
    token_count, model_width = tokens.shape
    slot_local = token_count // SLOT
    capacity = token_count * TOP // EXPERTS
    local_experts = w_gate.shape[0]
    local_units = w_gate.shape[2]
    column_share = model_width // lax.axis_size("tensor")
    column_start = tensor_index * column_share
    group_size = HEADS // KV_HEADS
    local_kv = w_key.shape[1] // HEAD_DIM
    local_heads = w_query.shape[1] // HEAD_DIM
    deal_count = deal_order.shape[1]
    every_tokens, every_grads = (
        lax.all_gather(tokens, "dp", axis=0, tiled=True),
        lax.all_gather(cotangent, "dp", axis=0, tiled=True),
    )
    my_sources = lax.dynamic_slice_in_dim(deal_order[0], dp_index * slot_local, slot_local)
    dealt_tokens = every_tokens.reshape(dp_count * slot_local, SLOT, model_width)[
        my_sources
    ].reshape(token_count, model_width)
    dealt_grads = every_grads.reshape(dp_count * slot_local, SLOT, model_width)[my_sources].reshape(
        token_count, model_width
    )
    slot_lengths = seq_lengths[0][my_sources]
    live_rows = jnp.arange(token_count, dtype=jnp.int32) % SLOT < jnp.repeat(
        slot_lengths, SLOT, total_repeat_length=token_count
    )
    live_float = live_rows.astype(jnp.float32)[:, None]
    kept_entry, target, filled, slot_token, slot_entry = route_tables(
        routes, slot_order[0], live_rows, capacity
    )
    kept_float = kept_entry.astype(jnp.float32)
    inputs = dealt_tokens.astype(jnp.float32)
    first_scale = rms_scale(inputs)
    first_normed = (inputs * first_scale * first_gain.astype(jnp.float32)).astype(jnp.bfloat16)
    query_pre = jnp.dot(first_normed, w_query, preferred_element_type=jnp.float32)
    key_pre = jnp.dot(first_normed, w_key, preferred_element_type=jnp.float32)
    value_rows = jnp.dot(first_normed, w_value, preferred_element_type=jnp.float32).astype(
        jnp.bfloat16
    )
    queries = rotate(query_pre.reshape(token_count, local_heads, HEAD_DIM), 1.0).astype(
        jnp.bfloat16
    )
    key_rows = rotate(key_pre.reshape(token_count, local_kv, HEAD_DIM), 1.0).astype(jnp.bfloat16)
    query_slots = queries.reshape(slot_local, SLOT, local_kv, group_size, HEAD_DIM)
    key_slots = key_rows.reshape(slot_local, SLOT, local_kv, HEAD_DIM)
    value_slots = value_rows.reshape(slot_local, SLOT, local_kv, HEAD_DIM)
    mixed_slots, logsums = lax.map(
        forward_slot, (query_slots, key_slots, value_slots, slot_lengths)
    )
    heads_out = mixed_slots.reshape(token_count, local_heads * HEAD_DIM).astype(jnp.bfloat16)
    attn_part = jnp.dot(heads_out, w_out, preferred_element_type=jnp.float32) * live_float
    attention = lax.psum(attn_part, "tensor")
    hidden = inputs + attention
    second_scale = rms_scale(hidden)
    second_normed = (hidden * second_scale * second_gain.astype(jnp.float32)).astype(jnp.bfloat16)
    logits = jnp.dot(second_normed, w_router, preferred_element_type=jnp.float32)
    chosen = jnp.take_along_axis(logits, routes, axis=1)
    gate_exp = jnp.exp(chosen - jnp.max(chosen, axis=-1, keepdims=True))
    gate_values = gate_exp / jnp.sum(gate_exp, axis=-1, keepdims=True)
    kept_gates = jnp.where(kept_entry, gate_values, 0.0)
    hidden_share = lax.dynamic_slice_in_dim(hidden, column_start, column_share, 1)
    send_rows = jnp.where(filled[:, None], second_normed[slot_token], jnp.zeros((), jnp.bfloat16))
    send_rows = send_rows.reshape(expert_count, local_experts * capacity, model_width)
    arrived = lax.all_to_all(send_rows, "expert", split_axis=0, concat_axis=0, tiled=True).reshape(
        expert_count, local_experts, capacity, model_width
    )

    def expert_forward(expert_slot, outputs):
        rows_here = lax.dynamic_index_in_dim(arrived, expert_slot, 1, keepdims=False)
        gate_weight = lax.dynamic_index_in_dim(w_gate, expert_slot, 0, keepdims=False)
        up_weight = lax.dynamic_index_in_dim(w_up, expert_slot, 0, keepdims=False)
        down_weight = lax.dynamic_index_in_dim(w_down, expert_slot, 0, keepdims=False)
        gate_here = jnp.einsum(
            "scd,df->scf", rows_here, gate_weight, preferred_element_type=jnp.float32
        )
        up_here = jnp.einsum(
            "scd,df->scf", rows_here, up_weight, preferred_element_type=jnp.float32
        )
        activated = (gate_here * jax.nn.sigmoid(gate_here) * up_here).astype(jnp.bfloat16)
        produced = jnp.einsum(
            "scf,fd->scd", activated, down_weight, preferred_element_type=jnp.float32
        ).astype(jnp.bfloat16)
        return lax.dynamic_update_index_in_dim(outputs, produced, expert_slot, 1)

    produced_all = lax.fori_loop(
        0,
        local_experts,
        expert_forward,
        jnp.zeros((expert_count, local_experts, capacity, model_width), jnp.bfloat16),
    )
    produced_flat = produced_all.reshape(expert_count, local_experts * capacity, model_width)
    returned = lax.all_to_all(
        produced_flat, "expert", split_axis=0, concat_axis=0, tiled=True
    ).reshape(EXPERTS * capacity, model_width)
    picked_rows = returned[target]
    combined = jnp.einsum(
        "tk,tkd->td",
        kept_gates,
        picked_rows.astype(jnp.float32),
        preferred_element_type=jnp.float32,
    )
    moe_columns = lax.psum_scatter(
        combined.astype(jnp.bfloat16), "tensor", scatter_dimension=1, tiled=True
    ).astype(jnp.float32)
    out_share = (hidden_share + moe_columns).astype(jnp.bfloat16)
    grads_out = dealt_grads.astype(jnp.float32)
    slot_gate = jnp.where(filled, gate_values.reshape(-1)[slot_entry], 0.0)
    grad_back = (
        (slot_gate[:, None] * grads_out[slot_token])
        .astype(jnp.bfloat16)
        .reshape(expert_count, local_experts * capacity, model_width)
    )
    rows_again, grad_arrived = (
        lax.all_to_all(send_rows, "expert", split_axis=0, concat_axis=0, tiled=True),
        lax.all_to_all(grad_back, "expert", split_axis=0, concat_axis=0, tiled=True),
    )
    rows_source = rows_again.reshape(expert_count, local_experts, capacity, model_width)
    grad_arrived = grad_arrived.reshape(expert_count, local_experts, capacity, model_width)

    def expert_backward(expert_slot, carried):
        row_grads, gate_acc, up_acc, down_acc = carried
        rows_here = lax.dynamic_index_in_dim(rows_source, expert_slot, 1, keepdims=False)
        grad_here = lax.dynamic_index_in_dim(grad_arrived, expert_slot, 1, keepdims=False)
        gate_weight = lax.dynamic_index_in_dim(w_gate, expert_slot, 0, keepdims=False)
        up_weight = lax.dynamic_index_in_dim(w_up, expert_slot, 0, keepdims=False)
        down_weight = lax.dynamic_index_in_dim(w_down, expert_slot, 0, keepdims=False)
        gate_here = jnp.einsum(
            "scd,df->scf", rows_here, gate_weight, preferred_element_type=jnp.float32
        )
        up_here = jnp.einsum(
            "scd,df->scf", rows_here, up_weight, preferred_element_type=jnp.float32
        )
        sigmoid_here = jax.nn.sigmoid(gate_here)
        silu_here = gate_here * sigmoid_here
        activated = (silu_here * up_here).astype(jnp.bfloat16)
        grad_act = jnp.einsum(
            "scd,fd->scf", grad_here, down_weight, preferred_element_type=jnp.float32
        )
        down_term = jnp.einsum(
            "scf,scd->fd", activated, grad_here, preferred_element_type=jnp.float32
        )
        grad_gate = (
            grad_act * up_here * sigmoid_here * (1.0 + gate_here * (1.0 - sigmoid_here))
        ).astype(jnp.bfloat16)
        grad_up = (grad_act * silu_here).astype(jnp.bfloat16)
        gate_term = jnp.einsum(
            "scd,scf->df", rows_here, grad_gate, preferred_element_type=jnp.float32
        )
        up_term = jnp.einsum("scd,scf->df", rows_here, grad_up, preferred_element_type=jnp.float32)
        grad_in = (
            jnp.einsum("scf,df->scd", grad_gate, gate_weight, preferred_element_type=jnp.float32)
            + jnp.einsum("scf,df->scd", grad_up, up_weight, preferred_element_type=jnp.float32)
        ).astype(jnp.bfloat16)
        return (
            lax.dynamic_update_index_in_dim(row_grads, grad_in, expert_slot, 1),
            lax.dynamic_update_index_in_dim(gate_acc, gate_term, expert_slot, 0),
            lax.dynamic_update_index_in_dim(up_acc, up_term, expert_slot, 0),
            lax.dynamic_update_index_in_dim(down_acc, down_term, expert_slot, 0),
        )

    start_carry = (
        jnp.zeros((expert_count, local_experts, capacity, model_width), jnp.bfloat16),
        jnp.zeros((local_experts, model_width, local_units), jnp.float32),
        jnp.zeros((local_experts, model_width, local_units), jnp.float32),
        jnp.zeros((local_experts, local_units, model_width), jnp.float32),
    )
    row_grads_all, gate_acc, up_acc, down_acc = lax.fori_loop(
        0, local_experts, expert_backward, start_carry
    )
    row_grads_flat = row_grads_all.reshape(expert_count, local_experts * capacity, model_width)
    rows_back = lax.all_to_all(
        row_grads_flat, "expert", split_axis=0, concat_axis=0, tiled=True
    ).reshape(EXPERTS * capacity, model_width)
    normed_part = jnp.einsum(
        "tk,tkd->td",
        kept_float,
        rows_back[target].astype(jnp.float32),
        preferred_element_type=jnp.float32,
    )
    gate_partial = (
        jnp.einsum(
            "td,tkd->tk",
            grads_out,
            picked_rows.astype(jnp.float32),
            preferred_element_type=jnp.float32,
        )
        * kept_float
    )
    normed_grad, gate_grad_sum = lax.psum((normed_part, gate_partial), "tensor")
    centered = gate_values * (
        gate_grad_sum - jnp.sum(gate_values * gate_grad_sum, axis=-1, keepdims=True)
    )
    expert_match = (
        routes[:, :, None] == jnp.arange(EXPERTS, dtype=jnp.int32)[None, None, :]
    ).astype(jnp.float32)
    logit_grad = jnp.sum(expert_match * centered[:, :, None], axis=1).astype(jnp.bfloat16)
    router_term = jnp.einsum(
        "td,te->de", second_normed, logit_grad, preferred_element_type=jnp.float32
    )
    normed_grad = normed_grad + jnp.einsum(
        "te,de->td", logit_grad, w_router, preferred_element_type=jnp.float32
    )
    second_hat = hidden * second_scale
    second_term = jnp.sum(normed_grad * second_hat, axis=0)
    scaled_grad = normed_grad * second_gain.astype(jnp.float32)
    hidden_grad = grads_out + second_scale * (
        scaled_grad - second_hat * jnp.mean(scaled_grad * second_hat, axis=-1, keepdims=True)
    )
    branch_grad = (hidden_grad * live_float).astype(jnp.bfloat16)
    out_term = jnp.einsum("ta,td->ad", heads_out, branch_grad, preferred_element_type=jnp.float32)
    heads_grad = jnp.einsum(
        "td,ad->ta", branch_grad, w_out, preferred_element_type=jnp.float32
    ).astype(jnp.bfloat16)
    grad_slots = heads_grad.reshape(slot_local, SLOT, local_kv, group_size, HEAD_DIM)
    query_grads, key_grads, value_grads = lax.map(
        backward_slot, (query_slots, key_slots, value_slots, grad_slots, logsums, slot_lengths)
    )
    query_back = (
        rotate(query_grads.reshape(token_count, local_heads, HEAD_DIM), -1.0)
        .reshape(token_count, local_heads * HEAD_DIM)
        .astype(jnp.bfloat16)
    )
    key_back = (
        rotate(key_grads.reshape(token_count, local_kv, HEAD_DIM), -1.0)
        .reshape(token_count, local_kv * HEAD_DIM)
        .astype(jnp.bfloat16)
    )
    value_back = value_grads.reshape(token_count, local_kv * HEAD_DIM).astype(jnp.bfloat16)
    query_term = jnp.einsum(
        "td,ta->da", first_normed, query_back, preferred_element_type=jnp.float32
    )
    key_term = jnp.einsum("td,ta->da", first_normed, key_back, preferred_element_type=jnp.float32)
    value_term = jnp.einsum(
        "td,ta->da", first_normed, value_back, preferred_element_type=jnp.float32
    )
    normed_first = jnp.einsum("ta,da->td", query_back, w_query, preferred_element_type=jnp.float32)
    normed_first = normed_first + jnp.einsum(
        "ta,da->td", key_back, w_key, preferred_element_type=jnp.float32
    )
    normed_first = normed_first + jnp.einsum(
        "ta,da->td", value_back, w_value, preferred_element_type=jnp.float32
    )
    first_grad = lax.psum(normed_first.astype(jnp.bfloat16), "tensor").astype(jnp.float32)
    first_hat = inputs * first_scale
    first_term = jnp.sum(first_grad * first_hat, axis=0)
    scaled_first = first_grad * first_gain.astype(jnp.float32)
    input_full = hidden_grad + first_scale * (
        scaled_first - first_hat * jnp.mean(scaled_first * first_hat, axis=-1, keepdims=True)
    )
    input_share = lax.dynamic_slice_in_dim(input_full, column_start, column_share, 1).astype(
        jnp.bfloat16
    )
    dense_sums = lax.psum(
        (first_term, second_term, router_term, query_term, key_term, value_term, out_term),
        ("expert", "dp"),
    )
    gate_sum, up_sum, down_sum = (
        lax.psum(gate_acc.astype(jnp.bfloat16), "dp").astype(jnp.float32),
        lax.psum(up_acc.astype(jnp.bfloat16), "dp").astype(jnp.float32),
        lax.psum(down_acc.astype(jnp.bfloat16), "dp").astype(jnp.float32),
    )
    every_out, every_input = (
        lax.all_gather(out_share, "dp", axis=0, tiled=True),
        lax.all_gather(input_share, "dp", axis=0, tiled=True),
    )
    inverse = (
        jnp.zeros((deal_count,), jnp.int32)
        .at[deal_order[0]]
        .set(jnp.arange(deal_count, dtype=jnp.int32))
    )
    given_places = lax.dynamic_slice_in_dim(inverse, dp_index * slot_local, slot_local)
    block_result = every_out.reshape(dp_count * slot_local, SLOT, column_share)[
        given_places
    ].reshape(token_count, column_share)
    input_result = every_input.reshape(dp_count * slot_local, SLOT, column_share)[
        given_places
    ].reshape(token_count, column_share)
    return (
        block_result,
        input_result,
        dense_sums[0],
        dense_sums[3],
        dense_sums[4],
        dense_sums[5],
        dense_sums[6],
        dense_sums[1],
        dense_sums[2],
        gate_sum,
        up_sum,
        down_sum,
    )


def solution(mesh):
    placed = (
        P(("expert", "dp"), None),
        P(("expert", "dp"), None),
        P("expert", None),
        P("expert", None),
        P(("expert", "dp"), None),
        P(("expert", "dp"), None),
        P(),
        P(None, "tensor"),
        P(None, "tensor"),
        P(None, "tensor"),
        P("tensor", None),
        P(),
        P(),
        P("expert", None, "tensor"),
        P("expert", None, "tensor"),
        P("expert", "tensor", None),
    )
    return jax.shard_map(
        on_device,
        mesh=mesh,
        in_specs=placed,
        out_specs=(
            P(("expert", "dp"), "tensor"),
            P(("expert", "dp"), "tensor"),
            P(),
            P(None, "tensor"),
            P(None, "tensor"),
            P(None, "tensor"),
            P("tensor", None),
            P(),
            P(),
            P("expert", None, "tensor"),
            P("expert", None, "tensor"),
            P("expert", "tensor", None),
        ),
        check_vma=False,
    )
```

profile of v0, /device:TPU:0, one launch (start us, length us, event | category | flops | bytes accessed | tf_op | source)
XLA Modules:
  0.0 1763.1 jit_solution(3198966666830467296)
XLA Ops:
  17.3 24.4 %gather_fusion = pred[4096]{0:T(1024)(128)(4,1)S(1)} fusion(pred[512]{0:T(512)(128)(4,1)S(1)} %fusion.124, s32[4096]{0:T(1024)S(1)} %broadcast_clamp_fusion.2), kind=kCustom, calls=%fused_computation | custom fusion | bytes 24576 | tf_op jit(solution)/shard_map/jit(_take)/gather | solution.py:49
  41.7 25.6 %gather_fusion.2 = pred[4096]{0:T(1024)(128)(4,1)S(1)} fusion(pred[4096]{0:T(1024)(128)(4,1)S(1)} %gather_fusion, s32[4096]{0:T(1024)S(1)} %broadcast_clamp_fusion.1), kind=kCustom, calls=%fused_computation.2 | custom fusion | bytes 24576 | tf_op jit(solution)/shard_map/gather | solution.py:51
  67.4 23.0 %gather_fusion.1 = s32[4096]{0:T(1024)S(1)} fusion(s32[4096]{0:T(1024)S(1)} %reshape.809, s32[4096]{0:T(1024)S(1)} %broadcast_clamp_fusion.1), kind=kCustom, calls=%fused_computation.1 | custom fusion | bytes 49152 | tf_op jit(solution)/shard_map/gather | solution.py:50
  114.3 15.5 scatter_custom_fusion
  129.9 15.5 scatter_custom_fusion.1
  146.1 21.9 %all-reduce.9.cloned.1.call-done = f32[512,1024]{1,0:T(8,128)} async-done(((f32[512,1024]{1,0:T(8,128)}), f32[512,1024]{1,0:T(8,128)}) %all-reduce.9.cloned.1.call-update) | async-done | bytes 2097168 | tf_op jit(solution)/shard_map/psum | solution.py:200
  171.7 18.1 %gather_fusion.3 = bf16[4096,1024]{1,0:T(8,128)(2,1)} fusion(bf16[512,1024]{1,0:T(8,128)(2,1)S(1)} %multiply_convert_fusion.6, s32[4096]{0:T(1024)S(1)} %get-tuple-element.555), kind=kCustom, calls=%fused_computation.3 | custom fusion | bytes 16793600 | tf_op jit(solution)/shard_map/gather | solution.py:210
  205.0 91.8 %all-to-all-done = bf16[2,2048,1024]{2,1,0:T(8,128)(2,1)} async-done(((bf16[2,2048,1024]{2,1,0:T(8,128)(2,1)}), bf16[2,2048,1024]{2,1,0:T(8,128)(2,1)}, u32[]{:S(2)}, u32[]{:S(2)}) %all-to-all-start) | async-done | bytes 8388640 | tf_op jit(solution)/shard_map/all_to_all | solution.py:212
  309.7 62.1 %while.51 = (s32[]{:T(128)}, bf16[2,16,128,1024]{3,2,1,0:T(8,128)(2,1)}, bf16[2,16,128,1024]{3,2,0,1:T(8,128)(2,1)}, bf16[16,1024,128]{2,1,0:T(8,128)(2,1)}, bf1...) while((s32[]{:T(128)}, bf16[2,16,128,1024]{3,2,1,0:T(8,128)(2,1)}, ...), condition=%wide.region_13.14_spmd, body=%wide.region_12.13_spmd.sunk | while | flops 201785344 | bytes 2624597 | solution.py:233
  382.7 18.5 %gather_fusion.6 = f32[4096,1024]{1,0:T(8,128)} fusion(f32[512,1024]{1,0:T(8,128)S(1)} %get-tuple-element.541, s32[4096]{0:T(1024)S(1)} %get-tuple-element.555), kind=kCustom, calls=%fused_computation.6 | custom fusion | bytes 33570816 | tf_op jit(solution)/shard_map/gather | solution.py:257
  402.8 33.0 %gather_fusion.8 = f32[4096]{0:T(1024)S(1)} fusion(f32[512,32]{0,1:T(8,128)S(1)} %fusion.138, s32[4096]{0:T(1024)S(1)} %reshape.1000), kind=kCustom, calls=%fused_computation.8 | custom fusion | bytes 65536 | tf_op jit(solution)/shard_map/jit(take_along_axis)/gather | solution.py:205
  436.2 34.4 %all-to-all-done.1 = bf16[2,2048,1024]{2,1,0:T(8,128)(2,1)} async-done(((bf16[2,2048,1024]{2,1,0:T(8,128)(2,1)}), bf16[2,2048,1024]{2,1,0:T(8,128)(2,1)}, u32[]{:S(2)}, u32[]{:S(2)}) %all-to-all-start.1) | async-done | bytes 8388640 | tf_op jit(solution)/shard_map/all_to_all | solution.py:240
  470.6 25.3 %gather_fusion.4 = bf16[4096,1024]{1,0:T(8,128)(2,1)} fusion(bf16[4096,1024]{1,0:T(8,128)(2,1)} %bitcast.54, s32[4096]{0:T(1024)S(1)} %broadcast_clamp_fusion), kind=kCustom, calls=%fused_computation.4 | custom fusion | bytes 16793600 | tf_op jit(solution)/shard_map/gather | solution.py:243
  514.4 23.0 %gather_fusion.5 = f32[4096]{0:T(1024)S(1)} fusion(f32[4096]{0:T(1024)S(1)} %div.106, s32[4096]{0:T(1024)S(1)} %copy-done.43), kind=kCustom, calls=%fused_computation.5 | custom fusion | bytes 49152 | tf_op jit(solution)/shard_map/gather | solution.py:255
  553.8 91.6 %all-to-all-done.2 = bf16[2,2048,1024]{2,1,0:T(8,128)(2,1)} async-done(((bf16[2,2048,1024]{2,1,0:T(8,128)(2,1)}), bf16[2,2048,1024]{2,1,0:T(8,128)(2,1)}, u32[]{:S(2)}, u32[]{:S(2)}) %all-to-all-start.2) | async-done | bytes 8388640 | tf_op jit(solution)/shard_map/all_to_all | solution.py:263
  649.8 220.3 %while.52 = (s32[]{:T(128)}, bf16[2,16,128,1024]{3,2,1,0:T(8,128)(2,1)}, bf16[16,1024,128]{2,1,0:T(8,128)(2,1)}, bf16[16,1024,128]{2,1,0:T(8,128)(2,1)}, bf16[16...) while((s32[]{:T(128)}, ...), condition=%wide.region_17.18_spmd, body=%wide.region_16.17_spmd.sunk | while | flops 538017792 | bytes 9837689 | solution.py:315
  877.7 90.2 %all-to-all-done.3 = bf16[2,2048,1024]{2,1,0:T(8,128)(2,1)} async-done(((bf16[2,2048,1024]{2,1,0:T(8,128)(2,1)}), bf16[2,2048,1024]{2,1,0:T(8,128)(2,1)}, u32[]{:S(2)}, u32[]{:S(2)}) %all-to-all-start.3) | async-done | bytes 8388640 | tf_op jit(solution)/shard_map/all_to_all | solution.py:319
  967.9 25.2 %gather_fusion.7 = bf16[4096,1024]{1,0:T(8,128)(2,1)} fusion(bf16[4096,1024]{1,0:T(8,128)(2,1)} %bitcast.67, s32[4096]{0:T(1024)S(1)} %broadcast_clamp_fusion), kind=kCustom, calls=%fused_computation.7 | custom fusion | bytes 16793600 | tf_op jit(solution)/shard_map/gather | solution.py:325
  1008.3 43.5 %all-reduce.11.cloned.1.call-done = f32[512,1024]{1,0:T(8,128)} async-done(((f32[512,1024]{1,0:T(8,128)}), f32[512,1024]{1,0:T(8,128)}) %all-reduce.11.cloned.1.call-update) | async-done | bytes 2097168 | tf_op jit(solution)/shard_map/psum | solution.py:337
  1064.0 15.8 reduce-scatter.2.cloned.1.call-done
  1081.6 37.2 %all-reduce.13.cloned.1.call-done = bf16[512,1024]{1,0:T(8,128)(2,1)} async-done(((bf16[512,1024]{1,0:T(8,128)(2,1)}), bf16[512,1024]{1,0:T(8,128)(2,1)}) %all-reduce.13.cloned.1.call-update) | async-done | bytes 1048592 | tf_op jit(solution)/shard_map/psum | solution.py:391
  1150.9 21.5 %all-reduce = (f32[1024]{0:T(1024)}, f32[1024]{0:T(1024)}) all-reduce(f32[1024]{0:T(1024)S(1)} %get-tuple-element.488, f32[1024]{0:T(1024)S(1)} %get-tuple-element.490), channel_id=1, replica_groups=mesh['expert'=2,'tensor'=4,'dp'=4] {'expert','dp'}, use_global_device_ids=true, to_apply=%region_27.28 | all-reduce | flops 2048 | bytes 16384 | tf_op jit(solution)/shard_map/psum | solution.py:401
  1180.9 428.3 %all-reduce.17.cloned.1.call-done = (bf16[16,1024,128]{2,1,0:T(8,128)(2,1)}, bf16[16,1024,128]{2,1,0:T(8,128)(2,1)}, bf16[16,128,1024]{2,1,0:T(8,128)(2,1)}) async-done(((bf16[16,1024,128]{2,1,0:T(8,128)(2,1)}, bf16[16,1024,128]{2,1,0:T(8,128)(2,1)}, bf16[16,128,1024]{2,1,0:T(8,128)(2,1)}), (bf16[16,1024,128]{2,1,0:T(8,128)(2,1)}, bf16[16,1024,128]{2,1,0:T(8,128)(2,1)}, ...) | async-done | bytes 12582928 | tf_op jit(solution)/shard_map/psum | solution.py:406
  1625.1 123.0 %all-reduce.15.cloned.1.call-done = (f32[1024,256]{1,0:T(8,128)}, f32[1024,128]{1,0:T(8,128)}, f32[1024,128]{1,0:T(8,128)}, f32[256,1024]{1,0:T(8,128)}, f32[1024,32]{0,1:T(8,128)}) async-done(((f32[1024,256]{1,0:T(8,128)}, f32[1024,128]{1,0:T(8,128)}, f32[1024,128]{1,0:T(8,128)}, f32[256,1024]{1,0:T(8,128)}, f32[1024,32]{0,1:T(8,128)}), (f32[1024,256]{1,0:T(8,128)}, f32[1024,128]{1,0:T(8,128)}, ...) | async-done | bytes 3276816 | tf_op jit(solution)/shard_map/psum | solution.py:401
  (436 shorter events, 496.4 us)
Async XLA Ops:
  7.2 104.7 %copy-start = (bf16[256,1024]{1,0:T(8,128)(2,1)S(1)}, bf16[256,1024]{1,0:T(8,128)(2,1)}, u32[]{:S(2)}) copy-start(bf16[256,1024]{1,0:T(8,128)(2,1)} %param.36) | copy-start | bytes 1572868
  7.2 34.5 %copy-start.58 = (s32[1,4096]{1,0:T(1,128)S(1)}, s32[1,4096]{1,0:T(1,128)}, u32[]{:S(2)}) copy-start(s32[1,4096]{1,0:T(1,128)} %param.31) | copy-start | bytes 49156
  7.2 96.2 %all-gather.5.cloned.1.call-start = ((), (), s32[]{:S(2)}) async-start(), calls=%async_computation.5 | async-start | bytes 5242880 | tf_op jit(solution)/shard_map/all_gather | solution.py:161
  7.9 160.0 %all-reduce.9.cloned.1.call-start = ((), (), s32[]{:S(2)}) async-start(), calls=%async_computation.6 | async-start | bytes 4194304 | tf_op jit(solution)/shard_map/psum | solution.py:200
  11.2 159.0 %copy-start.41 = (f32[1024]{0:T(1024)}, f32[1024]{0:T(1024)S(1)}, u32[]{:S(2)}) copy-start(f32[1024]{0:T(1024)S(1)} %convert_element_type.302) | copy-start | bytes 12292
  11.9 93.1 %copy-start.46 = (f32[1024]{0:T(1024)}, f32[1024]{0:T(1024)S(1)}, u32[]{:S(2)}) copy-start(f32[1024]{0:T(1024)S(1)} %convert_element_type.291) | copy-start | bytes 12292
  197.1 99.7 %all-to-all-start = ((bf16[2,2048,1024]{2,1,0:T(8,128)(2,1)}), bf16[2,2048,1024]{2,1,0:T(8,128)(2,1)}, u32[]{:S(2)}, u32[]{:S(2)}) async-start(bf16[2,2048,1024]{2,1,0:T(8,128)(2,1)} %broadcast_select_fusion), calls=%async_computation | async-start | bytes 16777216 | tf_op jit(solution)/shard_map/all_to_all | solution.py:212
  204.3 175.9 %all-gather.9.cloned.1.call-start = ((), (), s32[]{:S(2)}) async-start(), calls=%async_computation.9 | async-start | bytes 5242880 | tf_op jit(solution)/shard_map/all_gather | solution.py:162
  371.8 98.8 %all-to-all-start.1 = ((bf16[2,2048,1024]{2,1,0:T(8,128)(2,1)}), bf16[2,2048,1024]{2,1,0:T(8,128)(2,1)}, u32[]{:S(2)}, u32[]{:S(2)}) async-start(bf16[2,2048,1024]{2,1,0:T(8,128)(2,1)} %bitcast.325), calls=%async_computation.1 | async-start | bytes 16777216 | tf_op jit(solution)/shard_map/all_to_all | solution.py:240
  546.5 98.8 %all-to-all-start.2 = ((bf16[2,2048,1024]{2,1,0:T(8,128)(2,1)}), bf16[2,2048,1024]{2,1,0:T(8,128)(2,1)}, u32[]{:S(2)}, u32[]{:S(2)}) async-start(bf16[2,2048,1024]{2,1,0:T(8,128)(2,1)} %multiply_convert_fusion.4), calls=%async_computation.3 | async-start | bytes 16777216 | tf_op jit(solution)/shard_map/all_to_all | solution.py:263
  870.1 97.8 %all-to-all-start.3 = ((bf16[2,2048,1024]{2,1,0:T(8,128)(2,1)}), bf16[2,2048,1024]{2,1,0:T(8,128)(2,1)}, u32[]{:S(2)}, u32[]{:S(2)}) async-start(bf16[2,2048,1024]{2,1,0:T(8,128)(2,1)} %bitcast.324), calls=%async_computation.4 | async-start | bytes 16777216 | tf_op jit(solution)/shard_map/all_to_all | solution.py:319
  877.2 174.6 %all-reduce.11.cloned.1.call-start = ((), (), s32[]{:S(2)}) async-start(), calls=%async_computation.10 | async-start | bytes 4194304 | tf_op jit(solution)/shard_map/psum | solution.py:337
  1000.6 79.1 %reduce-scatter.2.cloned.1.call-start = ((), (), s32[]{:S(2)}) async-start(), calls=%async_computation.7 | async-start | bytes 1310720 | tf_op jit(solution)/shard_map/reduce_scatter | solution.py:250
  1006.5 45.3 %copy-start.6 = (f32[512,1024]{1,0:T(8,128)S(1)}, f32[512,1024]{1,0:T(8,128)}, u32[]{:S(2)}) copy-start(f32[512,1024]{1,0:T(8,128)} %copy-done.5) | copy-start | bytes 6291460
  1006.6 45.3 %copy-start.33 = (bf16[1024,32]{0,1:T(8,128)(2,1)S(1)}, bf16[1024,32]{0,1:T(8,128)(2,1)}, u32[]{:S(2)}) copy-start(bf16[1024,32]{0,1:T(8,128)(2,1)} %param.38) | copy-start | bytes 196612
  1006.6 45.3 %copy-start.42 = (f32[1024]{0:T(1024)S(1)}, f32[1024]{0:T(1024)}, u32[]{:S(2)}) copy-start(f32[1024]{0:T(1024)} %copy-done.41) | copy-start | bytes 12292
  1006.6 45.3 %copy-start.55 = (f32[512]{0:T(512)S(1)}, f32[512]{0:T(512)}, u32[]{:S(2)}) copy-start(f32[512]{0:T(512)} %copy-done.54) | copy-start | bytes 6148
  1008.0 110.8 %all-reduce.13.cloned.1.call-start = ((), (), s32[]{:S(2)}) async-start(), calls=%async_computation.11 | async-start | bytes 2097152 | tf_op jit(solution)/shard_map/psum | solution.py:391
  1062.4 56.4 %copy-start.47 = (f32[1024]{0:T(1024)S(1)}, f32[1024]{0:T(1024)}, u32[]{:S(2)}) copy-start(f32[1024]{0:T(1024)} %copy-done.46) | copy-start | bytes 12292
  1062.4 56.4 %copy-start.57 = (f32[512]{0:T(512)S(1)}, f32[512]{0:T(512)}, u32[]{:S(2)}) copy-start(f32[512]{0:T(512)} %copy-done.56) | copy-start | bytes 6148
  1063.9 85.3 %all-gather.7.cloned.1.call-start = ((), (), s32[]{:S(2)}) async-start(), calls=%async_computation.8 | async-start | bytes 1310720 | tf_op jit(solution)/shard_map/all_gather | solution.py:411
  1081.5 97.7 %all-gather.11.cloned.1.call-start = ((), (), s32[]{:S(2)}) async-start(), calls=%async_computation.12 | async-start | bytes 1310720 | tf_op jit(solution)/shard_map/all_gather | solution.py:412
  1123.1 486.1 %all-reduce.17.cloned.1.call-start = ((), (), s32[]{:S(2)}) async-start(), calls=%async_computation.14 | async-start | bytes 25165824 | tf_op jit(solution)/shard_map/psum | solution.py:406
  1123.9 624.2 %all-reduce.15.cloned.1.call-start = ((), (), s32[]{:S(2)}) async-start(), calls=%async_computation.13 | async-start | bytes 6553600 | tf_op jit(solution)/shard_map/psum | solution.py:401
  (50 other events, 319.8 us)
Sparse Core Ops, SparseCore 0:
  9.6 83.4 all-gather.4
  113.8 54.0 all-reduce.8
  206.8 81.3 all-gather.8
  1000.7 51.0 all-reduce.10
  1054.8 24.9 reduce-scatter.1
  1082.7 36.0 all-reduce.12
  1120.9 28.2 all-gather.6
  1151.4 27.7 all-gather.10
  1182.0 427.1 all-reduce.16
  1614.4 133.5 all-reduce.14
where the time goes:
time: 1780 us; the launch traced here: 1760 us
  waiting for transfers between devices  1000 us (56%)
  matrix products  323 us (18%)
  local copies, waits for them, and re-layouts  291 us (16%)
  other arithmetic  66.4 us (4%)
  blocking collectives  31.7 us (2%)
  starting transfers between devices  29.2 us (2%)
  between operations  19.7 us (1%)
    psum x1, waiting for transfers between devices, on_device(): lax.psum(gate_acc.astype(jnp.bfloat16), 'dp').astype(jnp.float32)  428 us
    psum x1, waiting for transfers between devices, on_device(): lax.psum((first_term, second_term, router_term, query_term, key_term, val...  123 us
    all_to_all x1, waiting for transfers between devices, on_device(): lax.all_to_all(send_rows, 'expert', split_axis=0, concat_axis=0, tiled=True)  91.8 us
    all_to_all x1, waiting for transfers between devices, on_device(): lax.all_to_all(grad_back, 'expert', split_axis=0, concat_axis=0, tiled=True)  91.6 us
    all_to_all x1, waiting for transfers between devices, on_device(): lax.all_to_all(row_grads_flat, 'expert', split_axis=0, concat_axis=0, til...  90.2 us
    psum x1, waiting for transfers between devices, on_device(): normed_grad, gate_grad_sum = lax.psum((normed_part, gate_partial), 'tensor')  43.5 us
    dot_general x16, matrix products, expert_forward(): jnp.einsum('scf,fd->scd', activated, down_weight, preferred_element_type=...  39.8 us
    psum x1, waiting for transfers between devices, on_device(): lax.psum(normed_first.astype(jnp.bfloat16), 'tensor').astype(jnp.float32)  37.2 us
  transfers between devices with their start and end apart: 14, of which 12 were waited for; matrix products, arithmetic and copies ran while one was open for 18% of the time, Pallas kernels for 0%

commit v1 on v0

v1 whole, which is shorter than its diff:
```python
import functools

import jax
import jax.numpy as jnp
import numpy as np
from jax import lax
from jax.experimental import pallas as pl
from jax.experimental.pallas import tpu as pltpu
from jax.sharding import PartitionSpec as P

HEADS = 16
KV_HEADS = 8
HEAD_DIM = 64
EXPERTS = 32
TOP = 8
SLOT = 512

EPS = 1e-06
THETA = 10000.0
NEG = -1e30
BF = jnp.bfloat16
F32 = jnp.float32
MIB = 1 << 20


def dot(a, b, ca=1, cb=0):
    return lax.dot_general(a, b, (((ca,), (cb,)), ((), ())), preferred_element_type=F32)


def vmem(count=1):
    return [pl.BlockSpec(memory_space=pltpu.VMEM)] * count


def params(mib, **more):
    return pltpu.CompilerParams(vmem_limit_bytes=mib * MIB, **more)


def rotary_tables(rows):
    places = np.arange(rows, dtype=np.float32)[:, None]
    halfway = HEAD_DIM // 2
    spread = np.float32(THETA) ** (-2.0 * np.arange(halfway, dtype=np.float32) / HEAD_DIM)
    angles = (places * spread.astype(np.float32)[None, :]).astype(np.float32)
    copies = 128 // halfway
    return (
        np.tile(np.cos(angles), (1, copies)).astype(np.float32),
        np.tile(np.sin(angles), (1, copies)).astype(np.float32),
    )


def rotate128(values, cosine, sine, low_half):
    half = HEAD_DIM // 2
    up = pltpu.roll(values, 128 - half, 1)
    down = pltpu.roll(values, half, 1)
    return values * cosine + jnp.where(low_half, -up, down) * sine


def lanes(shape):
    return lax.broadcasted_iota(jnp.int32, shape, len(shape) - 1)


def sublanes(shape):
    return lax.broadcasted_iota(jnp.int32, shape, len(shape) - 2)


def table_kernel(length_ref, routes_ref, order_ref, table_ref):
    rows = routes_ref.shape[0]
    capacity = rows * TOP // EXPERTS
    entries = rows * TOP
    chunk = 512
    length = length_ref[0]
    routes_t = jnp.transpose(routes_ref[...].astype(F32)).astype(BF)
    upper = (sublanes((chunk, chunk)) < lanes((chunk, chunk))).astype(F32).astype(BF)
    expert_row = sublanes((EXPERTS, chunk))

    def body(step, carried):
        counts, table = carried
        entry = order_ref[:, pl.ds(pl.multiple_of(step * chunk, chunk), chunk)]
        row, choice = entry // TOP, entry % TOP
        onehot_row = (sublanes((rows, chunk)) == row).astype(F32).astype(BF)
        picked = dot(routes_t, onehot_row)
        expert = jnp.sum(jnp.where(sublanes((TOP, chunk)) == choice, picked, 0.0), axis=0, keepdims=True)
        member = (expert_row == expert.astype(jnp.int32)) & (row < length)
        member_f = member.astype(F32)
        before = dot(member_f.astype(BF), upper) + counts
        value = jnp.where(member, jnp.minimum(before, float(capacity)) + 1.0, 0.0)
        table = table + dot(value.astype(BF), onehot_row, 1, 1)
        return counts + jnp.sum(member_f, axis=1, keepdims=True), table

    _, table = lax.fori_loop(
        0, entries // chunk, body, (jnp.zeros((EXPERTS, 1), F32), jnp.zeros((EXPERTS, rows), F32))
    )
    table_ref[...] = table.astype(BF)


def make_table(length, routes, order):
    rows = routes.shape[0]
    return pl.pallas_call(
        table_kernel,
        out_shape=jax.ShapeDtypeStruct((EXPERTS, rows), BF),
        in_specs=[pl.BlockSpec(memory_space=pltpu.SMEM)] + vmem(2),
        out_specs=vmem()[0],
        compiler_params=params(32),
        name="tables",
    )(length, routes, order)


def head_parts(q, k_a, k_b, index, low_lane):
    block = q[:, (index // 2) * 128 : (index // 2) * 128 + 128]
    mine = low_lane if index % 2 == 0 else jnp.logical_not(low_lane)
    return jnp.where(mine, block, jnp.zeros((), block.dtype)), (k_a if index % 2 == (index // 2) % 2 else k_b)


def swap(block):
    return pltpu.roll(block.astype(F32), HEAD_DIM, 1).astype(BF)


def attend_kernel(
    length_ref, x_ref, gain_ref, wq_ref, wk_ref, wv_ref, wo_ref, cos_ref, sin_ref,
    part_ref, normed_ref, q_ref, k_ref, v_ref, heads_ref, logsum_ref,
):
    rows = x_ref.shape[0]
    length = length_ref[0]
    x = x_ref[...].astype(F32)
    scale = lax.rsqrt(jnp.mean(x * x, axis=-1, keepdims=True) + EPS)
    normed = (x * scale * gain_ref[...].astype(F32)).astype(BF)
    normed_ref[...] = normed
    cosine, sine = cos_ref[...], sin_ref[...]
    lane = lanes((rows, 128))
    low_half = lane % HEAD_DIM < HEAD_DIM // 2
    low_lane = lane < HEAD_DIM
    q_pre = dot(normed, wq_ref[...])
    for block in range(q_pre.shape[1] // 128):
        cut = slice(block * 128, block * 128 + 128)
        q_ref[:, cut] = rotate128(q_pre[:, cut], cosine, sine, low_half).astype(BF)
    k = rotate128(dot(normed, wk_ref[...]), cosine, sine, low_half).astype(BF)
    v = dot(normed, wv_ref[...]).astype(BF)
    k_ref[...] = k
    v_ref[...] = v
    q = q_ref[...]
    k_b, v_b = swap(k), swap(v)
    row, col = sublanes((rows, rows)), lanes((rows, rows))
    allowed = (col <= row) & (col < length)
    logsum = jnp.zeros((rows, 128), F32)
    pair = None
    for index in range(q.shape[1] // HEAD_DIM):
        q_one, k_one = head_parts(q, k, k_b, index, low_lane)
        v_one = v if index % 2 == (index // 2) % 2 else v_b
        scores = jnp.where(allowed, dot(q_one, k_one, 1, 1) * (HEAD_DIM**-0.5), NEG)
        highest = jnp.max(scores, axis=-1, keepdims=True)
        weights = jnp.exp(scores - highest)
        total = jnp.sum(weights, axis=-1, keepdims=True)
        mixed = dot((weights / total).astype(BF), v_one)
        logsum = jnp.where(lane == index, highest + jnp.log(total), logsum)
        if index % 2 == 0:
            pair = mixed
        else:
            cut = slice((index // 2) * 128, (index // 2) * 128 + 128)
            heads_ref[:, cut] = jnp.where(low_lane, pair, mixed).astype(BF)
    logsum_ref[...] = logsum
    live = (sublanes((rows, 1)) < length).astype(F32)
    part_ref[...] = (dot(heads_ref[...], wo_ref[...]) * live).astype(BF)


def attend(length, x, gain, wq, wk, wv, wo, cosine, sine):
    rows, width = x.shape
    shape = jax.ShapeDtypeStruct
    return pl.pallas_call(
        attend_kernel,
        out_shape=(
            shape((rows, width), BF), shape((rows, width), BF), shape((rows, wq.shape[1]), BF),
            shape((rows, wk.shape[1]), BF), shape((rows, wv.shape[1]), BF), shape((rows, wq.shape[1]), BF),
            shape((rows, 128), F32),
        ),
        in_specs=[pl.BlockSpec(memory_space=pltpu.SMEM)] + vmem(8),
        out_specs=tuple(vmem(7)),
        compiler_params=params(48),
        name="attend",
    )(length, x, gain, wq, wk, wv, wo, cosine, sine)


def attend_back_kernel(
    length_ref, hidden_grad_ref, x_ref, gain_ref, normed_ref, q_ref, k_ref, v_ref, heads_ref, logsum_ref,
    wq_ref, wk_ref, wv_ref, wo_ref, cos_ref, sin_ref,
    first_ref, stat_ref, gain_grad_ref, q_grad_ref, k_grad_ref, v_grad_ref, back_ref,
):
    rows, width = hidden_grad_ref.shape
    length = length_ref[0]
    inv = HEAD_DIM**-0.5
    live = (sublanes((rows, 1)) < length).astype(F32)
    branch = (hidden_grad_ref[...].astype(F32) * live).astype(BF)
    heads_grad = dot(branch, wo_ref[...], 1, 1).astype(BF)
    cosine, sine = cos_ref[...], -sin_ref[...]
    lane = lanes((rows, 128))
    low_half = lane % HEAD_DIM < HEAD_DIM // 2
    low_lane = lane < HEAD_DIM
    q, k, v = q_ref[...], k_ref[...], v_ref[...]
    k_b, v_b = swap(k), swap(v)
    key, query = sublanes((rows, rows)), lanes((rows, rows))
    allowed = (key <= query) & (key < length)
    logsum_rows = jnp.transpose(logsum_ref[...])
    dk = [jnp.zeros((rows, 128), F32), jnp.zeros((rows, 128), F32)]
    dv = [jnp.zeros((rows, 128), F32), jnp.zeros((rows, 128), F32)]
    q_width = q.shape[1]
    pair = None
    for index in range(q_width // HEAD_DIM):
        same = index % 2 == (index // 2) % 2
        q_one, k_one = head_parts(q, k, k_b, index, low_lane)
        g_one, v_one = head_parts(heads_grad, v, v_b, index, low_lane)
        scores = jnp.where(allowed, dot(k_one, q_one, 1, 1) * inv, NEG)
        prob = jnp.exp(scores - logsum_rows[index : index + 1, :])
        grad_prob = dot(v_one, g_one, 1, 1)
        center = jnp.sum(prob * grad_prob, axis=0, keepdims=True)
        score_grad = (prob * (grad_prob - center)).astype(BF)
        dq = dot(score_grad, k_one, 0, 0) * inv
        place = 0 if same else 1
        dk[place] = dk[place] + dot(score_grad, q_one) * inv
        dv[place] = dv[place] + dot(prob.astype(BF), g_one)
        if index % 2 == 0:
            pair = dq
        else:
            cut = slice((index // 2) * 128, (index // 2) * 128 + 128)
            both = jnp.where(low_lane, pair, dq)
            back_ref[:, cut] = rotate128(both, cosine, sine, low_half).astype(BF)
    k_width = k.shape[1]
    k_total = dk[0] + pltpu.roll(dk[1], HEAD_DIM, 1)
    v_total = dv[0] + pltpu.roll(dv[1], HEAD_DIM, 1)
    back_ref[:, q_width : q_width + k_width] = rotate128(k_total, cosine, sine, low_half).astype(BF)
    back_ref[:, q_width + k_width :] = v_total.astype(BF)
    back = back_ref[...]
    grads = dot(normed_ref[...], back, 0, 0)
    q_grad_ref[...] = grads[:, :q_width].astype(BF)
    k_grad_ref[...] = grads[:, q_width : q_width + k_width].astype(BF)
    v_grad_ref[...] = grads[:, q_width + k_width :].astype(BF)
    first = (
        dot(back[:, :q_width], wq_ref[...], 1, 1)
        + dot(back[:, q_width : q_width + k_width], wk_ref[...], 1, 1)
        + dot(back[:, q_width + k_width :], wv_ref[...], 1, 1)
    )
    x = x_ref[...].astype(F32)
    hat = x * lax.rsqrt(jnp.mean(x * x, axis=-1, keepdims=True) + EPS)
    along = first * hat
    gain_grad_ref[...] = jnp.sum(along, axis=0, keepdims=True)
    stat_ref[...] = jnp.broadcast_to(
        jnp.sum(along * gain_ref[...].astype(F32), axis=-1, keepdims=True), (rows, 128)
    )
    first_ref[...] = first.astype(BF)


def attend_back(length, hidden_grad, x, gain, normed, q, k, v, heads, logsum, wq, wk, wv, wo, cosine, sine):
    rows, width = x.shape
    shape = jax.ShapeDtypeStruct
    return pl.pallas_call(
        attend_back_kernel,
        out_shape=(
            shape((rows, width), BF), shape((rows, 128), F32), shape((1, width), F32),
            shape(wq.shape, BF), shape(wk.shape, BF), shape(wv.shape, BF),
        ),
        in_specs=[pl.BlockSpec(memory_space=pltpu.SMEM)] + vmem(15),
        out_specs=tuple(vmem(6)),
        scratch_shapes=[pltpu.VMEM((rows, wq.shape[1] + wk.shape[1] + wv.shape[1]), BF)],
        compiler_params=params(56),
        name="attend_back",
    )(length, hidden_grad, x, gain, normed, q, k, v, heads, logsum, wq, wk, wv, wo, cosine, sine)


def gate_rows(router_t, rows, table):
    logits = dot(router_t, rows, 1, 1)
    chosen = table > 0.5
    masked = jnp.where(chosen, logits, NEG)
    weights = jnp.where(chosen, jnp.exp(masked - jnp.max(masked, axis=0, keepdims=True)), 0.0)
    total = jnp.sum(weights, axis=0, keepdims=True)
    return weights / jnp.where(total > 0.0, total, 1.0)


def expert_kernel(
    own, groups, dp_count, capacity,
    place_ref, x_ref, dy_ref, table_ref, router_ref, wg_ref, wu_ref, wd_ref, *rest,
):
    if own:
        out_c_ref, out_g_ref, gi_ref, gg_ref, gu_ref, gd_ref, gates, xs, ys, gs, mats, gi_rows, acc_c_ref, acc_g_ref = rest
    else:
        gin_g_ref, gin_u_ref, gin_d_ref, gg_ref, gu_ref, gd_ref, gates, xs, ys, gs, mats = rest
    chunk, pair = pl.program_id(0), pl.program_id(1)
    first_expert = place_ref[1] + pair * 2
    dp_here = place_ref[0]
    rows = x_ref.shape[2]
    per_group = 1 if own else dp_count - 1
    units = groups * per_group
    slots = 2 * capacity

    def unit_place(i):
        if own:
            return i, 0
        d = dp_here + 1 + i % per_group
        return i // per_group, jnp.where(d >= dp_count, d - dp_count, d)

    @pl.when(pair == 0)
    def _():
        @pl.loop(0, units)
        def _(i):
            g, d = unit_place(i)
            gates[i] = gate_rows(router_ref[...], x_ref[g, d], table_ref[g, d].astype(F32))

    slot_id = sublanes((capacity, rows))

    @pl.loop(0, units)
    def _(i):
        g, d = unit_place(i)
        table = table_ref[g, d].astype(F32)
        pieces = []
        for j in range(2):
            pick = sublanes((EXPERTS, rows)) == first_expert + j
            ranks = jnp.sum(jnp.where(pick, table, 0.0), axis=0, keepdims=True).astype(jnp.int32) - 1
            gate = jnp.sum(jnp.where(pick, gates[i], 0.0), axis=0, keepdims=True)
            hit = slot_id == ranks
            hit_f = jnp.where(hit, 1.0, 0.0)
            gs[j, i] = jnp.broadcast_to(
                jnp.sum(jnp.where(hit, gate, 0.0), axis=-1, keepdims=True), (capacity, 128)
            )
            pieces.append(hit_f.astype(BF))
        onehot = jnp.concatenate(pieces, axis=0)
        if own:
            mats[i] = onehot
        moved_x = dot(onehot, x_ref[g, d]).astype(BF)
        moved_y = dot(onehot, dy_ref[g, d]).astype(BF)
        for j in range(2):
            cut = slice(j * capacity, (j + 1) * capacity)
            xs[j, i] = moved_x[cut]
            ys[j, i] = moved_y[cut]

    width = x_ref.shape[3]
    hidden = wg_ref.shape[2]
    terms_c, terms_g = [], []
    for j in range(2):
        x_here = xs[j].reshape(units * capacity, width)
        y_here = ys[j].reshape(units * capacity, width)
        scale = gs[j].reshape(units * capacity, 128)
        both = dot(x_here, jnp.concatenate([wg_ref[j], wu_ref[j]], axis=1))
        g_here, u_here = both[:, :hidden], both[:, hidden:]
        act_back = dot(y_here, wd_ref[j], 1, 1)
        sig = 1.0 / (1.0 + jnp.exp(-g_here))
        silu = g_here * sig
        act = silu * u_here
        act_gated = (act * scale).astype(BF)
        grad_act = act_back * scale
        grad_gate = (grad_act * u_here * sig * (1.0 + g_here * (1.0 - sig))).astype(BF)
        grad_up = (grad_act * silu).astype(BF)
        grads = jnp.concatenate([grad_gate, grad_up], axis=1)
        weight_grads = dot(x_here, grads, 0, 0)
        down = dot(act_gated, y_here, 0, 0)
        if own:
            gg_ref[j] = weight_grads[:, :hidden]
            gu_ref[j] = weight_grads[:, hidden:]
            gd_ref[j] = down
            inner = jnp.sum(act * act_back, axis=-1, keepdims=True)
            stacked = jnp.concatenate([act_gated, grads], axis=1)
            for i in range(units):
                cut = slice(i * capacity, (i + 1) * capacity)
                back = mats[i, j * capacity : (j + 1) * capacity, :]
                mats_t = dot(back, stacked[cut], 0, 0).astype(BF)
                terms_c.append(mats_t[:, :hidden])
                terms_g.append(mats_t[:, hidden:])
                gi_rows[i, j : j + 1, :] = jnp.sum(back.astype(F32) * inner[cut], axis=0, keepdims=True)
        else:
            gg_ref[j] = gin_g_ref[j] + weight_grads[:, :hidden]
            gu_ref[j] = gin_u_ref[j] + weight_grads[:, hidden:]
            gd_ref[j] = gin_d_ref[j] + down
    if own:
        down_pair = wd_ref[...].reshape(2 * hidden, width)
        in_pair = jnp.concatenate([wg_ref[0], wu_ref[0], wg_ref[1], wu_ref[1]], axis=1)
        for i in range(units):
            left_c = jnp.concatenate([terms_c[i], terms_c[units + i]], axis=1)
            left_g = jnp.concatenate([terms_g[i], terms_g[units + i]], axis=1)
            add_c = dot(left_c, down_pair)
            add_g = dot(left_g, in_pair, 1, 1)

            @pl.when(pair == 0)
            def _():
                acc_c_ref[i] = add_c
                acc_g_ref[i] = add_g
                gi_ref[i] = jnp.zeros_like(gi_ref[i])

            @pl.when(pair != 0)
            def _():
                acc_c_ref[i] += add_c
                acc_g_ref[i] += add_g

            @pl.when(pair == pl.num_programs(1) - 1)
            def _():
                out_c_ref[i] = acc_c_ref[i].astype(BF)
                out_g_ref[i] = acc_g_ref[i].astype(BF)

            pick = sublanes((EXPERTS, rows))
            gi_ref[i] = jnp.where(
                pick == first_expert, gi_rows[i, 0:1, :],
                jnp.where(pick == first_expert + 1, gi_rows[i, 1:2, :], gi_ref[i]),
            )


def expert_call(own, place, x, dy, table, router_t, wg, wu, wd, partial=None):
    groups_all, dp_count, rows, width = x.shape
    chunk_groups = 2
    chunks = groups_all // chunk_groups
    local, _, hidden = wg.shape
    pairs = local // 2
    assert chunks == 1 or pairs == 1
    capacity = rows * TOP // EXPERTS
    shape = jax.ShapeDtypeStruct
    units = chunk_groups * (1 if own else dp_count - 1)
    dp_block = 1 if own else dp_count
    dp_at = (lambda s: s[0]) if own else (lambda s: 0)
    row_block = pl.BlockSpec(
        (chunk_groups, dp_block, rows, width), lambda c, p, s: (c, dp_at(s), 0, 0), pipeline_mode=pl.Buffered(1)
    )
    in_block = pl.BlockSpec((2, width, hidden), lambda c, p, s: (p, 0, 0))
    down_block = pl.BlockSpec((2, hidden, width), lambda c, p, s: (p, 0, 0))
    in_specs = [
        row_block, row_block,
        pl.BlockSpec((chunk_groups, dp_block, EXPERTS, rows), lambda c, p, s: (c, dp_at(s), 0, 0)),
        pl.BlockSpec((EXPERTS, width), lambda c, p, s: (0, 0)),
        in_block, in_block, down_block,
    ]
    grads_out = (shape(wg.shape, F32), shape(wu.shape, F32), shape(wd.shape, F32))
    grad_specs = (in_block, in_block, down_block)
    scratch = [
        pltpu.VMEM((units, EXPERTS, rows), F32),
        pltpu.VMEM((2, units, capacity, width), BF),
        pltpu.VMEM((2, units, capacity, width), BF),
        pltpu.VMEM((2, units, capacity, 128), F32),
        pltpu.VMEM((units, 2 * capacity, rows), BF),
    ]
    operands = [x, dy, table, router_t, wg, wu, wd]
    if own:
        acc = pl.BlockSpec((chunk_groups, rows, width), lambda c, p, s: (c, 0, 0))
        out_shape = (
            shape((groups_all, rows, width), BF), shape((groups_all, rows, width), BF),
            shape((groups_all, EXPERTS, rows), F32), *grads_out,
        )
        out_specs = (acc, acc, pl.BlockSpec((chunk_groups, EXPERTS, rows), lambda c, p, s: (c, 0, 0)), *grad_specs)
        scratch += [pltpu.VMEM((units, 2, rows), F32)] + [pltpu.VMEM((units, rows, width), F32)] * 2
        aliases = {}
    else:
        out_shape, out_specs = grads_out, grad_specs
        in_specs += list(grad_specs)
        operands += list(partial)
        aliases = {8: 0, 9: 1, 10: 2}
    return pl.pallas_call(
        functools.partial(expert_kernel, own, chunk_groups, dp_count, capacity),
        out_shape=out_shape,
        grid_spec=pltpu.PrefetchScalarGridSpec(
            num_scalar_prefetch=1, grid=(chunks, pairs), in_specs=in_specs, out_specs=out_specs, scratch_shapes=scratch
        ),
        input_output_aliases=aliases,
        compiler_params=params(60, dimension_semantics=("arbitrary", "arbitrary")),
        name="experts_own" if own else "experts_other",
    )(place, *operands)


def on_device(
    tokens, cotangent, seq_lengths, deal_order, routes, slot_order, first_gain, w_query, w_key, w_value, w_out,
    second_gain, w_router, w_gate, w_up, w_down,
):
    dp_count = lax.axis_size("dp")
    dp_index = lax.axis_index("dp")
    tensor_count = lax.axis_size("tensor")
    tensor_index = lax.axis_index("tensor")
    expert_count = lax.axis_size("expert")
    expert_index = lax.axis_index("expert")
    rows, width = tokens.shape
    row_share, col_share = rows // tensor_count, width // tensor_count
    row_start = tensor_index * row_share
    everywhere = ("expert", "dp", "tensor")
    rows_all = ("expert", "dp")

    def own_rows(values):
        return lax.dynamic_slice_in_dim(values, row_start, row_share, 0)

    order = deal_order[0]
    dealt_length = seq_lengths[0][order[dp_index]]
    table = make_table(dealt_length.reshape(1), routes, slot_order)
    tables_dealt = lax.all_gather(table, "dp", axis=0)
    inverse = jnp.sum(
        jnp.where(
            order[None, :] == jnp.arange(dp_count, dtype=jnp.int32)[:, None],
            jnp.arange(dp_count, dtype=jnp.int32)[None, :], 0,
        ), axis=1,
    )
    my_table = tables_dealt[inverse[dp_index]]
    tables = lax.all_gather(my_table, rows_all, axis=0).reshape(expert_count, dp_count, EXPERTS, rows)
    length = seq_lengths[0][dp_index].reshape(1)

    dy_all = lax.all_gather(own_rows(cotangent), everywhere, axis=0, tiled=True)
    dy_all = dy_all.reshape(expert_count, dp_count, rows, width)

    cosine, sine = (jnp.asarray(values) for values in rotary_tables(rows))
    gain1 = first_gain.reshape(1, width)
    gain2 = second_gain.reshape(1, width).astype(F32)
    part, normed, q, k, v, heads, logsum = attend(
        length, tokens, gain1, w_query, w_key, w_value, w_out, cosine, sine
    )
    attention = lax.psum_scatter(part, "tensor", scatter_dimension=0, tiled=True)
    x_share = own_rows(tokens).astype(F32)
    hidden = x_share + attention.astype(F32)
    scale2 = lax.rsqrt(jnp.mean(hidden * hidden, axis=-1, keepdims=True) + EPS)
    hat2 = hidden * scale2
    second_normed = (hat2 * gain2).astype(BF)
    x_all = lax.all_gather(second_normed, everywhere, axis=0, tiled=True).reshape(expert_count, dp_count, rows, width)

    router_t = w_router.T
    place = jnp.stack([dp_index, expert_index * w_gate.shape[0]]).astype(jnp.int32)
    acc_c, acc_g, gi, pg, pu, pd = expert_call(
        True, place, x_all, dy_all, tables, router_t, w_gate, w_up, w_down
    )
    both = ("expert", "tensor")
    moe_rows = lax.psum_scatter(acc_c.reshape(-1, width), both, scatter_dimension=0, tiled=True)
    moe_grad = lax.psum_scatter(acc_g.reshape(-1, width), both, scatter_dimension=0, tiled=True)
    gate_in = lax.psum_scatter(
        gi.transpose(0, 2, 1).reshape(-1, EXPERTS), both, scatter_dimension=0, tiled=True
    )
    out_rows = (hidden + moe_rows.astype(F32)).astype(BF)
    block_out = lax.all_to_all(out_rows, "tensor", split_axis=1, concat_axis=0, tiled=True)

    share_table = own_rows(my_table.astype(F32).T)
    logits = jnp.dot(second_normed, w_router, preferred_element_type=F32)
    chosen = share_table > 0.5
    masked = jnp.where(chosen, logits, NEG)
    weights = jnp.where(chosen, jnp.exp(masked - jnp.max(masked, axis=-1, keepdims=True)), 0.0)
    total = jnp.sum(weights, axis=-1, keepdims=True)
    gates = weights / jnp.where(total > 0.0, total, 1.0)
    logit_grad = (gates * (gate_in - jnp.sum(gates * gate_in, axis=-1, keepdims=True))).astype(BF)
    router_term = jnp.einsum("td,te->de", second_normed, logit_grad, preferred_element_type=F32)
    normed_grad = moe_grad.astype(F32) + jnp.einsum("te,de->td", logit_grad, w_router, preferred_element_type=F32)
    second_term = jnp.sum(normed_grad * hat2, axis=0)
    scaled = normed_grad * gain2
    hidden_grad = own_rows(cotangent).astype(F32) + scale2 * (
        scaled - hat2 * jnp.mean(scaled * hat2, axis=-1, keepdims=True)
    )
    hidden_grad_all = lax.all_gather(hidden_grad.astype(BF), "tensor", axis=0, tiled=True)
    live = (jnp.arange(rows, dtype=jnp.int32) < length[0])[:, None]
    branch = jnp.where(live, hidden_grad_all, jnp.zeros((), BF))
    out_term = jnp.einsum("ta,td->ad", heads, branch, preferred_element_type=F32).astype(BF)
    first, stat, gain1_term, q_term, k_term, v_term = attend_back(
        length, hidden_grad_all, tokens, gain1, normed, q, k, v, heads, logsum,
        w_query, w_key, w_value, w_out, cosine, sine,
    )
    gate_grad, up_grad, down_grad = expert_call(
        False, place, x_all, dy_all, tables, router_t, w_gate, w_up, w_down, (pg, pu, pd)
    )
    first_cols = lax.psum_scatter(first, "tensor", scatter_dimension=1, tiled=True).astype(F32)
    stat_sum = lax.psum(stat[:, 0], "tensor")[:, None] / width
    out_sum, q_sum, k_sum, v_sum = lax.psum((out_term, q_term, k_term, v_term), rows_all)
    gain1_sum, gain2_sum, router_sum = lax.psum((gain1_term, second_term, router_term), everywhere)
    cols = functools.partial(lax.dynamic_slice_in_dim, start_index=tensor_index * col_share, slice_size=col_share, axis=1)
    x32 = tokens.astype(F32)
    scale1 = lax.rsqrt(jnp.mean(x32 * x32, axis=-1, keepdims=True) + EPS)
    input_grad = cols(hidden_grad_all).astype(F32) + scale1 * (
        first_cols * cols(gain1.astype(F32)) - cols(x32) * scale1 * stat_sum
    )
    return (
        block_out, input_grad.astype(BF), gain1_sum.reshape(width), q_sum.astype(F32), k_sum.astype(F32),
        v_sum.astype(F32), out_sum.astype(F32), gain2_sum, router_sum, gate_grad, up_grad, down_grad,
    )


def solution(mesh):
    rows2 = P(("expert", "dp"), None)
    placed = (
        rows2, rows2, P("expert", None), P("expert", None), rows2, rows2, P(),
        P(None, "tensor"), P(None, "tensor"), P(None, "tensor"), P("tensor", None), P(), P(),
        P("expert", None, "tensor"), P("expert", None, "tensor"), P("expert", "tensor", None),
    )
    return jax.shard_map(
        on_device,
        mesh=mesh,
        in_specs=placed,
        out_specs=(
            P(("expert", "dp"), "tensor"), P(("expert", "dp"), "tensor"), P(),
            P(None, "tensor"), P(None, "tensor"), P(None, "tensor"), P("tensor", None), P(), P(),
            P("expert", None, "tensor"), P("expert", None, "tensor"), P("expert", "tensor", None),
        ),
        check_vma=False,
    )
```

time: 1780 us -> 667 us (0.37)
  waiting for transfers between devices: 1000 us -> 345 us
  matrix products: 323 us -> 4.97 us
  local copies, waits for them, and re-layouts: 291 us -> 20.2 us
  Pallas kernels: 0 us -> 159 us
  blocking collectives: 31.7 us -> 94.7 us
  other arithmetic: 66.4 us -> 18.8 us
  starting transfers between devices: 29.2 us -> 4 us
    psum x5 -> x2, waiting for transfers between devices: 654 us -> 99.1 us  [the longest x1 99.1 us: on_device(): lax.psum((gain1_term, second_term, router_term), everywhere)]
    dot_general x183 -> x3, matrix products: 322 us -> 4.14 us  [the longest x1 2.55 us: on_device(): jnp.einsum('ta,td->ad', heads, branch, preferred_element_type=F32)]
    all_to_all x4 -> x1, waiting for transfers between devices: 308 us -> 5.09 us  [on_device(): lax.all_to_all(out_rows, 'tensor', split_axis=1, concat_axis=0, tiled=True)]
    gather x14 -> x0, local copies, waits for them, and re-layouts: 218 us -> none  [the longest x5 33.6 us: on_device(): chosen = jnp.take_along_axis(logits, routes, axis=1)]
    pallas_call x0 -> x5, Pallas kernels: none -> 159 us  [the longest x2 137 us: expert_call(): pl.pallas_call(functools.partial(expert_kernel, own, chunk_groups, dp_cou...]
    reduce_scatter x1 -> x5, waiting for transfers between devices: 15.8 us -> 143 us  [the longest x1 43.8 us: on_device(): lax.psum_scatter(acc_g.reshape(-1, width), both, scatter_dimension=0, til...]
    all_gather x4 -> x3, waiting for transfers between devices: 22 us -> 94.9 us  [the longest x1 78.7 us: on_device(): lax.all_gather(second_normed, everywhere, axis=0, tiled=True)]
    all_gather x0 -> x2, blocking collectives: none -> 48.7 us  [the longest x1 34.6 us: on_device(): lax.all_gather(my_table, rows_all, axis=0)]
  transfers between devices with their start and end apart: 14 -> 11, of which waited for: 12 -> 8; matrix products, arithmetic and copies ran while one was open for 18% -> 3% of each run, Pallas kernels for 0% -> 13%
where the time goes in v1:
time: 667 us; the launch traced here: 666 us
  waiting for transfers between devices  345 us (52%)
  Pallas kernels  159 us (24%)
  blocking collectives  94.7 us (14%)
  local copies, waits for them, and re-layouts  20.2 us (3%)
  between operations  19.8 us (3%)
  other arithmetic  18.8 us (3%)
    pallas_call x2, Pallas kernels, expert_call(): pl.pallas_call(functools.partial(expert_kernel, own, chunk_groups, dp_cou...  137 us
    psum x1, waiting for transfers between devices, on_device(): lax.psum((gain1_term, second_term, router_term), everywhere)  99.1 us
    all_gather x1, waiting for transfers between devices, on_device(): lax.all_gather(second_normed, everywhere, axis=0, tiled=True)  78.7 us
    reduce_scatter x1, waiting for transfers between devices, on_device(): lax.psum_scatter(acc_g.reshape(-1, width), both, scatter_dimension=0, til...  43.8 us
    reduce_scatter x1, waiting for transfers between devices, on_device(): lax.psum_scatter(acc_c.reshape(-1, width), both, scatter_dimension=0, til...  43.4 us
    psum x1, blocking collectives, on_device(): lax.psum((gain1_term, second_term, router_term), everywhere)  40.2 us
    all_gather x1, blocking collectives, on_device(): lax.all_gather(my_table, rows_all, axis=0)  34.6 us
    reduce_scatter x1, waiting for transfers between devices, on_device(): lax.psum_scatter(gi.transpose(0, 2, 1).reshape(-1, EXPERTS), both, scatte...  30.3 us
  transfers between devices with their start and end apart: 11, of which 8 were waited for; matrix products, arithmetic and copies ran while one was open for 3% of the time, Pallas kernels for 13%

profile of v1, /device:TPU:0, one launch (start us, length us, event | category | flops | bytes accessed | tf_op | source)
XLA Modules:
  0.0 666.2 jit_solution(7857109841425780319)
XLA Ops:
  19.3 6.7 %attend.1 = (bf16[512,1024]{1,0:T(8,128)(2,1)}, bf16[512,1024]{1,0:T(8,128)(2,1)S(1)}, bf16[512,256]{1,0:T(8,128)(2,1)S(1)}, bf16[512,128]{1,0:T(8,128)(2,1)S(1)...) custom-call(s32[1]{0:T(128)} %bitcast.length_ref, bf16[512,1024]{1,0:T(8,128)(2,1)} %x_ref.3, ...), custom_call_target="tpu_custom_call" | custom-call | tf_op jit(solution)/shard_map/attend/pallas_call | solution.py:167
  31.5 25.9 %reduce-scatter.6.cloned.1.call-done = bf16[128,1024]{1,0:T(8,128)(2,1)} async-done(((bf16[512,1024]{1,0:T(8,128)(2,1)}), bf16[128,1024]{1,0:T(8,128)(2,1)}) %reduce-scatter.6.cloned.1.call-update) | async-done | bytes 262160 | tf_op jit(solution)/shard_map/reduce_scatter | solution.py:501
  63.3 5.5 tables.1
  68.8 14.1 %all-gather = bf16[128,512]{1,0:T(8,128)(2,1)S(1)} all-gather(bf16[32,512]{1,0:T(8,128)(2,1)S(1)} %tables.1), channel_id=2, replica_groups=mesh['expert'=2,'tensor'=4,'dp'=4] {'dp'}, dimensions={0}, use_global_device_ids=true | all-gather | bytes 163840 | tf_op jit(solution)/shard_map/all_gather | solution.py:481
  83.5 34.6 %all_gather.22 = bf16[8,32,512]{2,1,0:T(8,128)(2,1)} all-gather(bf16[1,32,512]{2,1,0:T(8,128)(2,1)S(1)} %constant_dynamic-slice_fusion), channel_id=1, replica_groups=mesh['expert'=2,'tensor'=4,'dp'=4] {'expert','dp'}, dimensions={0}, use_global_device_ids=true | all-gather | bytes 294912 | tf_op jit(solution)/shard_map/all_gather | solution.py:489
  118.1 78.7 %all-gather.5.cloned.1.call-done = bf16[4096,1024]{1,0:T(8,128)(2,1)} async-done(((bf16[128,1024]{1,0:T(8,128)(2,1)}), bf16[4096,1024]{1,0:T(8,128)(2,1)}) %all-gather.5.cloned.1.call-update) | async-done | bytes 8388624 | tf_op jit(solution)/shard_map/all_gather | solution.py:507
  196.9 58.0 %experts_own.1 = (bf16[2,512,1024]{2,1,0:T(8,128)(2,1)}, bf16[2,512,1024]{2,1,0:T(8,128)(2,1)}, f32[2,32,512]{2,1,0:T(8,128)}, f32[16,1024,128]{2,1,0:T(8,128)},...) custom-call(s32[2]{0:T(128)} %pad_add_fusion.place_ref, bf16[2,4,512,1024]{3,2,1,0:T(8,128)(2,1)} %bitcast.53, ...), custom_call_target="tpu_custom_call" | custom-call | tf_op jit(solution)/shard_map/experts_own/pallas_call | solution.py:447
  258.4 30.3 %reduce-scatter.12.cloned.1.call-done = f32[128,32]{0,1:T(8,128)} async-done(((f32[1024,32]{0,1:T(8,128)}), f32[128,32]{0,1:T(8,128)}) %reduce-scatter.12.cloned.1.call-update) | async-done | bytes 16400 | tf_op jit(solution)/shard_map/reduce_scatter | solution.py:517
  289.5 43.8 %reduce-scatter.10.cloned.1.call-done = bf16[128,1024]{1,0:T(8,128)(2,1)} async-done(((bf16[1024,1024]{1,0:T(8,128)(2,1)}), bf16[128,1024]{1,0:T(8,128)(2,1)}) %reduce-scatter.10.cloned.1.call-update) | async-done | bytes 262160 | tf_op jit(solution)/shard_map/reduce_scatter | solution.py:516
  334.7 43.4 %reduce-scatter.8.cloned.1.call-done = bf16[128,1024]{1,0:T(8,128)(2,1)} async-done(((bf16[1024,1024]{1,0:T(8,128)(2,1)}), bf16[128,1024]{1,0:T(8,128)(2,1)}) %reduce-scatter.8.cloned.1.call-update) | async-done | bytes 262160 | tf_op jit(solution)/shard_map/reduce_scatter | solution.py:515
  378.1 2.0 add_convert_fusion.1
  380.8 16.2 %all-gather.9.cloned.1.call-done.hidden_grad_ref = bf16[512,1024]{1,0:T(8,128)(2,1)} async-done(((bf16[128,1024]{1,0:T(8,128)(2,1)}), bf16[512,1024]{1,0:T(8,128)(2,1)}) %all-gather.9.cloned.1.call-update) | async-done | bytes 1048592 | tf_op jit(solution)/shard_map/all_gather | solution.py:538
  396.9 2.5 convolution_convert_fusion
  399.5 10.5 %attend_back.1 = (bf16[512,1024]{1,0:T(8,128)(2,1)}, f32[512,128]{1,0:T(8,128)}, f32[1,1024]{1,0:T(1,128)}, bf16[1024,256]{1,0:T(8,128)(2,1)}, bf16[1024,128]{1,0:T(8,128)(2,1)}, /*index=5*/bf16[1024,128]{1,0:T(8,128)(2,1)}) custom-call(s32[1]{0:T(128)} %bitcast.length_ref, bf16[512,1024]{1,0:T(8,128)(2,1)} %all-gather.9.cloned.1.call-done.hidden_grad_ref, ...), custom_call_target="tpu_custom_call" | custom-call | tf_op jit(solution)/shard_map/attend_back/pallas_call | solution.py:252
  412.7 78.5 %experts_other.1 = (f32[16,1024,128]{2,1,0:T(8,128)}, f32[16,1024,128]{2,1,0:T(8,128)}, f32[16,128,1024]{2,1,0:T(8,128)}) custom-call(s32[2]{0:T(128)} %pad_add_fusion.place_ref, bf16[2,4,512,1024]{3,2,1,0:T(8,128)(2,1)} %bitcast.54, bf16[2,4,512,1024]{3,2,1,0:T(8,128)(2,1)} %bitcast.52, ...), custom_call_target="tpu_custom_call", output_to_operand_aliasing={{0}: (8, {}), {1}: (9, {}), {2}: (10, {})} | custom-call | tf_op jit(solution)/shard_map/experts_other/pallas_call | solution.py:447
  492.0 3.4 all-to-all-start
  496.3 5.1 all-to-all-done
  501.5 5.8 psum.56
  507.3 40.2 %all-reduce = (f32[1024]{0:T(1024)}, f32[1024]{0:T(1024)}) all-reduce(f32[1024]{0:T(1024)S(1)} %bitcast.71, f32[1024]{0:T(1024)S(1)} %get-tuple-element.56), channel_id=1, replica_groups=mesh['expert'=2,'tensor'=4,'dp'=4] {'expert','dp','tensor'}, use_global_device_ids=true, to_apply=%region_13.14 | all-reduce | flops 2048 | bytes 16384 | tf_op jit(solution)/shard_map/psum | solution.py:552
  547.5 2.1 convert_element_type.82
  549.6 1.8 convert_element_type.83
  553.2 2.1 convert_element_type.86
  555.3 2.1 add_convert_fusion
  557.4 99.1 %all-reduce.5.cloned.1.call-done = f32[1024,32]{0,1:T(8,128)} async-done(((f32[1024,32]{0,1:T(8,128)}), f32[1024,32]{0,1:T(8,128)}) %all-reduce.5.cloned.1.call-update) | async-done | bytes 131088 | tf_op jit(solution)/shard_map/psum | solution.py:552
  (107 shorter events, 34.0 us)
Async XLA Ops:
  8.0 52.4 %copy-start.25 = (s32[1,4]{1,0:T(1,128)S(1)}, s32[1,4]{1,0:T(1,128)}, u32[]{:S(2)}) copy-start(s32[1,4]{1,0:T(1,128)} %param.21) | copy-start | bytes 52
  8.0 54.4 %copy-start.21 = (s32[512,8]{0,1:T(8,128)S(1)}, s32[512,8]{0,1:T(8,128)}, u32[]{:S(2)}) copy-start(s32[512,8]{0,1:T(8,128)} %param.22) | copy-start | bytes 49156
  8.0 55.2 %copy-start.13 = (s32[1,4096]{1,0:T(1,128)S(1)}, s32[1,4096]{1,0:T(1,128)}, u32[]{:S(2)}) copy-start(s32[1,4096]{1,0:T(1,128)} %order_ref.1) | copy-start | bytes 49156
  8.0 49.4 %reduce-scatter.6.cloned.1.call-start = ((), (), s32[]{:S(2)}) async-start(), calls=%async_computation.6 | async-start | bytes 1310720 | tf_op jit(solution)/shard_map/reduce_scatter | solution.py:501
  11.3 243.6 %copy-start.12 = (bf16[1,1024]{1,0:T(2,128)(2,1)}, bf16[1,1024]{1,0:T(2,128)(2,1)S(1)}, u32[]{:S(2)}) copy-start(bf16[1,1024]{1,0:T(2,128)(2,1)S(1)} %reshape.100.gain_ref) | copy-start | bytes 6148
  19.2 12.3 %copy-start.24 = (bf16[1024]{0:T(1024)(128)(2,1)S(1)}, bf16[1024]{0:T(1024)(128)(2,1)}, u32[]{:S(2)}) copy-start(bf16[1024]{0:T(1024)(128)(2,1)} %param.29) | copy-start | bytes 6148
  19.3 38.2 %copy-start.14 = (bf16[512,1024]{1,0:T(8,128)(2,1)S(1)}, bf16[512,1024]{1,0:T(8,128)(2,1)}, u32[]{:S(2)}) copy-start(bf16[512,1024]{1,0:T(8,128)(2,1)} %x_ref.3) | copy-start | bytes 3145732
  29.6 367.3 %copy-start.8 = (bf16[512,256]{1,0:T(8,128)(2,1)}, bf16[512,256]{1,0:T(8,128)(2,1)S(1)}, u32[]{:S(2)}) copy-start(bf16[512,256]{1,0:T(8,128)(2,1)S(1)} %get-tuple-element.42.heads_ref) | copy-start | bytes 786436
  29.7 88.5 %all-gather.7.cloned.1.call-start = ((), (), s32[]{:S(2)}) async-start(), calls=%async_computation.8 | async-start | bytes 8650752 | tf_op jit(solution)/shard_map/all_gather | solution.py:492
  31.5 165.4 %all-gather.5.cloned.1.call-start = ((), (), s32[]{:S(2)}) async-start(), calls=%async_computation.7 | async-start | bytes 8650752 | tf_op jit(solution)/shard_map/all_gather | solution.py:507
  60.4 228.3 %reduce-scatter.12.cloned.1.call-start = ((), (), s32[]{:S(2)}) async-start(), calls=%async_computation.11 | async-start | bytes 147456 | tf_op jit(solution)/shard_map/reduce_scatter | solution.py:517
  254.9 3.2 copy-start.16
  254.9 78.4 %copy-start.17 = (bf16[128,1024]{1,0:T(8,128)(2,1)S(1)}, bf16[128,1024]{1,0:T(8,128)(2,1)}, u32[]{:S(2)}) copy-start(bf16[128,1024]{1,0:T(8,128)(2,1)} %reduce-scatter.6.cloned.1.call-done) | copy-start | bytes 786436
  256.6 76.7 %reduce-scatter.10.cloned.1.call-start = ((), (), s32[]{:S(2)}) async-start(), calls=%async_computation.10 | async-start | bytes 2359296 | tf_op jit(solution)/shard_map/reduce_scatter | solution.py:516
  257.3 120.7 %reduce-scatter.8.cloned.1.call-start = ((), (), s32[]{:S(2)}) async-start(), calls=%async_computation.9 | async-start | bytes 2359296 | tf_op jit(solution)/shard_map/reduce_scatter | solution.py:515
  257.9 139.0 %all-gather.9.cloned.1.call-start = ((), (), s32[]{:S(2)}) async-start(), calls=%async_computation.12 | async-start | bytes 1310720 | tf_op jit(solution)/shard_map/all_gather | solution.py:538
  380.1 167.5 %all-reduce.7.cloned.1.call-start = ((), (), s32[]{:S(2)}) async-start(), calls=%async_computation.15 | async-start | bytes 3145728 | tf_op jit(solution)/shard_map/psum | solution.py:551
  399.5 11.2 %copy-start.15 = (bf16[512,1024]{1,0:T(8,128)(2,1)S(1)}, bf16[512,1024]{1,0:T(8,128)(2,1)}, u32[]{:S(2)}) copy-start(bf16[512,1024]{1,0:T(8,128)(2,1)} %x_ref.3) | copy-start | bytes 3145732
  410.0 145.3 %reduce-scatter.14.cloned.1.call-start = ((), (), s32[]{:S(2)}) async-start(), calls=%async_computation.13 | async-start | bytes 1310720 | tf_op jit(solution)/shard_map/reduce_scatter | solution.py:549
  412.7 82.8 %copy-start.20 = (f32[128,32]{0,1:T(8,128)S(1)}, f32[128,32]{0,1:T(8,128)}, u32[]{:S(2)}) copy-start(f32[128,32]{0,1:T(8,128)} %reduce-scatter.12.cloned.1.call-done) | copy-start | bytes 49156
  412.7 88.7 %copy-start.19 = (f32[512,128]{1,0:T(8,128)S(1)}, f32[512,128]{1,0:T(8,128)}, u32[]{:S(2)}) copy-start(f32[512,128]{1,0:T(8,128)} %get-tuple-element.45) | copy-start | bytes 786436
  412.7 94.6 %copy-start.23 = (f32[1,1024]{1,0:T(1,128)S(1)}, f32[1,1024]{1,0:T(1,128)}, u32[]{:S(2)}) copy-start(f32[1,1024]{1,0:T(1,128)} %get-tuple-element.46) | copy-start | bytes 12292
  492.0 9.4 %all-to-all-start = ((bf16[128,4,256]{2,0,1:T(8,128)(2,1)}), bf16[128,4,256]{2,0,1:T(8,128)(2,1)S(1)}, u32[]{:S(2)}, u32[]{:S(2)}) async-start(bf16[128,4,256]{2,0,1:T(8,128)(2,1)} %bitcast.50), calls=%async_computation.2 | async-start | bytes 524288 | tf_op jit(solution)/shard_map/all_to_all | solution.py:521
  495.4 161.1 %all-reduce.5.cloned.1.call-start = ((), (), s32[]{:S(2)}) async-start(), calls=%async_computation.14 | async-start | bytes 262144 | tf_op jit(solution)/shard_map/psum | solution.py:552
  (13 other events, 15.2 us)
Sparse Core Ops, SparseCore 0:
  29.8 27.6 reduce-scatter.5
  256.7 31.9 reduce-scatter.11
  292.0 41.2 reduce-scatter.9
  336.8 41.2 reduce-scatter.7
  380.2 16.6 all-gather.8
  410.1 89.9 all-reduce.6
  502.6 24.4 reduce-scatter.13
  534.2 122.3 all-reduce.4
Sparse Core Ops, SparseCore 1:
  34.0 82.2 all-gather.6
  120.1 76.8 all-gather.4

commit v2 on v1

v2 whole, which is shorter than its diff:
```python
import functools

import jax
import jax.numpy as jnp
import numpy as np
from jax import lax
from jax.experimental import pallas as pl
from jax.experimental.pallas import tpu as pltpu
from jax.sharding import PartitionSpec as P

HEADS = 16
KV_HEADS = 8
HEAD_DIM = 64
EXPERTS = 32
TOP = 8
SLOT = 512

EPS = 1e-06
THETA = 10000.0
NEG = -1e30
BF = jnp.bfloat16
F32 = jnp.float32
MIB = 1 << 20


def dot(a, b, ca=1, cb=0):
    return lax.dot_general(a, b, (((ca,), (cb,)), ((), ())), preferred_element_type=F32)


def vmem(count=1):
    return [pl.BlockSpec(memory_space=pltpu.VMEM)] * count


def params(mib, **more):
    return pltpu.CompilerParams(vmem_limit_bytes=mib * MIB, **more)


def rotary_tables(rows):
    places = np.arange(rows, dtype=np.float32)[:, None]
    halfway = HEAD_DIM // 2
    spread = np.float32(THETA) ** (-2.0 * np.arange(halfway, dtype=np.float32) / HEAD_DIM)
    angles = (places * spread.astype(np.float32)[None, :]).astype(np.float32)
    copies = 128 // halfway
    return (
        np.tile(np.cos(angles), (1, copies)).astype(np.float32),
        np.tile(np.sin(angles), (1, copies)).astype(np.float32),
    )


def rotate128(values, cosine, sine, low_half):
    half = HEAD_DIM // 2
    up = pltpu.roll(values, 128 - half, 1)
    down = pltpu.roll(values, half, 1)
    return values * cosine + jnp.where(low_half, -up, down) * sine


def lanes(shape):
    return lax.broadcasted_iota(jnp.int32, shape, len(shape) - 1)


def sublanes(shape):
    return lax.broadcasted_iota(jnp.int32, shape, len(shape) - 2)


def bits_of(count):
    return [1 << i for i in range(count.bit_length() - 1)]


def flip(value, mask):
    for bit in bits_of(1 << 16):
        if mask & bit:
            value = value + bit - 2 * bit * lax.rem(lax.div(value, bit), 2)
    return value


class Net:
    def __init__(self, send_sem, recv_sem):
        self.send_sem, self.recv_sem, self.used, self.copies = send_sem, recv_sem, 0, []
        self.me = {axis: lax.axis_index(axis) for axis in ("expert", "tensor", "dp")}

    def barrier(self, partners):
        sem = pltpu.get_barrier_semaphore()
        for axis, mask in partners:
            pl.semaphore_signal(
                sem, inc=1, device_id={axis: flip(self.me[axis], mask)}, device_id_type=pl.DeviceIdType.MESH
            )
        pl.semaphore_wait(sem, len(partners))

    def send(self, source, target, axis, mask):
        k = self.used
        self.used += 1
        copy = pltpu.make_async_remote_copy(
            src_ref=source, dst_ref=target, send_sem=self.send_sem.at[k], recv_sem=self.recv_sem.at[k],
            device_id={axis: flip(self.me[axis], mask)}, device_id_type=pl.DeviceIdType.MESH,
        )
        copy.start()
        self.copies.append(copy)
        return copy

    def close(self):
        for copy in self.copies:
            copy.wait_send()


class Gather:
    def __init__(self, net, at, steps, known=((0, 0),), first=None):
        self.net, self.at, self.steps, self.known, self.first, self.flight = net, at, list(steps), list(known), first, []

    def start(self):
        axis, mask = self.steps.pop(0)
        fresh = []
        for re, rt in self.known:
            place = self.at(re, rt)
            source = self.first if self.first is not None and (re, rt) == (0, 0) else place
            self.flight.append(self.net.send(source, place, axis, mask))
            fresh.append((re ^ mask, rt) if axis == "expert" else (re, rt ^ mask))
        self.known += fresh

    def finish(self):
        for copy in self.flight:
            copy.wait_recv()
        self.flight = []


class Reduce:
    def __init__(self, net, at, landing, steps, chunks):
        self.net, self.at, self.landing, self.steps, self.live = net, at, landing, list(steps), list(chunks)
        self.used, self.flight = 0, []

    def start(self):
        axis, mask = self.steps.pop(0)
        side = 0 if axis == "expert" else 1
        going = [r for r in self.live if r[side] & mask]
        self.live = [r for r in self.live if not r[side] & mask]
        for r in going:
            kept = (r[0] ^ mask, r[1]) if side == 0 else (r[0], r[1] ^ mask)
            copy = self.net.send(self.at(*r), self.landing(self.used), axis, mask)
            self.flight.append((kept, copy, self.used))
            self.used += 1
        if self.steps:
            axis, mask = self.steps[0]
            side = 0 if axis == "expert" else 1
            self.flight.sort(key=lambda item: 0 if item[0][side] & mask else 1)

    def finish(self):
        for kept, copy, slot in self.flight:
            copy.wait_recv()
            place = self.at(*kept)
            place[...] = (place[...].astype(F32) + self.landing(slot)[...].astype(F32)).astype(BF)
        self.flight = []


TABLE_ROWS = 48


def table_of(length, routes_ref, order_ref):
    rows = routes_ref.shape[1]
    capacity = rows * TOP // EXPERTS
    entries = rows * TOP
    chunk = 512
    routes_t = routes_ref[...].astype(F32).astype(BF)
    upper = (sublanes((chunk, chunk)) < lanes((chunk, chunk))).astype(F32).astype(BF)
    expert_row = sublanes((EXPERTS, chunk))

    def body(step, carried):
        counts, table = carried
        entry = order_ref[:, pl.ds(pl.multiple_of(step * chunk, chunk), chunk)]
        row, choice = entry // TOP, entry % TOP
        onehot_row = (sublanes((rows, chunk)) == row).astype(F32).astype(BF)
        picked = dot(routes_t, onehot_row)
        expert = jnp.sum(jnp.where(sublanes((TOP, chunk)) == choice, picked, 0.0), axis=0, keepdims=True)
        member = (expert_row.astype(F32) == expert) & (row < length)
        member_f = member.astype(F32)
        before = dot(member_f.astype(BF), upper) + counts
        value = jnp.where(member, jnp.minimum(before, float(capacity)) + 1.0, 0.0)
        table = table + dot(value.astype(BF), onehot_row, 1, 1)
        return counts + jnp.sum(member_f, axis=1, keepdims=True), table

    _, table = lax.fori_loop(
        0, entries // chunk, body, (jnp.zeros((EXPERTS, 1), F32), jnp.zeros((EXPERTS, rows), F32))
    )
    return table


def given_table(tables, index, dp_here):
    total = 0.0
    for j in range(tables.shape[1]):
        source = tables[index, j, EXPERTS : EXPERTS + 16, :].astype(F32)[0:1]
        total = total + jnp.where(source == dp_here, tables[index, j, 0:EXPERTS, :].astype(F32), 0.0)
    return total


def head_parts(q, k_a, k_b, index, low_lane):
    block = q[:, (index // 2) * 128 : (index // 2) * 128 + 128]
    mine = low_lane if index % 2 == 0 else jnp.logical_not(low_lane)
    return jnp.where(mine, block, jnp.zeros((), block.dtype)), (k_a if index % 2 == (index // 2) % 2 else k_b)


def swap(block):
    return pltpu.roll(block.astype(F32), HEAD_DIM, 1).astype(BF)


def front_kernel(
    sizes,
    lengths_ref, order_of_ref, x_ref, gain_ref, wq_ref, wk_ref, wv_ref, wo_ref, cos_ref, sin_ref, gain2_ref, routes_ref, order_ref, dy_ref,
    normed_ref, q_ref, k_ref, v_ref, heads_ref, logsum_ref, hidden_ref, share_ref, tables_ref, xown_ref, dyown_ref,
    part, landing, send_sem, recv_sem, local_sem,
):
    expert_count, tensor_count, dp_count = sizes
    rows, width = x_ref.shape
    share = rows // tensor_count
    half = rows // 2
    net = Net(send_sem, recv_sem)
    me_e, me_t, me_d = net.me["expert"], net.me["tensor"], net.me["dp"]
    expert_bits = [("expert", b) for b in bits_of(expert_count)]
    tensor_bits = [("tensor", b) for b in bits_of(tensor_count)]
    net.barrier(expert_bits + tensor_bits + [("dp", m) for m in range(1, dp_count)])

    keep_dy = pltpu.make_async_copy(dy_ref, dyown_ref.at[me_e], local_sem.at[0])
    keep_dy.start()
    half_start = pl.multiple_of(lax.rem(me_t, 2) * half, half)
    dy_half = Gather(
        net, lambda re, rt: dyown_ref.at[flip(me_e, re), pl.ds(half_start, half)], expert_bits,
        first=dy_ref.at[pl.ds(half_start, half)],
    )
    dy_half.start()

    length, source, dealt_length = lengths_ref[0, me_d], order_of_ref[0, me_d], 0
    for i in range(dp_count):
        dealt_length = jnp.where(source == i, lengths_ref[0, i], dealt_length)
    x = x_ref[...].astype(F32)
    scale = lax.rsqrt(jnp.mean(x * x, axis=-1, keepdims=True) + EPS)
    normed = (x * scale * gain_ref[...].astype(F32)[None, :]).astype(BF)
    normed_ref[...] = normed
    cosine, sine = cos_ref[...], sin_ref[...]
    lane = lanes((rows, 128))
    low_half = lane % HEAD_DIM < HEAD_DIM // 2
    low_lane = lane < HEAD_DIM
    q_pre = dot(normed, wq_ref[...])
    for block in range(q_pre.shape[1] // 128):
        cut = slice(block * 128, block * 128 + 128)
        q_ref[:, cut] = rotate128(q_pre[:, cut], cosine, sine, low_half).astype(BF)
    k = rotate128(dot(normed, wk_ref[...]), cosine, sine, low_half).astype(BF)
    v = dot(normed, wv_ref[...]).astype(BF)
    k_ref[...] = k
    v_ref[...] = v
    q = q_ref[...]
    k_b, v_b = swap(k), swap(v)
    row, col = sublanes((rows, rows)), lanes((rows, rows))
    allowed = (col <= row) & (col < length)
    logsum = jnp.zeros((rows, 128), F32)
    pair = None
    for index in range(q.shape[1] // HEAD_DIM):
        q_one, k_one = head_parts(q, k, k_b, index, low_lane)
        v_one = v if index % 2 == (index // 2) % 2 else v_b
        scores = jnp.where(allowed, dot(q_one, k_one, 1, 1) * (HEAD_DIM**-0.5), NEG)
        highest = jnp.max(scores, axis=-1, keepdims=True)
        weights = jnp.exp(scores - highest)
        total = jnp.sum(weights, axis=-1, keepdims=True)
        mixed = dot((weights / total).astype(BF), v_one)
        logsum = jnp.where(lane == index, highest + jnp.log(total), logsum)
        if index % 2 == 0:
            pair = mixed
        else:
            cut = slice((index // 2) * 128, (index // 2) * 128 + 128)
            heads_ref[:, cut] = jnp.where(low_lane, pair, mixed).astype(BF)
    logsum_ref[...] = logsum
    live = (sublanes((rows, 1)) < length).astype(F32)
    part[...] = (dot(heads_ref[...], wo_ref[...]) * live).astype(BF).reshape(part.shape)

    attn = Reduce(
        net, lambda re, rt: part.at[flip(me_t, rt)], lambda i: landing.at[i], tensor_bits,
        [(0, r) for r in range(tensor_count)],
    )
    attn.start()
    table = table_of(dealt_length, routes_ref, order_ref)
    source = jnp.broadcast_to(source.astype(F32), (TABLE_ROWS - EXPERTS, rows))
    tables_ref[me_e, me_d] = jnp.concatenate([table, source], axis=0).astype(BF)
    mine = tables_ref.at[me_e, me_d]
    table_copies = [net.send(mine, mine, "dp", m) for m in range(1, dp_count)]
    attn.finish()
    while attn.steps:
        attn.start()
        if not attn.steps:
            dy_half.finish()
            while dy_half.steps:
                dy_half.start()
                dy_half.finish()
            for re, _ in dy_half.known[1:]:
                place = dy_half.at(re, 0)
                dy_half.flight.append(net.send(place, place, "tensor", 1))
        attn.finish()

    start = pl.multiple_of(me_t * share, share)
    hidden = x_ref[pl.ds(start, share), :].astype(F32) + part[me_t].astype(F32)
    hidden_ref[...] = hidden
    scale2 = lax.rsqrt(jnp.mean(hidden * hidden, axis=-1, keepdims=True) + EPS)
    share_ref[...] = (hidden * scale2 * gain2_ref[...].astype(F32)[None, :]).astype(BF)
    keep_x = pltpu.make_async_copy(share_ref, xown_ref.at[me_e, pl.ds(start, share)], local_sem.at[1])
    keep_x.start()
    high_bits = tensor_bits[1:][::-1]
    gathers = []
    for part_index, steps in enumerate((high_bits + expert_bits, expert_bits + high_bits)):
        size = share // 2

        def at(re, rt, offset=part_index * size):
            begin = pl.multiple_of(flip(me_t, rt) * share + offset, size)
            return xown_ref.at[flip(me_e, re), pl.ds(begin, size)]

        gathers.append(
            Gather(net, at, steps + tensor_bits[:1], first=share_ref.at[pl.ds(part_index * size, size)])
        )
    table_all = Gather(net, lambda re, rt: tables_ref.at[flip(me_e, re)], expert_bits)
    first_step = True
    while gathers[0].steps:
        for gather in gathers:
            gather.start()
        if first_step:
            for copy in table_copies:
                copy.wait_recv()
            first_step = False
        else:
            table_all.finish()
        if table_all.steps:
            table_all.start()
        for gather in gathers:
            gather.finish()
    table_all.finish()
    dy_half.finish()
    net.close()
    keep_dy.wait()
    keep_x.wait()


def front(lengths, order_of, x, gain, wq, wk, wv, wo, cosine, sine, gain2, routes, order, dy):
    rows, width = x.shape
    sizes = tuple(lax.axis_size(axis) for axis in ("expert", "tensor", "dp"))
    expert_count, tensor_count, dp_count = sizes
    share = rows // tensor_count
    shape = jax.ShapeDtypeStruct
    copies = 96
    return pl.pallas_call(
        functools.partial(front_kernel, sizes),
        out_shape=(
            shape((rows, width), BF), shape((rows, wq.shape[1]), BF), shape((rows, wk.shape[1]), BF),
            shape((rows, wv.shape[1]), BF), shape((rows, wq.shape[1]), BF), shape((rows, 128), F32),
            shape((share, width), F32), shape((share, width), BF), shape((expert_count, dp_count, TABLE_ROWS, rows), BF),
            shape((expert_count, rows, width), BF), shape((expert_count, rows, width), BF),
        ),
        in_specs=[pl.BlockSpec(memory_space=pltpu.SMEM)] * 2 + vmem(11) + [pl.BlockSpec(memory_space=pl.ANY)],
        out_specs=tuple(vmem(9)) + (pl.BlockSpec(memory_space=pl.ANY),) * 2,
        scratch_shapes=[
            pltpu.VMEM((tensor_count, share, width), BF),
            pltpu.VMEM((tensor_count - 1, share, width), BF),
            pltpu.SemaphoreType.DMA((copies,)),
            pltpu.SemaphoreType.DMA((copies,)),
            pltpu.SemaphoreType.DMA((2,)),
        ],
        compiler_params=params(56, collective_id=1, has_side_effects=True),
        cost_estimate=pl.CostEstimate(flops=2 * rows * width * 4096, bytes_accessed=16 * MIB, transcendentals=0),
        name="front",
    )(lengths, order_of, x, gain, wq, wk, wv, wo, cosine, sine, gain2, routes, order, dy)


def back_kernel(
    sizes, wait_count,
    lengths_ref, dy_ref, x_ref, gain_ref, gain2_ref, router_ref, hidden_ref, tables_ref,
    normed_ref, q_ref, k_ref, v_ref, heads_ref, logsum_ref, wq_ref, wk_ref, wv_ref, wo_ref, cos_ref, sin_ref,
    grad_in_ref, out_in_ref, xown_ref, *rest,
):
    (
        block_ref, input_ref, q_grad_ref, k_grad_ref, v_grad_ref, out_grad_ref, small_ref,
        grad, grad_landing, out, out_landing, normed2, spread, first_part, first_landing, tiny, tiny_landing, back_ref, picked,
        send_sem, recv_sem, local_sem,
    ) = rest[wait_count:]
    group_count, tensor_count, dp_count = sizes
    rows, width = x_ref.shape
    share = rows // tensor_count
    net = Net(send_sem, recv_sem)
    me_e, me_t, me_d = net.me["expert"], net.me["tensor"], net.me["dp"]
    here = me_e if group_count > 1 else 0
    expert_bits = [("expert", b) for b in bits_of(group_count)]
    tensor_bits = [("tensor", b) for b in bits_of(tensor_count)]
    load_grad = pltpu.make_async_copy(grad_in_ref, grad, local_sem.at[0])
    load_out = pltpu.make_async_copy(out_in_ref, out, local_sem.at[1])
    load_x = pltpu.make_async_copy(xown_ref.at[here], normed2, local_sem.at[2])
    load_grad.start()
    load_out.start()
    load_x.start()
    net.barrier(expert_bits + tensor_bits + [("tensor", m) for m in range(3, tensor_count)])
    load_grad.wait()
    load_out.wait()
    high_bits = tensor_bits[1:]
    chunks = [(e, t) for e in range(group_count) for t in range(tensor_count)]
    sums = []
    size = share // 2
    for part_index, steps in enumerate((high_bits + expert_bits, expert_bits + high_bits)):

        def at(re, rt, offset=part_index * size):
            begin = pl.multiple_of(flip(me_t, rt) * share + offset, size)
            return grad.at[flip(here, re) if re else here, pl.ds(begin, size)]

        sums.append(Reduce(
            net, at, lambda i, p=part_index: grad_landing.at[p, i], tensor_bits[:1] + steps, chunks
        ))
    out_sum = Reduce(
        net, lambda re, rt: out.at[flip(here, re) if re else here, flip(me_t, rt)], lambda i: out_landing.at[i],
        tensor_bits[:1] + high_bits + expert_bits, chunks,
    )

    def advance(reduction):
        if reduction.flight:
            reduction.finish()
        if reduction.steps:
            reduction.start()

    step = 0
    while sums[0].steps:
        for one in sums:
            one.start()
        if step == 1:
            out_sum.start()
        step += 1
        for one in sums:
            one.finish()

    start = pl.multiple_of(me_t * share, share)
    gain2 = gain2_ref[...].astype(F32)[None, :]
    hidden = hidden_ref[...]
    scale2 = lax.rsqrt(jnp.mean(hidden * hidden, axis=-1, keepdims=True) + EPS)
    hat2 = hidden * scale2
    second_normed = (hat2 * gain2).astype(BF)
    picked[...] = given_table(tables_ref, me_e, me_d.astype(F32))
    table = picked[:, pl.ds(start, share)]
    table = jnp.concatenate([table, jnp.zeros((128 - EXPERTS, share), F32)], axis=0)
    table = jnp.transpose(table)[:, :EXPERTS]
    logits = dot(second_normed, router_ref[...], 1, 1)
    chosen = table > 0.5
    masked = jnp.where(chosen, logits, NEG)
    weights = jnp.where(chosen, jnp.exp(masked - jnp.max(masked, axis=-1, keepdims=True)), 0.0)
    total = jnp.sum(weights, axis=-1, keepdims=True)
    gates = weights / jnp.where(total > 0.0, total, 1.0)
    gate_in = grad[here, pl.ds(start, share), width:].astype(F32)[:, :EXPERTS]
    logit_grad = (gates * (gate_in - jnp.sum(gates * gate_in, axis=-1, keepdims=True))).astype(BF)
    normed_grad = grad[here, pl.ds(start, share), :width].astype(F32) + dot(logit_grad, router_ref[...])
    along2 = normed_grad * hat2
    gain2_part = jnp.sum(along2, axis=0, keepdims=True)
    scaled = normed_grad * gain2
    hidden_grad = dy_ref[pl.ds(start, share), :].astype(F32) + scale2 * (
        scaled - hat2 * jnp.mean(scaled * hat2, axis=-1, keepdims=True)
    )
    spread[me_t, 0:share, :width] = hidden_grad.astype(BF)
    spread[me_t, 0:share, width:] = jnp.concatenate(
        [logit_grad.astype(F32), jnp.zeros((share, 128 - EXPERTS), F32)], axis=1
    ).astype(BF)
    high = gain2_part.astype(BF).astype(F32)
    spread[me_t, share : share + 16, :width] = jnp.concatenate(
        [high, gain2_part - high, jnp.zeros((14, width), F32)], axis=0
    ).astype(BF)
    spread[me_t, share : share + 16, width:] = jnp.zeros((16, 128), BF)
    gather = Gather(net, lambda re, rt: spread.at[flip(me_t, rt)], high_bits[::-1] + tensor_bits[:1])
    while gather.steps:
        gather.start()
        advance(out_sum)
        gather.finish()

    length = lengths_ref[0, me_d]
    inv = HEAD_DIM**-0.5
    live = (sublanes((rows, 1)) < length).astype(F32)
    hidden_grad_all = spread[:, 0:share, :width].reshape(rows, width)
    branch = (hidden_grad_all.astype(F32) * live).astype(BF)
    heads_grad = dot(branch, wo_ref[...], 1, 1).astype(BF)
    cosine, sine = cos_ref[...], -sin_ref[...]
    lane = lanes((rows, 128))
    low_half = lane % HEAD_DIM < HEAD_DIM // 2
    low_lane = lane < HEAD_DIM
    q, k, v = q_ref[...], k_ref[...], v_ref[...]
    k_b, v_b = swap(k), swap(v)
    key, query = sublanes((rows, rows)), lanes((rows, rows))
    allowed = (key <= query) & (key < length)
    logsum_rows = jnp.transpose(logsum_ref[...])
    dk = [jnp.zeros((rows, 128), F32), jnp.zeros((rows, 128), F32)]
    dv = [jnp.zeros((rows, 128), F32), jnp.zeros((rows, 128), F32)]
    q_width = q.shape[1]
    pair = None
    for index in range(q_width // HEAD_DIM):
        same = index % 2 == (index // 2) % 2
        q_one, k_one = head_parts(q, k, k_b, index, low_lane)
        g_one, v_one = head_parts(heads_grad, v, v_b, index, low_lane)
        scores = jnp.where(allowed, dot(k_one, q_one, 1, 1) * inv, NEG)
        prob = jnp.exp(scores - logsum_rows[index : index + 1, :])
        grad_prob = dot(v_one, g_one, 1, 1)
        center = jnp.sum(prob * grad_prob, axis=0, keepdims=True)
        score_grad = (prob * (grad_prob - center)).astype(BF)
        dq = dot(score_grad, k_one, 0, 0) * inv
        place = 0 if same else 1
        dk[place] = dk[place] + dot(score_grad, q_one) * inv
        dv[place] = dv[place] + dot(prob.astype(BF), g_one)
        if index % 2 == 0:
            pair = dq
        else:
            cut = slice((index // 2) * 128, (index // 2) * 128 + 128)
            both = jnp.where(low_lane, pair, dq)
            back_ref[:, cut] = rotate128(both, cosine, sine, low_half).astype(BF)
            advance(out_sum)
    k_width = k.shape[1]
    k_total = dk[0] + pltpu.roll(dk[1], HEAD_DIM, 1)
    v_total = dv[0] + pltpu.roll(dv[1], HEAD_DIM, 1)
    back_ref[:, q_width : q_width + k_width] = rotate128(k_total, cosine, sine, low_half).astype(BF)
    back_ref[:, q_width + k_width :] = v_total.astype(BF)
    back = back_ref[...]
    first = (
        dot(back[:, :q_width], wq_ref[...], 1, 1)
        + dot(back[:, q_width : q_width + k_width], wk_ref[...], 1, 1)
        + dot(back[:, q_width + k_width :], wv_ref[...], 1, 1)
    )
    columns = width // tensor_count
    for t in range(tensor_count):
        first_part[t] = first[:, t * columns : (t + 1) * columns].astype(BF)
    first_sum = Reduce(
        net, lambda re, rt: first_part.at[flip(me_t, rt)], lambda i: first_landing.at[i], tensor_bits,
        [(0, r) for r in range(tensor_count)],
    )
    first_sum.start()
    x = x_ref[...].astype(F32)
    scale = lax.rsqrt(jnp.mean(x * x, axis=-1, keepdims=True) + EPS)
    along = first * (x * scale)
    stat = jnp.sum(along * gain_ref[...].astype(F32)[None, :], axis=-1, keepdims=True)
    stat_row = jnp.transpose(jnp.broadcast_to(stat, (rows, 128)))[0:8, :]
    tiny[:, :width] = jnp.broadcast_to(jnp.sum(along, axis=0, keepdims=True), (8, width))
    tiny[:, width:] = stat_row
    tiny_copies = [net.send(tiny, tiny_landing.at[m - 1], "tensor", m) for m in range(1, tensor_count)]
    first_sum.finish()
    while first_sum.steps:
        first_sum.start()
        grads = dot(normed_ref[...], back, 0, 0)
        q_grad_ref[...] = grads[:, :q_width].astype(BF)
        k_grad_ref[...] = grads[:, q_width : q_width + k_width].astype(BF)
        v_grad_ref[...] = grads[:, q_width + k_width :].astype(BF)
        out_grad_ref[...] = dot(heads_ref[...], branch, 0, 0).astype(BF)
        load_x.wait()
        router_rows = dot(spread[:, 0:share, width:].reshape(rows, 128), normed2[...], 0, 0)
        small_ref[0:EXPERTS, :] = router_rows[0:EXPERTS].astype(BF)
        first_sum.finish()
    for copy in tiny_copies:
        copy.wait_recv()
    tiny_all = tiny[...]
    for m in range(1, tensor_count):
        tiny_all = tiny_all + tiny_landing[m - 1]
    gain2_sum = jnp.zeros((1, width), F32)
    for t in range(tensor_count):
        block = spread[t, share : share + 16, :width].astype(F32)
        gain2_sum = gain2_sum + block[0:1] + block[1:2]
    small_ref[EXPERTS:, :] = jnp.concatenate(
        [tiny_all[0:1, :width], gain2_sum, jnp.zeros((14, width), F32)], axis=0
    ).astype(BF)
    stat_all = jnp.transpose(
        jnp.concatenate([tiny_all[:, width:], jnp.zeros((120, rows), F32)], axis=0)
    )[:, 0:1] / width
    begin = pl.multiple_of(me_t * columns, columns)
    cut = pl.ds(begin, columns)
    old = jnp.concatenate([spread[t, 0:share, cut] for t in range(tensor_count)], axis=0).astype(F32)
    input_ref[...] = (
        old + scale * (
            first_part[me_t].astype(F32) * gain_ref[cut].astype(F32)[None, :] - x_ref[:, cut].astype(F32) * scale * stat_all
        )
    ).astype(BF)
    while out_sum.flight or out_sum.steps:
        advance(out_sum)
    block_ref[...] = out[here, me_t]
    net.close()


def back_call(group_count, lengths, vmem_operands, grad, out, xown, waits):
    dy, x = vmem_operands[0], vmem_operands[1]
    rows, width = x.shape
    wq, wk, wv, wo = vmem_operands[13:17]
    tensor_count, dp_count = lax.axis_size("tensor"), lax.axis_size("dp")
    share, columns = rows // tensor_count, width // tensor_count
    chunks = group_count * tensor_count
    shape = jax.ShapeDtypeStruct
    copies = 96
    return pl.pallas_call(
        functools.partial(back_kernel, (group_count, tensor_count, dp_count), len(waits)),
        out_shape=(
            shape((rows, columns), BF), shape((rows, columns), BF),
            shape(wq.shape, BF), shape(wk.shape, BF), shape(wv.shape, BF), shape(wo.shape, BF),
            shape((TABLE_ROWS, width), BF),
        ),
        in_specs=[pl.BlockSpec(memory_space=pltpu.SMEM)] + vmem(len(vmem_operands)) + [pl.BlockSpec(memory_space=pl.ANY)] * (3 + len(waits)),
        out_specs=tuple(vmem(7)),
        scratch_shapes=[
            pltpu.VMEM(grad.shape, BF),
            pltpu.VMEM((2, chunks - 1, share // 2, width + 128), BF),
            pltpu.VMEM(out.shape, BF),
            pltpu.VMEM((chunks - 1, rows, columns), BF),
            pltpu.VMEM((rows, width), BF),
            pltpu.VMEM((tensor_count, share + 16, width + 128), BF),
            pltpu.VMEM((tensor_count, rows, columns), BF),
            pltpu.VMEM((tensor_count - 1, rows, columns), BF),
            pltpu.VMEM((8, width + rows), F32),
            pltpu.VMEM((tensor_count - 1, 8, width + rows), F32),
            pltpu.VMEM((rows, wq.shape[1] + wk.shape[1] + wv.shape[1]), BF),
            pltpu.VMEM((EXPERTS, rows), F32),
            pltpu.SemaphoreType.DMA((copies,)),
            pltpu.SemaphoreType.DMA((copies,)),
            pltpu.SemaphoreType.DMA((3,)),
        ],
        compiler_params=params(60, collective_id=2, has_side_effects=True),
        cost_estimate=pl.CostEstimate(flops=2 * rows * width * 8192, bytes_accessed=16 * MIB, transcendentals=0),
        name="back",
    )(lengths, *vmem_operands, grad, out, xown, *waits)


def gate_rows(router_t, rows, table):
    logits = dot(router_t, rows, 1, 1)
    chosen = table > 0.5
    masked = jnp.where(chosen, logits, NEG)
    weights = jnp.where(chosen, jnp.exp(masked - jnp.max(masked, axis=0, keepdims=True)), 0.0)
    total = jnp.sum(weights, axis=0, keepdims=True)
    return weights / jnp.where(total > 0.0, total, 1.0)


def expert_kernel(own, groups, dp_count, capacity, local, distance, x_ref, dy_ref, table_ref, router_ref, wg_ref, wu_ref, wd_ref, *rest):
    if own:
        hidden_ref, *rest = rest
        out_c_ref, out_g_ref, gg_ref, gu_ref, gd_ref, gates, ranks, xs, ys, gs, mats, gi_rows, acc_c, acc_g = rest[-14:]
    else:
        gin_g_ref, gin_u_ref, gin_d_ref, gg_ref, gu_ref, gd_ref, gates, ranks, xs, ys, gs = rest
    chunk, pair = pl.program_id(0), pl.program_id(1)
    dp_here, me_t, me_e = lax.axis_index("dp"), lax.axis_index("tensor"), lax.axis_index("expert")
    first_expert = me_e * local + pair * 2
    rows, width = x_ref.shape[-2:]
    single = own or distance > 0
    per_group = 1 if single else dp_count - 1
    units = groups * per_group

    def unit_place(i):
        if single:
            return (i,), i, lax.rem(dp_here + distance, dp_count)
        d = dp_here + 1 + i % per_group
        d = jnp.where(d >= dp_count, d - dp_count, d)
        return (i // per_group, d), i // per_group, d

    @pl.when(pair == 0)
    def _():
        @pl.loop(0, units)
        def _(i):
            at, group, d = unit_place(i)
            table = given_table(table_ref, group, d.astype(F32))
            ranks[i] = table
            gates[i] = gate_rows(router_ref[...], x_ref[at], table)

    slot_id = sublanes((capacity, rows))

    @pl.loop(0, units)
    def _(i):
        at, _, _ = unit_place(i)
        pieces = []
        for j in range(2):
            rank = ranks[i, pl.ds(first_expert + j, 1), :].astype(jnp.int32) - 1
            gate = gates[i, pl.ds(first_expert + j, 1), :]
            hit = slot_id == rank
            gs[j, i] = jnp.broadcast_to(
                jnp.sum(jnp.where(hit, gate, 0.0), axis=-1, keepdims=True), (capacity, 128)
            )
            pieces.append(jnp.where(hit, 1.0, 0.0).astype(BF))
        onehot = jnp.concatenate(pieces, axis=0)
        if own:
            mats[i] = onehot
        moved_x = dot(onehot, x_ref[at]).astype(BF)
        moved_y = dot(onehot, dy_ref[at]).astype(BF)
        for j in range(2):
            cut = slice(j * capacity, (j + 1) * capacity)
            xs[j, i] = moved_x[cut]
            ys[j, i] = moved_y[cut]

    hidden = wg_ref.shape[2]
    if own:

        @pl.when(pair == 0)
        def _():
            gi_rows[...] = jnp.zeros_like(gi_rows)

    terms_c, terms_g = [], []
    for j in range(2):
        x_here = xs[j].reshape(units * capacity, width)
        y_here = ys[j].reshape(units * capacity, width)
        scale = gs[j].reshape(units * capacity, 128)
        both = dot(x_here, jnp.concatenate([wg_ref[j], wu_ref[j]], axis=1))
        g_here, u_here = both[:, :hidden], both[:, hidden:]
        act_back = dot(y_here, wd_ref[j], 1, 1)
        sig = 1.0 / (1.0 + jnp.exp(-g_here))
        silu = g_here * sig
        act = silu * u_here
        act_gated = (act * scale).astype(BF)
        grad_act = act_back * scale
        grad_gate = (grad_act * u_here * sig * (1.0 + g_here * (1.0 - sig))).astype(BF)
        grad_up = (grad_act * silu).astype(BF)
        grads = jnp.concatenate([grad_gate, grad_up], axis=1)
        weight_grads = dot(x_here, grads, 0, 0)
        down = dot(act_gated, y_here, 0, 0)
        if own:
            gg_ref[j] = weight_grads[:, :hidden]
            gu_ref[j] = weight_grads[:, hidden:]
            gd_ref[j] = down
            inner = jnp.sum(act * act_back, axis=-1, keepdims=True)
            stacked = jnp.concatenate([act_gated, grads], axis=1)
            for i in range(units):
                cut = slice(i * capacity, (i + 1) * capacity)
                back = mats[i, j * capacity : (j + 1) * capacity, :]
                mats_t = dot(back, stacked[cut], 0, 0).astype(BF)
                terms_c.append(mats_t[:, :hidden])
                terms_g.append(mats_t[:, hidden:])
                gi_rows[i, pl.ds(first_expert + j, 1), :] = jnp.sum(back.astype(F32) * inner[cut], axis=0, keepdims=True)
        else:
            gg_ref[j] = gin_g_ref[j] + weight_grads[:, :hidden]
            gu_ref[j] = gin_u_ref[j] + weight_grads[:, hidden:]
            gd_ref[j] = gin_d_ref[j] + down
    if own:
        down_pair = wd_ref[...].reshape(2 * hidden, width)
        in_pair = jnp.concatenate([wg_ref[0], wu_ref[0], wg_ref[1], wu_ref[1]], axis=1)
        blocks, columns = out_c_ref.shape[1], out_c_ref.shape[3]
        share = hidden_ref.shape[0]
        for i in range(units):
            left_c = jnp.concatenate([terms_c[i], terms_c[units + i]], axis=1)
            left_g = jnp.concatenate([terms_g[i], terms_g[units + i]], axis=1)
            add_c = dot(left_c, down_pair)
            add_g = dot(left_g, in_pair, 1, 1)

            @pl.when(pair == 0)
            def _():
                acc_c[i] = add_c
                acc_g[i] = add_g

            @pl.when(pair != 0)
            def _():
                acc_c[i] += add_c
                acc_g[i] += add_g

        @pl.when(pair == pl.num_programs(1) - 1)
        def _():
            for i in range(units):

                @pl.when(chunk * groups + i == me_e)
                def _():
                    cut = pl.ds(pl.multiple_of(me_t * share, share), share)
                    acc_c[i, cut, :] += hidden_ref[...]

                for t in range(blocks):
                    out_c_ref[i, t] = acc_c[i, :, t * columns : (t + 1) * columns].astype(BF)
                out_g_ref[i, :, :width] = acc_g[i].astype(BF)
                out_g_ref[i, :, width:] = jnp.transpose(gi_rows[i]).astype(BF)


def expert_call(own, x, dy, table, router_t, wg, wu, wd, more, distance=0):
    groups_all, dp_count = table.shape[:2]
    rows, width = x.shape[-2:]
    chunk_groups = 2
    chunks = groups_all // chunk_groups
    local, _, hidden = wg.shape
    pairs = local // 2
    assert chunks == 1 or pairs == 1
    capacity = rows * TOP // EXPERTS
    shape = jax.ShapeDtypeStruct
    units = chunk_groups * (1 if own or distance else dp_count - 1)
    row_shape = (chunk_groups, *x.shape[1:])
    row_block = pl.BlockSpec(
        row_shape, lambda c, p: (c,) + (0,) * (len(row_shape) - 1), pipeline_mode=pl.Buffered(1)
    )
    in_block = pl.BlockSpec((2, width, hidden), lambda c, p: (p, 0, 0))
    down_block = pl.BlockSpec((2, hidden, width), lambda c, p: (p, 0, 0))
    in_specs = [
        row_block, row_block,
        pl.BlockSpec((chunk_groups, dp_count, TABLE_ROWS, rows), lambda c, p: (c, 0, 0, 0)),
        pl.BlockSpec((EXPERTS, width), lambda c, p: (0, 0)),
        in_block, in_block, down_block,
    ]
    grads_out = (shape(wg.shape, F32), shape(wu.shape, F32), shape(wd.shape, F32))
    grad_specs = (in_block, in_block, down_block)
    scratch = [
        pltpu.VMEM((units, EXPERTS, rows), F32),
        pltpu.VMEM((units, EXPERTS, rows), F32),
        pltpu.VMEM((2, units, capacity, width), BF),
        pltpu.VMEM((2, units, capacity, width), BF),
        pltpu.VMEM((2, units, capacity, 128), F32),
    ]
    operands = [x, dy, table, router_t, wg, wu, wd]
    if own:
        hidden_share, *waits = more
        blocks = lax.axis_size("tensor")
        columns = width // blocks
        in_specs.append(pl.BlockSpec(hidden_share.shape, lambda c, p: (0, 0)))
        operands.append(hidden_share)
        in_specs += [pl.BlockSpec(memory_space=pl.ANY)] * len(waits)
        operands += waits
        out_shape = (
            shape((groups_all, blocks, rows, columns), BF), shape((groups_all, rows, width + 128), BF), *grads_out,
        )
        out_specs = (
            pl.BlockSpec((chunk_groups, blocks, rows, columns), lambda c, p: (c, 0, 0, 0)),
            pl.BlockSpec((chunk_groups, rows, width + 128), lambda c, p: (c, 0, 0)),
            *grad_specs,
        )
        scratch += [pltpu.VMEM((units, 2 * capacity, rows), BF), pltpu.VMEM((units, 128, rows), F32)]
        scratch += [pltpu.VMEM((units, rows, width), F32)] * 2
        aliases = {}
    else:
        out_shape, out_specs = grads_out, grad_specs
        in_specs += list(grad_specs)
        operands += list(more)
        aliases = {7: 0, 8: 1, 9: 2}
    flops = 2 * chunks * pairs * 2 * units * capacity * width * hidden * (28 if own else 14)
    return pl.pallas_call(
        functools.partial(expert_kernel, own, chunk_groups, dp_count, capacity, local, distance),
        out_shape=out_shape,
        grid=(chunks, pairs),
        in_specs=in_specs,
        out_specs=out_specs,
        scratch_shapes=scratch,
        input_output_aliases=aliases,
        compiler_params=params(60, dimension_semantics=("arbitrary", "arbitrary")),
        cost_estimate=pl.CostEstimate(flops=2 * flops, bytes_accessed=60 * MIB, transcendentals=0),
        name="experts_own" if own else "experts_other",
    )(*operands)


def on_device(
    tokens, cotangent, seq_lengths, deal_order, routes, slot_order, first_gain, w_query, w_key, w_value, w_out,
    second_gain, w_router, w_gate, w_up, w_down,
):
    dp_count = lax.axis_size("dp")
    dp_index = lax.axis_index("dp")
    tensor_count = lax.axis_size("tensor")
    tensor_index = lax.axis_index("tensor")
    expert_count = lax.axis_size("expert")
    expert_index = lax.axis_index("expert")
    rows, width = tokens.shape
    share = rows // tensor_count
    everywhere = ("expert", "dp", "tensor")
    unit_shape = (expert_count, dp_count, rows, width)

    cosine, sine = (jnp.asarray(values) for values in rotary_tables(rows))
    gain1, gain2 = first_gain, second_gain
    router_t = w_router.T
    normed, q, k, v, heads, logsum, hidden, normed_share, tables, x_own, dy_own = front(
        seq_lengths, deal_order, tokens, gain1, w_query, w_key, w_value, w_out, cosine, sine, gain2, routes.T, slot_order, cotangent
    )
    dy_share = lax.dynamic_slice_in_dim(cotangent, tensor_index * share, share, 0)
    never = seq_lengths[0, 0] < 0

    def after(values, other):
        return jnp.where(never, other.astype(values.dtype), values)

    def gathered(values):
        return lax.all_gather(values, everywhere, axis=0, tiled=True).reshape(unit_shape)

    small_mesh = expert_count == 2
    extra = ()
    if small_mesh:
        dy_all = gathered(dy_share)
        x_all = gathered(normed_share)
    out_c, out_g, pg, pu, pd = expert_call(
        True, x_own, dy_own, tables, router_t, w_gate, w_up, w_down, (hidden,) + ((dy_all,) if small_mesh else ())
    )
    group_count = expert_count
    if small_mesh:
        extra = (x_all,)
    else:
        out_c = lax.psum_scatter(out_c, "expert", scatter_dimension=0, tiled=True)
        out_g = lax.psum_scatter(out_g, "expert", scatter_dimension=0, tiled=True)
        x_own = lax.dynamic_slice_in_dim(x_own, expert_index, 1, 0)
        group_count = 1
    block_out, input_grad, q_term, k_term, v_term, out_term, small = back_call(
        group_count, seq_lengths,
        (cotangent, tokens, gain1, gain2, router_t, hidden, tables, normed, q, k, v, heads, logsum,
         w_query, w_key, w_value, w_out, cosine, sine),
        out_g, out_c, x_own, extra,
    )
    out_sum, q_sum, k_sum, v_sum, small_sum = lax.psum((out_term, q_term, k_term, v_term, small), ("expert", "dp"))
    grads = (pg, pu, pd)
    if small_mesh:
        grads = expert_call(False, x_all, dy_all, tables, router_t, w_gate, w_up, w_down, grads)
    else:
        for distance in range(1, dp_count):
            pairs = [(i, (i - distance) % dp_count) for i in range(dp_count)]
            moved = (
                lax.all_gather(
                    lax.ppermute(after(values, small[0, 0] + grads[2][0, 0, 0].astype(BF)), "dp", pairs),
                    ("expert", "tensor"), axis=0, tiled=True,
                ).reshape(expert_count, rows, width)
                for values in (normed_share, dy_share)
            )
            grads = expert_call(False, *moved, tables, router_t, w_gate, w_up, w_down, grads, distance)
    gate_grad, up_grad, down_grad = grads
    last = down_grad[0, 0, 0]
    out_sum, q_sum, k_sum, v_sum, small_sum = (
        after(values.astype(F32), last) for values in (out_sum, q_sum, k_sum, v_sum, small_sum)
    )
    return (
        block_out, input_grad, small_sum[EXPERTS], q_sum.astype(F32), k_sum.astype(F32), v_sum.astype(F32),
        out_sum.astype(F32), small_sum[EXPERTS + 1], small_sum[:EXPERTS].T, gate_grad, up_grad, down_grad,
    )


def solution(mesh):
    rows2 = P(("expert", "dp"), None)
    placed = (
        rows2, rows2, P("expert", None), P("expert", None), rows2, rows2, P(),
        P(None, "tensor"), P(None, "tensor"), P(None, "tensor"), P("tensor", None), P(), P(),
        P("expert", None, "tensor"), P("expert", None, "tensor"), P("expert", "tensor", None),
    )
    return jax.shard_map(
        on_device,
        mesh=mesh,
        in_specs=placed,
        out_specs=(
            P(("expert", "dp"), "tensor"), P(("expert", "dp"), "tensor"), P(),
            P(None, "tensor"), P(None, "tensor"), P(None, "tensor"), P("tensor", None), P(), P(),
            P("expert", None, "tensor"), P("expert", None, "tensor"), P("expert", "tensor", None),
        ),
        check_vma=False,
    )
```

time: 667 us -> 352 us (0.53)
  waiting for transfers between devices: 345 us -> 74.4 us
  blocking collectives: 94.7 us -> 0 us
  Pallas kernels: 159 us -> 248 us
  local copies, waits for them, and re-layouts: 20.2 us -> 5.56 us
  other arithmetic: 18.8 us -> 9.77 us
    reduce_scatter x5 -> x0, waiting for transfers between devices: 143 us -> none  [the longest x1 43.8 us: on_device(): lax.psum_scatter(acc_g.reshape(-1, width), both, scatter_dimension=0, til...]
    pallas_call x3 -> x2, Pallas kernels: 22.7 us -> 114 us  [the longest x1 64.9 us: back_call(): pl.pallas_call(functools.partial(back_kernel, (group_count, tensor_count,...]
    psum x2 -> x1, waiting for transfers between devices: 99.1 us -> 14 us  [on_device(): lax.psum((out_term, q_term, k_term, v_term, small), ('expert', 'dp'))]
    all_gather x2 -> x0, blocking collectives: 48.7 us -> none  [the longest x1 34.6 us: on_device(): lax.all_gather(my_table, rows_all, axis=0)]
    psum x2 -> x0, blocking collectives: 46 us -> none  [the longest x1 40.2 us: on_device(): lax.psum((gain1_term, second_term, router_term), everywhere)]
    all_gather x3 -> x2, waiting for transfers between devices: 94.9 us -> 60.4 us  [gathered(): lax.all_gather(values, everywhere, axis=0, tiled=True).reshape(unit_shape)]
    convert_element_type x9 -> x0, other arithmetic: 15.2 us -> none  [the longest x1 2.13 us: on_device(): out_sum.astype(F32)]
    unnamed x55 -> x8, local copies, waits for them, and re-layouts: 12 us -> 1.42 us
  transfers between devices with their start and end apart: 11 -> 3, of which waited for: 8 -> 3; matrix products, arithmetic and copies ran while one was open for 3% -> 0% of each run, Pallas kernels for 13% -> 52%
where the time goes in v2:
time: 352 us; the launch traced here: 351 us
  Pallas kernels  248 us (70%)
  waiting for transfers between devices  74.4 us (21%)
  between operations  13.9 us (4%)
  other arithmetic  9.77 us (3%)
  local copies, waits for them, and re-layouts  5.56 us (2%)
    pallas_call x2, Pallas kernels, expert_call(): pl.pallas_call(functools.partial(expert_kernel, own, chunk_groups, dp_cou...  134 us
    pallas_call x1, Pallas kernels, back_call(): pl.pallas_call(functools.partial(back_kernel, (group_count, tensor_count,...  64.9 us
    all_gather x2, waiting for transfers between devices, gathered(): lax.all_gather(values, everywhere, axis=0, tiled=True).reshape(unit_shape)  60.4 us
    pallas_call x1, Pallas kernels, front(): pl.pallas_call(functools.partial(front_kernel, sizes), out_shape=(shape((...  48.9 us
    psum x1, waiting for transfers between devices, on_device(): lax.psum((out_term, q_term, k_term, v_term, small), ('expert', 'dp'))  14 us
    select_n x4, other arithmetic, after(): return jnp.where(never, other.astype(values.dtype), values)  9.77 us
  transfers between devices with their start and end apart: 3, of which 3 were waited for; matrix products, arithmetic and copies ran while one was open for 0% of the time, Pallas kernels for 52%

profile of v2, /device:TPU:0, one launch (start us, length us, event | category | flops | bytes accessed | tf_op | source)
XLA Modules:
  0.0 351.3 jit_solution(14724615925194217069)
XLA Ops:
  7.2 0.0 all-gather.3.cloned.1.call-start
  7.2 0.0 copy-start.2
  7.2 1.7 constant_dynamic-slice_fusion
  8.9 0.0 all-gather.3.cloned.1.call-update
  8.9 0.0 all-gather.5.cloned.1.call-start
  9.0 48.9 %front.1 = (bf16[512,1024]{1,0:T(8,128)(2,1)}, bf16[512,256]{1,0:T(8,128)(2,1)}, bf16[512,128]{1,0:T(8,128)(2,1)}, bf16[512,128]{1,0:T(8,128)(2,1)}, bf16[512,25...) custom-call(s32[1,4]{1,0:T(1,128)} %lengths_ref.3, ...), custom_call_target="tpu_custom_call" | custom-call | flops 4294967296 | bytes 16777216 | tf_op jit(solution)/shard_map/front/pallas_call | solution.py:342
  57.9 0.0 all-gather.5.cloned.1.call-update
  57.9 0.0 all-reduce.3.cloned.1.call-start
  58.0 38.0 %all-gather.3.cloned.1.call-done = bf16[4096,1024]{1,0:T(8,128)(2,1)} async-done(((bf16[128,1024]{1,0:T(8,128)(2,1)}), bf16[4096,1024]{1,0:T(8,128)(2,1)}) %all-gather.3.cloned.1.call-update) | async-done | bytes 8388624 | tf_op jit(solution)/shard_map/all_gather | solution.py:856
  96.0 56.7 %experts_own.1 = (bf16[2,4,512,256]{3,2,1,0:T(8,128)(2,1)}, bf16[2,512,1152]{2,1,0:T(8,128)(2,1)}, f32[16,1024,128]{2,1,0:T(8,128)}, f32[16,1024,128]{2,1,0:T(8,128)}, f32[16,128,1024]{2,1,0:T(8,128)}) custom-call(bf16[2,512,1024]{2,1,0:T(8,128)(2,1)} %get-tuple-element.46.x_ref.xown_ref, bf16[2,512,1024]{2,1,0:T(8,128)(2,1)} %get-tuple-element.47.dy_ref, ...), custom_call_target="tpu_custom_call" | custom-call | flops 60129542144 | bytes 62914560 | tf_op jit(solution)/shard_map/experts_own/pallas_call | solution.py:814
  152.8 22.3 %all-gather.5.cloned.1.call-done = bf16[4096,1024]{1,0:T(8,128)(2,1)} async-done(((bf16[128,1024]{1,0:T(8,128)(2,1)}), bf16[4096,1024]{1,0:T(8,128)(2,1)}) %all-gather.5.cloned.1.call-update) | async-done | bytes 8388624 | tf_op jit(solution)/shard_map/all_gather | solution.py:856
  175.1 64.9 %back.1 = (bf16[512,256]{1,0:T(8,128)(2,1)}, bf16[512,256]{1,0:T(8,128)(2,1)}, bf16[1024,256]{1,0:T(8,128)(2,1)}, bf16[1024,128]{1,0:T(8,128)(2,1)}, bf16[1024,1...) custom-call(s32[1,4]{1,0:T(1,128)} %lengths_ref.3, bf16[512,1024]{1,0:T(8,128)(2,1)} %dy_ref.3, ...), custom_call_target="tpu_custom_call" | custom-call | flops 8589934592 | bytes 16777216 | tf_op jit(solution)/shard_map/back/pallas_call | solution.py:583
  240.0 0.0 all-reduce.3.cloned.1.call-update
  240.1 77.0 %experts_other.1 = (f32[16,1024,128]{2,1,0:T(8,128)}, f32[16,1024,128]{2,1,0:T(8,128)}, f32[16,128,1024]{2,1,0:T(8,128)}) custom-call(bf16[2,4,512,1024]{3,2,1,0:T(8,128)(2,1)} %bitcast.16, bf16[2,4,512,1024]{3,2,1,0:T(8,128)(2,1)} %bitcast.14, ...), custom_call_target="tpu_custom_call", output_to_operand_aliasing={{0}: (7, {}), {1}: (8, {}), {2}: (9, {})} | custom-call | flops 90194313216 | bytes 62914560 | tf_op jit(solution)/shard_map/experts_other/pallas_call | solution.py:814
  317.1 1.2 slice.16
  318.3 14.0 %all-reduce.3.cloned.1.call-done = (bf16[48,1024]{1,0:T(8,128)(2,1)}, bf16[1024,256]{1,0:T(8,128)(2,1)}, bf16[1024,128]{1,0:T(8,128)(2,1)}, bf16[1024,128]{1,0:T(8,128)(2,1)}, bf16[256,1024]{1,0:T(8,128)(2,1)}) async-done(((bf16[48,1024]{1,0:T(8,128)(2,1)}, bf16[1024,256]{1,0:T(8,128)(2,1)}, bf16[1024,128]{1,0:T(8,128)(2,1)}, bf16[1024,128]{1,0:T(8,128)(2,1)}, bf16[256,1024]{1,0:T(8,128)(2,1)}), ...) | async-done | bytes 1671184 | tf_op jit(solution)/shard_map/psum | solution.py:880
  332.3 1.6 convert_select_fusion.4
  333.8 0.6 fusion
  334.5 0.7 slice_bitcast_fusion
  335.1 2.7 convert_select_fusion.1
  337.8 2.8 convert_select_fusion
  340.6 2.7 convert_select_fusion.2
  343.3 0.7 copy.43
  344.0 0.7 copy.44
  (5 shorter events, 0.0 us)
Async XLA Ops:
  7.2 88.9 %all-gather.3.cloned.1.call-start = ((), (), s32[]{:S(2)}) async-start(), calls=%async_computation | async-start | bytes 8650752 | tf_op jit(solution)/shard_map/all_gather | solution.py:856
  7.2 50.8 %copy-start.2 = (s32[1,4]{1,0:T(1,128)S(1)}, s32[1,4]{1,0:T(1,128)}, u32[]{:S(2)}) copy-start(s32[1,4]{1,0:T(1,128)} %lengths_ref.3) | copy-start | bytes 52
  8.9 166.2 %all-gather.5.cloned.1.call-start = ((), (), s32[]{:S(2)}) async-start(), calls=%async_computation.1 | async-start | bytes 8650752 | tf_op jit(solution)/shard_map/all_gather | solution.py:856
  57.9 274.3 %all-reduce.3.cloned.1.call-start = ((), (), s32[]{:S(2)}) async-start(), calls=%async_computation.2 | async-start | bytes 3342336 | tf_op jit(solution)/shard_map/psum | solution.py:880
  240.0 103.3 %copy-start.1 = (bf16[512,256]{1,0:T(8,128)(2,1)S(1)}, bf16[512,256]{1,0:T(8,128)(2,1)}, u32[]{:S(2)}) copy-start(bf16[512,256]{1,0:T(8,128)(2,1)} %get-tuple-element.85) | copy-start | bytes 786436
  240.1 104.0 %copy-start = (bf16[512,256]{1,0:T(8,128)(2,1)S(1)}, bf16[512,256]{1,0:T(8,128)(2,1)}, u32[]{:S(2)}) copy-start(bf16[512,256]{1,0:T(8,128)(2,1)} %get-tuple-element.86) | copy-start | bytes 786436
Sparse Core Ops, SparseCore 0:
  11.5 84.5 all-gather.2
  98.9 76.1 all-gather.4
  240.2 92.0 all-reduce.2

commit v3 on v2

v3 whole, which is shorter than its diff:
```python
import functools

import jax
import jax.numpy as jnp
import numpy as np
from jax import lax
from jax.experimental import pallas as pl
from jax.experimental.pallas import tpu as pltpu
from jax.sharding import PartitionSpec as P

HEADS = 16
KV_HEADS = 8
HEAD_DIM = 64
EXPERTS = 32
TOP = 8
SLOT = 512

EPS = 1e-06
THETA = 10000.0
NEG = -1e30
BF = jnp.bfloat16
F32 = jnp.float32
MIB = 1 << 20


def dot(a, b, ca=1, cb=0):
    return lax.dot_general(a, b, (((ca,), (cb,)), ((), ())), preferred_element_type=F32)


def vmem(count=1):
    return [pl.BlockSpec(memory_space=pltpu.VMEM)] * count


def params(mib, **more):
    return pltpu.CompilerParams(vmem_limit_bytes=mib * MIB, **more)


def rotary_tables(rows):
    places = np.arange(rows, dtype=np.float32)[:, None]
    halfway = HEAD_DIM // 2
    spread = np.float32(THETA) ** (-2.0 * np.arange(halfway, dtype=np.float32) / HEAD_DIM)
    angles = (places * spread.astype(np.float32)[None, :]).astype(np.float32)
    copies = 128 // halfway
    return (
        np.tile(np.cos(angles), (1, copies)).astype(np.float32),
        np.tile(np.sin(angles), (1, copies)).astype(np.float32),
    )


def rotate128(values, cosine, sine, low_half):
    half = HEAD_DIM // 2
    up = pltpu.roll(values, 128 - half, 1)
    down = pltpu.roll(values, half, 1)
    return values * cosine + jnp.where(low_half, -up, down) * sine


def lanes(shape):
    return lax.broadcasted_iota(jnp.int32, shape, len(shape) - 1)


def sublanes(shape):
    return lax.broadcasted_iota(jnp.int32, shape, len(shape) - 2)


def bits_of(count):
    return [1 << i for i in range(count.bit_length() - 1)]


def flip(value, mask):
    for bit in bits_of(1 << 16):
        if mask & bit:
            value = value + bit - 2 * bit * lax.rem(lax.div(value, bit), 2)
    return value


class Net:
    def __init__(self, send_sem, recv_sem):
        self.send_sem, self.recv_sem, self.used, self.copies = send_sem, recv_sem, 0, []
        self.me = {axis: lax.axis_index(axis) for axis in ("expert", "tensor", "dp")}

    def barrier(self, partners):
        sem = pltpu.get_barrier_semaphore()
        for axis, mask in partners:
            pl.semaphore_signal(
                sem, inc=1, device_id={axis: flip(self.me[axis], mask)}, device_id_type=pl.DeviceIdType.MESH
            )
        pl.semaphore_wait(sem, len(partners))

    def send(self, source, target, axis, mask):
        k = self.used
        self.used += 1
        copy = Copy(self, k, source, target, axis, mask)
        copy.build().start()
        self.copies.append(copy)
        return copy

    def close(self):
        for copy in self.copies:
            copy.build().wait_send()


class Copy:
    def __init__(self, net, index, source, target, axis, mask):
        self.net, self.index, self.source, self.target, self.axis, self.mask = net, index, source, target, axis, mask

    def build(self):
        source = self.source() if callable(self.source) else self.source
        target = self.target() if callable(self.target) else self.target
        return pltpu.make_async_remote_copy(
            src_ref=source, dst_ref=target,
            send_sem=self.net.send_sem.at[self.index], recv_sem=self.net.recv_sem.at[self.index],
            device_id={self.axis: flip(self.net.me[self.axis], self.mask)}, device_id_type=pl.DeviceIdType.MESH,
        )

    def wait_recv(self):
        self.build().wait_recv()


class Gather:
    def __init__(self, net, at, steps, known=((0, 0),), first=None):
        self.net, self.at, self.steps, self.known, self.first, self.flight = net, at, list(steps), list(known), first, []

    def start(self):
        axis, mask = self.steps.pop(0)
        fresh = []
        for re, rt in self.known:
            place = functools.partial(self.at, re, rt)
            source = self.first if self.first is not None and (re, rt) == (0, 0) else place
            self.flight.append(self.net.send(source, place, axis, mask))
            fresh.append((re ^ mask, rt) if axis == "expert" else (re, rt ^ mask))
        self.known += fresh

    def finish(self):
        for copy in self.flight:
            copy.wait_recv()
        self.flight = []


class Reduce:
    def __init__(self, net, at, landing, steps, chunks):
        self.net, self.at, self.landing, self.steps, self.live = net, at, landing, list(steps), list(chunks)
        self.used, self.flight = 0, []

    def start(self):
        axis, mask = self.steps.pop(0)
        side = 0 if axis == "expert" else 1
        going = [r for r in self.live if r[side] & mask]
        self.live = [r for r in self.live if not r[side] & mask]
        for r in going:
            kept = (r[0] ^ mask, r[1]) if side == 0 else (r[0], r[1] ^ mask)
            copy = self.net.send(functools.partial(self.at, *r), functools.partial(self.landing, self.used), axis, mask)
            self.flight.append((kept, copy, self.used))
            self.used += 1
        if self.steps:
            axis, mask = self.steps[0]
            side = 0 if axis == "expert" else 1
            self.flight.sort(key=lambda item: 0 if item[0][side] & mask else 1)

    def finish(self):
        for kept, copy, slot in self.flight:
            copy.wait_recv()
            place = self.at(*kept)
            place[...] = (place[...].astype(F32) + self.landing(slot)[...].astype(F32)).astype(BF)
        self.flight = []


class AllReduce:
    def __init__(self, net, stages, landing, steps):
        self.net, self.stages, self.landing, self.steps, self.flight = net, stages, landing, list(steps), []

    def finish(self):
        k = len(self.flight)
        self.flight[-1].wait_recv()
        self.stages[k] = self.stages[k - 1] + self.landing[k - 1]

    def start(self):
        k = len(self.flight)
        axis, mask = self.steps[k]
        self.flight.append(self.net.send(lambda: self.stages.at[k], lambda: self.landing.at[k], axis, mask))

    def advance(self, k):
        if 1 <= k <= len(self.steps):
            self.finish()
        if k < len(self.steps):
            self.start()


TABLE_ROWS = 48
SMALL_ROWS = 128


def table_of(length, routes_ref, order_ref):
    rows = routes_ref.shape[1]
    capacity = rows * TOP // EXPERTS
    entries = rows * TOP
    chunk = 512
    routes_t = routes_ref[...].astype(F32).astype(BF)
    upper = (sublanes((chunk, chunk)) < lanes((chunk, chunk))).astype(F32).astype(BF)
    expert_row = sublanes((EXPERTS, chunk))

    def body(step, carried):
        counts, table = carried
        entry = order_ref[:, pl.ds(pl.multiple_of(step * chunk, chunk), chunk)]
        row, choice = entry // TOP, entry % TOP
        onehot_row = (sublanes((rows, chunk)) == row).astype(F32).astype(BF)
        picked = dot(routes_t, onehot_row)
        expert = jnp.sum(jnp.where(sublanes((TOP, chunk)) == choice, picked, 0.0), axis=0, keepdims=True)
        member = (expert_row.astype(F32) == expert) & (row < length)
        member_f = member.astype(F32)
        before = dot(member_f.astype(BF), upper) + counts
        value = jnp.where(member, jnp.minimum(before, float(capacity)) + 1.0, 0.0)
        table = table + dot(value.astype(BF), onehot_row, 1, 1)
        return counts + jnp.sum(member_f, axis=1, keepdims=True), table

    _, table = lax.fori_loop(
        0, entries // chunk, body, (jnp.zeros((EXPERTS, 1), F32), jnp.zeros((EXPERTS, rows), F32))
    )
    return table


def given_table(tables, index, dp_here):
    total = 0.0
    for j in range(tables.shape[1]):
        source = tables[index, j, EXPERTS : EXPERTS + 16, :].astype(F32)[0:1]
        total = total + jnp.where(source == dp_here, tables[index, j, 0:EXPERTS, :].astype(F32), 0.0)
    return total


def head_parts(q, k_a, k_b, index, low_lane):
    block = q[:, (index // 2) * 128 : (index // 2) * 128 + 128]
    mine = low_lane if index % 2 == 0 else jnp.logical_not(low_lane)
    return jnp.where(mine, block, jnp.zeros((), block.dtype)), (k_a if index % 2 == (index // 2) % 2 else k_b)


def swap(block):
    return pltpu.roll(block.astype(F32), HEAD_DIM, 1).astype(BF)


def front_kernel(
    sizes,
    lengths_ref, order_of_ref, x_ref, gain_ref, wq_ref, wk_ref, wv_ref, wo_ref, cos_ref, sin_ref, gain2_ref, routes_ref, order_ref, dy_ref,
    normed_ref, q_ref, k_ref, v_ref, heads_ref, logsum_ref, hidden_ref, share_ref, tables_ref, far_dy_ref, xown_ref, dyown_ref,
    part, landing, send_sem, recv_sem, local_sem,
):
    expert_count, tensor_count, dp_count = sizes
    rows, width = x_ref.shape
    share = rows // tensor_count
    half = rows // 2
    net = Net(send_sem, recv_sem)
    me_e, me_t, me_d = net.me["expert"], net.me["tensor"], net.me["dp"]
    expert_bits = [("expert", b) for b in bits_of(expert_count)]
    tensor_bits = [("tensor", b) for b in bits_of(tensor_count)]
    net.barrier(expert_bits + tensor_bits + [("dp", m) for m in range(1, dp_count)])

    keep_dy = pltpu.make_async_copy(dy_ref, dyown_ref.at[me_e], local_sem.at[0])
    keep_dy.start()
    half_start = pl.multiple_of(lax.rem(me_t, 2) * half, half)
    dy_half = Gather(
        net, lambda re, rt: dyown_ref.at[flip(me_e, re), pl.ds(half_start, half)], expert_bits,
        first=dy_ref.at[pl.ds(half_start, half)],
    )
    dy_half.start()
    mine_rows = pl.multiple_of(me_t * share, share)
    far_copies = [
        net.send(dy_ref.at[pl.ds(mine_rows, share)], far_dy_ref.at[m - 1], "dp", m) for m in range(1, dp_count)
    ]

    length, source, dealt_length = lengths_ref[0, me_d], order_of_ref[0, me_d], 0
    for i in range(dp_count):
        dealt_length = jnp.where(source == i, lengths_ref[0, i], dealt_length)
    x = x_ref[...].astype(F32)
    scale = lax.rsqrt(jnp.mean(x * x, axis=-1, keepdims=True) + EPS)
    normed = (x * scale * gain_ref[...].astype(F32)[None, :]).astype(BF)
    normed_ref[...] = normed
    cosine, sine = cos_ref[...], sin_ref[...]
    lane = lanes((rows, 128))
    low_half = lane % HEAD_DIM < HEAD_DIM // 2
    low_lane = lane < HEAD_DIM
    q_pre = dot(normed, wq_ref[...])
    for block in range(q_pre.shape[1] // 128):
        cut = slice(block * 128, block * 128 + 128)
        q_ref[:, cut] = rotate128(q_pre[:, cut], cosine, sine, low_half).astype(BF)
    k = rotate128(dot(normed, wk_ref[...]), cosine, sine, low_half).astype(BF)
    v = dot(normed, wv_ref[...]).astype(BF)
    k_ref[...] = k
    v_ref[...] = v
    q = q_ref[...]
    k_b, v_b = swap(k), swap(v)
    row, col = sublanes((rows, rows)), lanes((rows, rows))
    allowed = (col <= row) & (col < length)
    logsum = jnp.zeros((rows, 128), F32)
    pair = None
    for index in range(q.shape[1] // HEAD_DIM):
        q_one, k_one = head_parts(q, k, k_b, index, low_lane)
        v_one = v if index % 2 == (index // 2) % 2 else v_b
        scores = jnp.where(allowed, dot(q_one, k_one, 1, 1) * (HEAD_DIM**-0.5), NEG)
        highest = jnp.max(scores, axis=-1, keepdims=True)
        weights = jnp.exp(scores - highest)
        total = jnp.sum(weights, axis=-1, keepdims=True)
        mixed = dot((weights / total).astype(BF), v_one)
        logsum = jnp.where(lane == index, highest + jnp.log(total), logsum)
        if index % 2 == 0:
            pair = mixed
        else:
            cut = slice((index // 2) * 128, (index // 2) * 128 + 128)
            heads_ref[:, cut] = jnp.where(low_lane, pair, mixed).astype(BF)
    logsum_ref[...] = logsum
    live = (sublanes((rows, 1)) < length).astype(F32)
    part[...] = (dot(heads_ref[...], wo_ref[...]) * live).astype(BF).reshape(part.shape)

    attn = Reduce(
        net, lambda re, rt: part.at[flip(me_t, rt)], lambda i: landing.at[i], tensor_bits,
        [(0, r) for r in range(tensor_count)],
    )
    attn.start()
    table = table_of(dealt_length, routes_ref, order_ref)
    source = jnp.broadcast_to(source.astype(F32), (TABLE_ROWS - EXPERTS, rows))
    tables_ref[me_e, me_d] = jnp.concatenate([table, source], axis=0).astype(BF)
    mine = tables_ref.at[me_e, me_d]
    table_copies = [net.send(mine, mine, "dp", m) for m in range(1, dp_count)]
    attn.finish()
    while attn.steps:
        attn.start()
        if not attn.steps:
            dy_half.finish()
            while dy_half.steps:
                dy_half.start()
                dy_half.finish()
            for re, _ in dy_half.known[1:]:
                place = dy_half.at(re, 0)
                dy_half.flight.append(net.send(place, place, "tensor", 1))
        attn.finish()

    start = pl.multiple_of(me_t * share, share)
    hidden = x_ref[pl.ds(start, share), :].astype(F32) + part[me_t].astype(F32)
    hidden_ref[...] = hidden
    scale2 = lax.rsqrt(jnp.mean(hidden * hidden, axis=-1, keepdims=True) + EPS)
    share_ref[...] = (hidden * scale2 * gain2_ref[...].astype(F32)[None, :]).astype(BF)
    keep_x = pltpu.make_async_copy(share_ref, xown_ref.at[me_e, pl.ds(start, share)], local_sem.at[1])
    keep_x.start()
    high_bits = tensor_bits[1:][::-1]
    gathers = []
    for part_index, steps in enumerate((high_bits + expert_bits, expert_bits + high_bits)):
        size = share // 2

        def at(re, rt, offset=part_index * size):
            begin = pl.multiple_of(flip(me_t, rt) * share + offset, size)
            return xown_ref.at[flip(me_e, re), pl.ds(begin, size)]

        gathers.append(
            Gather(net, at, steps + tensor_bits[:1], first=share_ref.at[pl.ds(part_index * size, size)])
        )
    table_all = Gather(net, lambda re, rt: tables_ref.at[flip(me_e, re)], expert_bits)
    first_step = True
    while gathers[0].steps:
        for gather in gathers:
            gather.start()
        if first_step:
            for copy in table_copies:
                copy.wait_recv()
            first_step = False
        else:
            table_all.finish()
        if table_all.steps:
            table_all.start()
        for gather in gathers:
            gather.finish()
    table_all.finish()
    dy_half.finish()
    for copy in far_copies:
        copy.wait_recv()
    net.close()
    keep_dy.wait()
    keep_x.wait()


def front(lengths, order_of, x, gain, wq, wk, wv, wo, cosine, sine, gain2, routes, order, dy):
    rows, width = x.shape
    sizes = tuple(lax.axis_size(axis) for axis in ("expert", "tensor", "dp"))
    expert_count, tensor_count, dp_count = sizes
    share = rows // tensor_count
    shape = jax.ShapeDtypeStruct
    copies = 96
    return pl.pallas_call(
        functools.partial(front_kernel, sizes),
        out_shape=(
            shape((rows, width), BF), shape((rows, wq.shape[1]), BF), shape((rows, wk.shape[1]), BF),
            shape((rows, wv.shape[1]), BF), shape((rows, wq.shape[1]), BF), shape((rows, 128), F32),
            shape((share, width), F32), shape((share, width), BF), shape((expert_count, dp_count, TABLE_ROWS, rows), BF),
            shape((dp_count - 1, share, width), BF), shape((expert_count, rows, width), BF), shape((expert_count, rows, width), BF),
        ),
        in_specs=[pl.BlockSpec(memory_space=pltpu.SMEM)] * 2 + vmem(11) + [pl.BlockSpec(memory_space=pl.ANY)],
        out_specs=tuple(vmem(10)) + (pl.BlockSpec(memory_space=pl.ANY),) * 2,
        scratch_shapes=[
            pltpu.VMEM((tensor_count, share, width), BF),
            pltpu.VMEM((tensor_count - 1, share, width), BF),
            pltpu.SemaphoreType.DMA((copies,)),
            pltpu.SemaphoreType.DMA((copies,)),
            pltpu.SemaphoreType.DMA((2,)),
        ],
        compiler_params=params(56, collective_id=1, has_side_effects=True),
        cost_estimate=pl.CostEstimate(flops=MIB, bytes_accessed=MIB, transcendentals=0),
        name="front",
    )(lengths, order_of, x, gain, wq, wk, wv, wo, cosine, sine, gain2, routes, order, dy)


def back_kernel(
    sizes, passes,
    lengths_ref, dy_ref, x_ref, gain_ref, gain2_ref, router_ref, hidden_ref, tables_ref,
    normed_ref, q_ref, k_ref, v_ref, heads_ref, logsum_ref, wq_ref, wk_ref, wv_ref, wo_ref, cos_ref, sin_ref,
    grad_in_ref, xown_ref, *rest,
):
    if passes:
        rest = rest[1:]
        other_ref = rest[7]
        rest = rest[:7] + rest[8:]
    (
        first_ref, tiny_ref, hidden_grad_ref, scale_ref, dense_ref, out_grad_ref, small_ref,
        grad, grad_landing, normed2, spread, back_ref, picked, send_sem, recv_sem, local_sem,
    ) = rest
    group_count, tensor_count, dp_count = sizes
    rows, width = x_ref.shape
    share = rows // tensor_count
    net = Net(send_sem, recv_sem)
    me_e, me_t, me_d = net.me["expert"], net.me["tensor"], net.me["dp"]
    here = me_e if group_count > 1 else 0
    expert_bits = [("expert", b) for b in bits_of(group_count)]
    tensor_bits = [("tensor", b) for b in bits_of(tensor_count)]
    load_grad = pltpu.make_async_copy(grad_in_ref, grad, local_sem.at[0])
    load_x = pltpu.make_async_copy(xown_ref.at[here], normed2, local_sem.at[1])
    load_grad.start()
    load_x.start()
    net.barrier(expert_bits + tensor_bits)
    load_grad.wait()
    high_bits = tensor_bits[1:]
    chunks = [(e, t) for e in range(group_count) for t in range(tensor_count)]
    sums = []
    size = share // 2
    for part_index, steps in enumerate((high_bits + expert_bits, expert_bits + high_bits)):

        def at(re, rt, offset=part_index * size):
            begin = pl.multiple_of(flip(me_t, rt) * share + offset, size)
            return grad.at[flip(here, re) if re else here, pl.ds(begin, size)]

        sums.append(Reduce(
            net, at, lambda i, p=part_index: grad_landing.at[p, i], tensor_bits[:1] + steps, chunks
        ))
    while sums[0].steps:
        for one in sums:
            one.start()
        for one in sums:
            one.finish()

    start = pl.multiple_of(me_t * share, share)
    gain2 = gain2_ref[...].astype(F32)[None, :]
    hidden = hidden_ref[...]
    scale2 = lax.rsqrt(jnp.mean(hidden * hidden, axis=-1, keepdims=True) + EPS)
    hat2 = hidden * scale2
    second_normed = (hat2 * gain2).astype(BF)
    picked[...] = given_table(tables_ref, me_e, me_d.astype(F32))
    table = picked[:, pl.ds(start, share)]
    table = jnp.concatenate([table, jnp.zeros((128 - EXPERTS, share), F32)], axis=0)
    table = jnp.transpose(table)[:, :EXPERTS]
    logits = dot(second_normed, router_ref[...], 1, 1)
    chosen = table > 0.5
    masked = jnp.where(chosen, logits, NEG)
    weights = jnp.where(chosen, jnp.exp(masked - jnp.max(masked, axis=-1, keepdims=True)), 0.0)
    total = jnp.sum(weights, axis=-1, keepdims=True)
    gates = weights / jnp.where(total > 0.0, total, 1.0)
    gate_in = grad[here, pl.ds(start, share), width:].astype(F32)[:, :EXPERTS]
    logit_grad = (gate_in - gates * jnp.sum(gate_in, axis=-1, keepdims=True)).astype(BF)
    normed_grad = grad[here, pl.ds(start, share), :width].astype(F32) + dot(logit_grad, router_ref[...])
    along2 = normed_grad * hat2
    gain2_part = jnp.sum(along2, axis=0, keepdims=True)
    scaled = normed_grad * gain2
    hidden_grad = dy_ref[pl.ds(start, share), :].astype(F32) + scale2 * (
        scaled - hat2 * jnp.mean(scaled * hat2, axis=-1, keepdims=True)
    )
    spread[me_t, 0:share, :width] = hidden_grad.astype(BF)
    spread[me_t, 0:share, width:] = jnp.concatenate(
        [logit_grad.astype(F32), jnp.zeros((share, 128 - EXPERTS), F32)], axis=1
    ).astype(BF)
    high = gain2_part.astype(BF).astype(F32)
    spread[me_t, share : share + 16, :width] = jnp.concatenate(
        [high, gain2_part - high, jnp.zeros((14, width), F32)], axis=0
    ).astype(BF)
    spread[me_t, share : share + 16, width:] = jnp.zeros((16, 128), BF)
    gather = Gather(net, lambda re, rt: spread.at[flip(me_t, rt)], high_bits[::-1] + tensor_bits[:1])
    while gather.steps:
        gather.start()
        gather.finish()

    row_parts = plane_gathers(net, other_ref, share, done=True) if passes else []
    for one in row_parts:
        one.start()
    length = lengths_ref[0, me_d]
    inv = HEAD_DIM**-0.5
    live = (sublanes((rows, 1)) < length).astype(F32)
    hidden_grad_all = spread[:, 0:share, :width].reshape(rows, width)
    hidden_grad_ref[...] = hidden_grad_all
    branch = (hidden_grad_all.astype(F32) * live).astype(BF)
    heads_grad = dot(branch, wo_ref[...], 1, 1).astype(BF)
    cosine, sine = cos_ref[...], -sin_ref[...]
    lane = lanes((rows, 128))
    low_half = lane % HEAD_DIM < HEAD_DIM // 2
    low_lane = lane < HEAD_DIM
    q, k, v = q_ref[...], k_ref[...], v_ref[...]
    k_b, v_b = swap(k), swap(v)
    key, query = sublanes((rows, rows)), lanes((rows, rows))
    allowed = (key <= query) & (key < length)
    logsum_rows = jnp.transpose(logsum_ref[...])
    dk = [jnp.zeros((rows, 128), F32), jnp.zeros((rows, 128), F32)]
    dv = [jnp.zeros((rows, 128), F32), jnp.zeros((rows, 128), F32)]
    q_width = q.shape[1]
    pair = None
    for index in range(q_width // HEAD_DIM):
        same = index % 2 == (index // 2) % 2
        q_one, k_one = head_parts(q, k, k_b, index, low_lane)
        g_one, v_one = head_parts(heads_grad, v, v_b, index, low_lane)
        scores = jnp.where(allowed, dot(k_one, q_one, 1, 1) * inv, NEG)
        prob = jnp.exp(scores - logsum_rows[index : index + 1, :])
        grad_prob = dot(v_one, g_one, 1, 1)
        center = jnp.sum(prob * grad_prob, axis=0, keepdims=True)
        score_grad = (prob * (grad_prob - center)).astype(BF)
        dq = dot(score_grad, k_one, 0, 0) * inv
        place = 0 if same else 1
        dk[place] = dk[place] + dot(score_grad, q_one) * inv
        dv[place] = dv[place] + dot(prob.astype(BF), g_one)
        if index % 2 == 0:
            pair = dq
        else:
            cut = slice((index // 2) * 128, (index // 2) * 128 + 128)
            both = jnp.where(low_lane, pair, dq)
            back_ref[:, cut] = rotate128(both, cosine, sine, low_half).astype(BF)
    k_width = k.shape[1]
    k_total = dk[0] + pltpu.roll(dk[1], HEAD_DIM, 1)
    v_total = dv[0] + pltpu.roll(dv[1], HEAD_DIM, 1)
    back_ref[:, q_width : q_width + k_width] = rotate128(k_total, cosine, sine, low_half).astype(BF)
    back_ref[:, q_width + k_width :] = v_total.astype(BF)
    back = back_ref[...]
    first = (
        dot(back[:, :q_width], wq_ref[...], 1, 1)
        + dot(back[:, q_width : q_width + k_width], wk_ref[...], 1, 1)
        + dot(back[:, q_width + k_width :], wv_ref[...], 1, 1)
    )
    columns = width // tensor_count
    for t in range(tensor_count):
        first_ref[t] = first[:, t * columns : (t + 1) * columns].astype(BF)
    x = x_ref[...].astype(F32)
    scale = lax.rsqrt(jnp.mean(x * x, axis=-1, keepdims=True) + EPS)
    scale_ref[...] = jnp.broadcast_to(scale, (rows, 128))
    along = first * (x * scale)
    stat = jnp.sum(along * gain_ref[...].astype(F32)[None, :], axis=-1, keepdims=True)
    tiny_ref[:, 0:rows] = jnp.transpose(jnp.broadcast_to(stat, (rows, 128)))[0:8, :]
    tiny_ref[:, rows:] = jnp.broadcast_to(jnp.sum(along, axis=0, keepdims=True), (8, width))
    dense_ref[...] = dot(normed_ref[...], back, 0, 0).astype(BF)
    out_grad_ref[...] = dot(heads_ref[...], branch, 0, 0).astype(BF)
    load_x.wait()
    router_rows = dot(spread[:, 0:share, width:].reshape(rows, 128), normed2[...], 0, 0)[0:EXPERTS]
    gain2_sum = jnp.zeros((1, width), F32)
    for t in range(tensor_count):
        block = spread[t, share : share + 16, :width].astype(F32)
        gain2_sum = gain2_sum + block[0:1] + block[1:2]
    half = width // 2
    pieces = [router_rows[:, :half], router_rows[:, half:], gain2_sum[:, :half], gain2_sum[:, half:]]
    for one in row_parts:
        one.finish()
    filled = sum(piece.shape[0] for piece in pieces)
    small_ref[...] = jnp.concatenate(pieces + [jnp.zeros((SMALL_ROWS - filled, half), F32)], axis=0).astype(BF)
    net.close()


def back_call(group_count, lengths, vmem_operands, grad, xown, other=None):
    dy, x = vmem_operands[0], vmem_operands[1]
    rows, width = x.shape
    wq, wk, wv, wo = vmem_operands[13:17]
    tensor_count, dp_count = lax.axis_size("tensor"), lax.axis_size("dp")
    share, columns = rows // tensor_count, width // tensor_count
    chunks = group_count * tensor_count
    inner = wq.shape[1] + wk.shape[1] + wv.shape[1]
    shape = jax.ShapeDtypeStruct
    copies = 64
    passed = [] if other is None else [other]
    return pl.pallas_call(
        functools.partial(back_kernel, (group_count, tensor_count, dp_count), other is not None),
        out_shape=(
            shape((tensor_count, rows, columns), BF), shape((8, rows + width), F32), shape((rows, width), BF),
            shape((rows, 128), F32), shape((width, inner), BF), shape(wo.shape, BF), shape((SMALL_ROWS, width // 2), BF),
            *[shape(one.shape, BF) for one in passed],
        ),
        in_specs=[pl.BlockSpec(memory_space=pltpu.SMEM)] + vmem(len(vmem_operands)) + [pl.BlockSpec(memory_space=pl.ANY)] * (2 + len(passed)),
        out_specs=tuple(vmem(7)) + (pl.BlockSpec(memory_space=pl.ANY),) * len(passed),
        input_output_aliases={len(vmem_operands) + 3: 7} if passed else {},
        scratch_shapes=[
            pltpu.VMEM(grad.shape, BF),
            pltpu.VMEM((2, chunks - 1, share // 2, width + 128), BF),
            pltpu.VMEM((rows, width), BF),
            pltpu.VMEM((tensor_count, share + 16, width + 128), BF),
            pltpu.VMEM((rows, inner), BF),
            pltpu.VMEM((EXPERTS, rows), F32),
            pltpu.SemaphoreType.DMA((copies,)),
            pltpu.SemaphoreType.DMA((copies,)),
            pltpu.SemaphoreType.DMA((2,)),
        ],
        compiler_params=params(60, collective_id=2, has_side_effects=True),
        cost_estimate=pl.CostEstimate(flops=MIB, bytes_accessed=MIB, transcendentals=0),
        name="back",
    )(lengths, *vmem_operands, grad, xown, *passed)


def gate_rows(router_t, rows, table):
    logits = dot(router_t, rows, 1, 1)
    chosen = table > 0.5
    masked = jnp.where(chosen, logits, NEG)
    weights = jnp.where(chosen, jnp.exp(masked - jnp.max(masked, axis=0, keepdims=True)), 0.0)
    total = jnp.sum(weights, axis=0, keepdims=True)
    return weights / jnp.where(total > 0.0, total, 1.0)


def bit_steps(expert_count, tensor_count):
    expert_bits = [("expert", b) for b in bits_of(expert_count)]
    tensor_bits = [("tensor", b) for b in bits_of(tensor_count)]
    return expert_bits, tensor_bits, tensor_bits[1:][::-1]


def plane_gathers(net, target, share, first=None, done=False):
    counts = lax.axis_size("expert"), lax.axis_size("tensor")
    expert_bits, _, high_bits = bit_steps(*counts)
    size = share // 2
    parts = []
    for index, steps in enumerate((high_bits + expert_bits, expert_bits + high_bits)):

        def at(re, rt, offset=index * size):
            begin = pl.multiple_of(flip(net.me["tensor"], rt) * share + offset, size)
            return target.at[:, flip(net.me["expert"], re), pl.ds(begin, size)]

        source = None if first is None else first.at[:, pl.ds(index * size, size)]
        known = [(0, 0)]
        if done:
            axis, mask = steps.pop(0)
            known.append((mask, 0) if axis == "expert" else (0, mask))
        parts.append(Gather(net, at, steps, known=known, first=source))
    return parts


def core_gather(net, target, share, known, which=slice(None)):
    def whole(re, rt):
        begin = pl.multiple_of(flip(net.me["tensor"], rt) * share, share)
        return target.at[which, flip(net.me["expert"], re), pl.ds(begin, share)]

    return Gather(net, whole, [("tensor", 1)], known=known)


def fill_units(table, gate, slot_id, first_expert, count, hits_ref, gated_ref):
    capacity = slot_id.shape[0]
    for j in range(count):
        rank = table(first_expert + j).astype(jnp.int32) - 1
        hit = slot_id == rank
        cut = slice(j * capacity, (j + 1) * capacity)
        hits_ref[cut, :] = jnp.where(hit, 1.0, 0.0).astype(BF)
        gated_ref[cut, :] = jnp.where(hit, gate(first_expert + j), 0.0).astype(BF)


def middle(both, grad_act, hidden):
    g_here, u_here = both[:, :hidden], both[:, hidden:]
    sig = 1.0 / (1.0 + jnp.exp(-g_here))
    silu = g_here * sig
    act = silu * u_here
    grad_gate = (grad_act * u_here * sig * (1.0 + g_here * (1.0 - sig))).astype(BF)
    grad_up = (grad_act * silu).astype(BF)
    return act, jnp.concatenate([grad_gate, grad_up], axis=1)


def own_kernel(
    sizes, groups, capacity, local, batch, gathers,
    x_ref, dy_ref, table_ref, router_ref, wg_ref, wu_ref, wd_ref, hidden_ref, share_ref, far_dy_ref,
    out_c_ref, out_g_ref, xs_out, ys_out, oth_ref, othy_ref,
    gates, ranks, hits, gated, xs, ys, made, back, gi_rows, acc_c, acc_g, send_sem, recv_sem, local_sem,
):
    chunk, pair = pl.program_id(0), pl.program_id(1)
    pairs = local // 2
    per_batch = batch // 2
    expert_count, tensor_count, dp_count = sizes
    net = Net(send_sem, recv_sem)
    dp_here, me_t, me_e = net.me["dp"], net.me["tensor"], net.me["expert"]
    rows, width = x_ref.shape[-2:]
    units = groups
    hidden = wg_ref.shape[2]
    slot_id = sublanes((capacity, rows))
    share = rows // tensor_count

    if gathers:
        expert_bits, tensor_bits, high_bits = bit_steps(expert_count, tensor_count)
        cotangent_parts = plane_gathers(net, othy_ref, share, first=far_dy_ref)
        row_parts = plane_gathers(net, oth_ref, share)
        mine = pl.ds(pl.multiple_of(me_t * share, share), share)
        keep = pltpu.make_async_copy(far_dy_ref, othy_ref.at[:, me_e, mine], local_sem.at[2])
        flight = []

        def first_steps():
            net.barrier(expert_bits + tensor_bits + [("dp", m) for m in range(1, dp_count)])
            keep.start()
            for one in cotangent_parts:
                one.start()
            for m in range(1, dp_count):
                flight.append(net.send(share_ref, lambda m=m: oth_ref.at[m - 1, me_e, mine], "dp", m))

        def second_steps():
            for one in cotangent_parts:
                one.finish()
            for one in cotangent_parts:
                one.start()

        def third_steps():
            for one in cotangent_parts:
                one.finish()
            keep.wait()
            cotangent_parts.append(core_gather(net, othy_ref, share, cotangent_parts[0].known))
            cotangent_parts[-1].start()
            for copy in flight:
                copy.wait_recv()
            for one in row_parts:
                one.start()

        def last_steps():
            cotangent_parts[-1].finish()
            for one in row_parts:
                one.finish()
            net.close()

        for time, steps in ((0, first_steps), (pairs * 2 // 8, second_steps), (pairs * 6 // 8, third_steps)):

            @pl.when(pair == time)
            def _(steps=steps):
                steps()

    @pl.when(pair == 0)
    def _():
        gi_rows[...] = jnp.zeros_like(gi_rows)

        @pl.loop(0, units)
        def _(i):
            table = given_table(table_ref, i, dp_here.astype(F32))
            ranks[i] = table
            gates[i] = gate_rows(router_ref[...], x_ref[i], table)

    place = lax.rem(pair, per_batch)
    half = lax.div(pair, per_batch)
    group_start = pl.multiple_of(chunk * groups, groups)
    outs = []
    for index, (source, target) in enumerate(((xs, xs_out), (ys, ys_out))):
        outs.append(pltpu.make_async_copy(
            source, target.at[pl.ds(half * batch, batch), pl.ds(group_start, groups)], local_sem.at[index]
        ))

    @pl.when(place == 0)
    def _():
        @pl.loop(0, units)
        def _(i):
            fill_units(
                lambda e: ranks[i, pl.ds(e, 1), :], lambda e: gates[i, pl.ds(e, 1), :], slot_id,
                me_e * local + half * batch, batch, hits.at[i], gated.at[i],
            )
            xs[:, i] = dot(hits[i], x_ref[i]).astype(BF).reshape(batch, capacity, width)
            ys[:, i] = dot(gated[i], dy_ref[i]).astype(BF).reshape(batch, capacity, width)

        for copy in outs:
            copy.start()

    for j in range(2):
        spot = place * 2 + j
        x_here = xs[spot].reshape(units * capacity, width)
        y_here = ys[spot].reshape(units * capacity, width)
        inner_w = jnp.concatenate([wg_ref[j], wu_ref[j]], axis=1)
        both = dot(x_here, inner_w)
        grad_act = dot(y_here, wd_ref[j], 1, 1)
        act, grads = middle(both, grad_act, hidden)
        result = dot(act.astype(BF), wd_ref[j]).astype(BF)
        moved = dot(grads, inner_w, 1, 1).astype(BF)
        inner = jnp.sum(act * grad_act, axis=-1, keepdims=True)
        at_slot = pl.ds(pl.multiple_of(spot * capacity, capacity), capacity)
        for i in range(units):
            cut = slice(i * capacity, (i + 1) * capacity)
            made[i, at_slot, :] = result[cut]
            back[i, at_slot, :] = moved[cut]
            gi_rows[i, pl.ds(me_e * local + pair * 2 + j, 1), :] = jnp.sum(
                hits[i, at_slot, :].astype(F32) * inner[cut], axis=0, keepdims=True
            )

    @pl.when(place == per_batch - 1)
    def _():
        for copy in outs:
            copy.wait()

        @pl.loop(0, units)
        def _(i):
            add_c = dot(gated[i], made[i], 0, 0)
            add_g = dot(hits[i], back[i], 0, 0)

            @pl.when(half == 0)
            def _():
                acc_c[i] = add_c
                acc_g[i] = add_g

            @pl.when(half != 0)
            def _():
                acc_c[i] += add_c
                acc_g[i] += add_g

    @pl.when(pair == pairs - 1)
    def _():
        blocks, columns = out_c_ref.shape[1], out_c_ref.shape[3]
        for i in range(units):

            @pl.when(chunk * groups + i == me_e)
            def _():
                cut = pl.ds(pl.multiple_of(me_t * share, share), share)
                acc_c[i, cut, :] += hidden_ref[...]

            for t in range(blocks):
                out_c_ref[i, t] = acc_c[i, :, t * columns : (t + 1) * columns].astype(BF)
            out_g_ref[i, :, :width] = acc_g[i].astype(BF)
            out_g_ref[i, :, width:] = jnp.transpose(gi_rows[i]).astype(BF)
        if gathers:
            last_steps()


def own_call(x, dy, table, router_t, wg, wu, wd, hidden_share, normed_share, far_dy):
    sizes = tuple(lax.axis_size(axis) for axis in ("expert", "tensor", "dp"))
    groups_all, dp_count = table.shape[:2]
    rows, width = x.shape[-2:]
    groups = 2
    chunks = groups_all // groups
    local, _, hidden = wg.shape
    pairs = local // 2
    assert chunks == 1 or pairs == 1
    batch = min(8, local)
    gathers = chunks == 1
    capacity = rows * TOP // EXPERTS
    shape = jax.ShapeDtypeStruct
    row_block = pl.BlockSpec((groups, rows, width), lambda c, p: (c, 0, 0), pipeline_mode=pl.Buffered(1))
    in_block = pl.BlockSpec((2, width, hidden), lambda c, p: (p, 0, 0))
    blocks = sizes[1]
    columns = width // blocks
    copies = 64
    slots = shape((local, groups_all, capacity, width), BF)
    anywhere = pl.BlockSpec(memory_space=pl.ANY)
    return pl.pallas_call(
        functools.partial(own_kernel, sizes, groups, capacity, local, batch, gathers),
        out_shape=(
            shape((groups_all, blocks, rows, columns), BF), shape((groups_all, rows, width + 128), BF), slots, slots,
            *[shape((dp_count - 1, groups_all, rows, width) if gathers else (16, 128), BF)] * 2,
        ),
        grid=(chunks, pairs),
        in_specs=[
            row_block, row_block,
            pl.BlockSpec((groups, dp_count, TABLE_ROWS, rows), lambda c, p: (c, 0, 0, 0)),
            pl.BlockSpec((EXPERTS, width), lambda c, p: (0, 0)),
            in_block, in_block, pl.BlockSpec((2, hidden, width), lambda c, p: (p, 0, 0)),
            pl.BlockSpec(hidden_share.shape, lambda c, p: (0, 0)), anywhere, anywhere,
        ],
        out_specs=(
            pl.BlockSpec((groups, blocks, rows, columns), lambda c, p: (c, 0, 0, 0)),
            pl.BlockSpec((groups, rows, width + 128), lambda c, p: (c, 0, 0)),
            anywhere, anywhere, anywhere, anywhere,
        ),
        scratch_shapes=[
            pltpu.VMEM((groups, EXPERTS, rows), F32),
            pltpu.VMEM((groups, EXPERTS, rows), F32),
            pltpu.VMEM((groups, batch * capacity, rows), BF),
            pltpu.VMEM((groups, batch * capacity, rows), BF),
            pltpu.VMEM((batch, groups, capacity, width), BF),
            pltpu.VMEM((batch, groups, capacity, width), BF),
            pltpu.VMEM((groups, batch * capacity, width), BF),
            pltpu.VMEM((groups, batch * capacity, width), BF),
            pltpu.VMEM((groups, 128, rows), F32),
            pltpu.VMEM((groups, rows, width), F32),
            pltpu.VMEM((groups, rows, width), F32),
            pltpu.SemaphoreType.DMA((copies,)),
            pltpu.SemaphoreType.DMA((copies,)),
            pltpu.SemaphoreType.DMA((4,)),
        ],
        compiler_params=params(
            60, dimension_semantics=("arbitrary", "arbitrary"),
            **(dict(collective_id=3, has_side_effects=True) if gathers else {}),
        ),
        cost_estimate=pl.CostEstimate(flops=MIB, bytes_accessed=MIB, transcendentals=0),
        name="experts_own",
    )(x, dy, table, router_t, wg, wu, wd, hidden_share, normed_share, far_dy)


def slots_kernel(
    sizes, masks, capacity, local, batch, reduces, x_hbm, dy_hbm, table_ref, router_ref, *rest,
):
    if reduces:
        (
            dense_in, heads_in, small_in, first_in, out_in, old_hbm, x_tok_hbm, stat_in, scale_ref, gain_ref,
            x_hbm, xs_ref, ys_ref, sums_ref, input_ref, block_ref, gain_out_ref,
            x_buf, y_buf, hits, gated, dense, heads, small, first, out, dense_land, heads_land, small_land, first_land, out_land,
            stat, stat_land, gains, gains_land, old, x_tok, load_sem, send_sem, recv_sem, local_sem,
        ) = rest
    else:
        xs_ref, ys_ref, x_buf, y_buf, hits, gated, load_sem = rest
    expert_count, tensor_count, dp_count = sizes
    unit = pl.program_id(0)
    units = pl.num_programs(0)
    rows, width = x_buf.shape[-2:]
    me_e, me_d = lax.axis_index("expert"), lax.axis_index("dp")
    per_mask = expert_count
    slot_id = sublanes((capacity, rows))

    def far_dp(m):
        value = me_d
        for bit in bits_of(dp_count):
            on = lax.rem(lax.div(m, bit), 2)
            value = value + on * (bit - 2 * bit * lax.rem(lax.div(me_d, bit), 2))
        return value

    def place(i):
        m = masks[0] + lax.div(i, per_mask)
        return m, lax.rem(i, per_mask), far_dp(m)

    def loads(i):
        m, group, d = place(i)
        slot = lax.rem(i, 2)
        y_source = dy_hbm.at[m - masks[0], group] if len(dy_hbm.shape) == 4 else dy_hbm.at[group]
        x_source = x_hbm.at[m - masks[0], group] if len(x_hbm.shape) == 4 else x_hbm.at[group]
        return (
            pltpu.make_async_copy(x_source, x_buf.at[slot], load_sem.at[slot, 0]),
            pltpu.make_async_copy(y_source, y_buf.at[slot], load_sem.at[slot, 1]),
        )

    if reduces:
        net = Net(send_sem, recv_sem)
        me_t = net.me["tensor"]
        ways = expert_count * dp_count
        expert_bits = [("expert", b) for b in bits_of(expert_count)]
        tensor_bits = [("tensor", b) for b in bits_of(tensor_count)]
        dp_bits = [("dp", b) for b in bits_of(dp_count)][::-1]
        chunks = [(e, d) for e in range(expert_count) for d in range(dp_count)]
        plane = [(e, t) for e in range(expert_count) for t in range(0, tensor_count, 2)]
        share = rows // tensor_count
        cores = [core_gather(net, x_hbm, share, plane, which) for which in range(dp_count - 1)]

        def chunk_of(ref):
            size = ref.shape[0] // ways

            def at(re, rd):
                index = flip(me_e, re) * dp_count + flip(me_d, rd)
                return ref.at[pl.ds(pl.multiple_of(index * size, size), size)]

            return at

        sums = [
            Reduce(net, chunk_of(dense), lambda i: dense_land.at[i], expert_bits + dp_bits, chunks),
            Reduce(net, chunk_of(heads), lambda i: heads_land.at[i], dp_bits + expert_bits, chunks),
            Reduce(net, chunk_of(small), lambda i: small_land.at[i], dp_bits + expert_bits, chunks),
            Reduce(
                net, lambda re, rt: out.at[flip(me_e, re), flip(me_t, rt)], lambda i: out_land.at[i],
                tensor_bits + expert_bits, [(e, t) for e in range(expert_count) for t in range(tensor_count)],
            ),
            Reduce(
                net, lambda re, rt: first.at[flip(me_t, rt)], lambda i: first_land.at[i], tensor_bits,
                [(0, t) for t in range(tensor_count)],
            ),
        ]
        chains = [
            AllReduce(net, stat, stat_land, tensor_bits),
            AllReduce(net, gains, gains_land, tensor_bits + expert_bits + dp_bits),
        ]
        columns = first.shape[2]
        begin = pl.multiple_of(me_t * columns, columns)

        count = len(masks) * expert_count
        times = [[0, 2, 4], [0, 2, 4], [0, 2, 4], [0, 2, 4], [0, 1]]

        def advance(k):
            for one, when in zip(sums, times):
                if k in when or k == count:
                    if one.flight:
                        one.finish()
                    if one.steps:
                        one.start()

        @pl.when(unit == 0)
        def _():
            pairs = (
                (dense_in, dense), (heads_in, heads), (small_in, small), (first_in, first), (out_in, out),
                (stat_in.at[:, 0:rows], stat.at[0]), (stat_in.at[:, rows:], gains.at[0]),
                (old_hbm.at[:, pl.ds(begin, columns)], old), (x_tok_hbm.at[:, pl.ds(begin, columns)], x_tok),
            )
            moves = [pltpu.make_async_copy(a, b, local_sem.at[i]) for i, (a, b) in enumerate(pairs)]
            for copy in moves:
                copy.start()
            net.barrier(expert_bits + tensor_bits + dp_bits)
            for one in cores:
                one.start()
            for copy in moves:
                copy.wait()
            advance(0)
            for chain in chains:
                chain.advance(0)

        for k in range(1, len(chains[1].steps)):

            @pl.when(unit == k)
            def _(k=k):
                advance(k)
                for chain in chains:
                    chain.advance(k)

        for m in range(dp_count - 1):

            @pl.when(unit == max(m * expert_count - 1, 0))
            def _(m=m):
                cores[m].finish()

    @pl.when(unit == 0)
    def _():
        for copy in loads(unit):
            copy.start()

    @pl.when(unit + 1 < units)
    def _():
        for copy in loads(unit + 1):
            copy.start()

    for copy in loads(unit):
        copy.wait()
    slot = lax.rem(unit, 2)
    _, group, d = place(unit)
    table = given_table(table_ref, group, d.astype(F32))
    gates = gate_rows(router_ref[...], x_buf[slot], table)
    router_rows = sublanes((EXPERTS, rows))

    def row_of(values):
        return lambda e: jnp.sum(jnp.where(router_rows == e, values, 0.0), axis=0, keepdims=True)

    for part in range(local // batch):
        fill_units(
            row_of(table), row_of(gates), slot_id, me_e * local + part * batch, batch, hits.at[part], gated.at[part]
        )
        cut = slice(part * batch, (part + 1) * batch)
        xs_ref[cut, 0] = dot(hits[part], x_buf[slot]).astype(BF).reshape(batch, capacity, width)
        ys_ref[cut, 0] = dot(gated[part], y_buf[slot]).astype(BF).reshape(batch, capacity, width)

    if reduces:

        @pl.when(unit == units - 1)
        def _():
            advance(count)
            chains[1].advance(len(chains[1].steps))
            here = me_e * dp_count + me_d
            d_rows, h_rows, s_rows = (ref.shape[0] // ways for ref in (dense, heads, small))
            half = heads.shape[1] // 2
            sums_ref[0:d_rows] = dense[pl.ds(pl.multiple_of(here * d_rows, d_rows), d_rows), :]
            mine = heads[pl.ds(pl.multiple_of(here * h_rows, h_rows), h_rows), :]
            sums_ref[d_rows : d_rows + h_rows] = mine[:, :half]
            sums_ref[d_rows + h_rows : d_rows + 2 * h_rows] = mine[:, half:]
            sums_ref[d_rows + 2 * h_rows :] = small[pl.ds(pl.multiple_of(here * s_rows, s_rows), s_rows), :]
            gain_out_ref[...] = gains[gains.shape[0] - 1]
            total = jnp.concatenate([stat[stat.shape[0] - 1], jnp.zeros((120, rows), F32)], axis=0)
            mean = jnp.transpose(total)[:, 0:1] / gain_ref.shape[0]
            scale = scale_ref[:, 0:1]
            input_ref[...] = (
                old[...].astype(F32) + scale * (
                    first[me_t].astype(F32) * gain_ref[pl.ds(begin, columns)].astype(F32)[None, :]
                    - x_tok[...].astype(F32) * scale * mean
                )
            ).astype(BF)
            block_ref[...] = out[me_e, me_t]
            net.close()


def slots_call(masks, x, dy, table, router_t, local, sums=None):
    sizes = tuple(lax.axis_size(axis) for axis in ("expert", "tensor", "dp"))
    expert_count, _, dp_count = sizes
    rows, width = x.shape[-2:]
    units = expert_count * len(masks)
    capacity = rows * TOP // EXPERTS
    batch = min(8, local)
    shape = jax.ShapeDtypeStruct
    anywhere = pl.BlockSpec(memory_space=pl.ANY)
    block = pl.BlockSpec((local, 1, capacity, width), lambda i: (0, i, 0, 0))
    whole = pl.BlockSpec(memory_space=pltpu.VMEM)
    out_shape = [shape((local, units, capacity, width), BF)] * 2
    out_specs = [block, block]
    aliases = {}
    operands = [x, dy, table, router_t]
    in_specs = [anywhere, anywhere, whole, whole]
    scratch = [
        pltpu.VMEM((2, rows, width), BF), pltpu.VMEM((2, rows, width), BF),
        pltpu.VMEM((local // batch, batch * capacity, rows), BF), pltpu.VMEM((local // batch, batch * capacity, rows), BF),
    ]
    tail = [pltpu.SemaphoreType.DMA((2, 2))]
    more = {}
    if sums is not None:
        dense, heads, small, first, out, old, tokens, stat, scale, gain = sums
        ways = expert_count * dp_count
        columns = first.shape[2]
        chunk = [values.shape[0] // ways for values in (dense, heads, small)]
        operands += [dense, heads, small, first, out, old, tokens, stat, scale, gain]
        in_specs += [anywhere] * 8 + [whole] * 2
        out_shape += [
            shape((chunk[0] + 2 * chunk[1] + chunk[2], dense.shape[1]), BF), shape((rows, columns), BF), shape((rows, columns), BF),
            shape((8, width), F32),
        ]
        out_specs += [whole] * 4
        out_shape = [shape(x.shape, BF)] + out_shape
        out_specs = [anywhere] + out_specs
        aliases = {0: 0}
        steps = len(bits_of(sizes[1]))
        rounds = steps + len(bits_of(ways))
        scratch += [pltpu.VMEM(values.shape, BF) for values in (dense, heads, small, first, out)]
        scratch += [
            pltpu.VMEM((ways - 1, chunk[0], dense.shape[1]), BF), pltpu.VMEM((ways - 1, chunk[1], heads.shape[1]), BF),
            pltpu.VMEM((ways - 1, chunk[2], small.shape[1]), BF), pltpu.VMEM((first.shape[0] - 1, rows, columns), BF),
            pltpu.VMEM((expert_count * sizes[1] - 1, rows, columns), BF),
            pltpu.VMEM((steps + 1, 8, rows), F32), pltpu.VMEM((steps, 8, rows), F32),
            pltpu.VMEM((rounds + 1, 8, width), F32), pltpu.VMEM((rounds, 8, width), F32),
            pltpu.VMEM((rows, columns), BF), pltpu.VMEM((rows, columns), BF),
        ]
        tail += [pltpu.SemaphoreType.DMA((64,)), pltpu.SemaphoreType.DMA((64,)), pltpu.SemaphoreType.DMA((9,))]
        more = dict(collective_id=4, has_side_effects=True)
    return pl.pallas_call(
        functools.partial(slots_kernel, sizes, masks, capacity, local, batch, sums is not None),
        out_shape=tuple(out_shape),
        grid=(units,),
        in_specs=in_specs,
        out_specs=tuple(out_specs),
        input_output_aliases=aliases,
        scratch_shapes=scratch + tail,
        compiler_params=params(60, dimension_semantics=("arbitrary",), **more),
        cost_estimate=pl.CostEstimate(flops=MIB, bytes_accessed=MIB, transcendentals=0),
        name="slots",
    )(*operands)


def weights_kernel(counts, chunks, capacity, has_partial, wg_ref, wu_ref, wd_ref, *rest):
    parts = len(counts)
    xs_refs, ys_refs, rest = rest[:parts], rest[parts : 2 * parts], rest[2 * parts :]
    if has_partial:
        in_g, in_u, in_d, gg_ref, gu_ref, gd_ref, x_buf, y_buf, sem = rest
    else:
        gg_ref, gu_ref, gd_ref, x_buf, y_buf, sem = rest
    expert, chunk = pl.program_id(0), pl.program_id(1)
    step = expert * chunks + chunk
    total = pl.num_programs(0) * chunks

    def loads(s):
        e, c, slot = lax.div(s, chunks), lax.rem(s, chunks), lax.rem(s, 2)
        copies, start = [], 0
        for index, count in enumerate(counts):
            take = count // chunks
            for which, (refs, buf) in enumerate(((xs_refs, x_buf), (ys_refs, y_buf))):
                copies.append(pltpu.make_async_copy(
                    refs[index].at[e, pl.ds(c * take, take)], buf.at[slot, pl.ds(start, take)], sem.at[slot, index, which]
                ))
            start += take
        return copies

    @pl.when(step == 0)
    def _():
        for copy in loads(step):
            copy.start()

    @pl.when(step + 1 < total)
    def _():
        for copy in loads(step + 1):
            copy.start()

    for copy in loads(step):
        copy.wait()
    slot = lax.rem(step, 2)
    width, hidden = wg_ref.shape[1:]
    x_here = x_buf[slot].reshape(-1, width)
    y_here = y_buf[slot].reshape(-1, width)
    both = dot(x_here, jnp.concatenate([wg_ref[0], wu_ref[0]], axis=1))
    grad_act = dot(y_here, wd_ref[0], 1, 1)
    act, grads = middle(both, grad_act, hidden)
    inner = dot(x_here, grads, 0, 0)
    down = dot(act.astype(BF), y_here, 0, 0)

    def put(ref, values, partial):
        if chunks == 1:
            ref[0] = values + partial[0] if has_partial else values
            return

        @pl.when(chunk == 0)
        def _():
            ref[0] = values + partial[0] if has_partial else values

        @pl.when(chunk != 0)
        def _():
            ref[0] += values

    put(gg_ref, inner[:, :hidden], in_g if has_partial else None)
    put(gu_ref, inner[:, hidden:], in_u if has_partial else None)
    put(gd_ref, down, in_d if has_partial else None)


def weights_call(slots, wg, wu, wd, partial=None):
    local, width, hidden = wg.shape
    capacity = slots[0][0].shape[2]
    counts = [xs.shape[1] for xs, _ in slots]
    chunks = max(1, sum(counts) // 8)
    assert len(counts) == 1 or chunks == 1
    shape = jax.ShapeDtypeStruct
    in_block = pl.BlockSpec((1, width, hidden), lambda e, c: (e, 0, 0))
    down_block = pl.BlockSpec((1, hidden, width), lambda e, c: (e, 0, 0))
    specs = (in_block, in_block, down_block)
    more = list(partial) if partial is not None else []
    buffer = pltpu.VMEM((2, sum(counts) // chunks, capacity, width), BF)
    return pl.pallas_call(
        functools.partial(weights_kernel, counts, chunks, capacity, partial is not None),
        out_shape=(shape(wg.shape, F32), shape(wu.shape, F32), shape(wd.shape, F32)),
        grid=(local, chunks),
        in_specs=list(specs) + [pl.BlockSpec(memory_space=pl.ANY)] * (2 * len(slots)) + (list(specs) if more else []),
        out_specs=specs,
        scratch_shapes=[buffer, buffer, pltpu.SemaphoreType.DMA((2, len(counts), 2))],
        compiler_params=params(60, dimension_semantics=("arbitrary", "arbitrary")),
        cost_estimate=pl.CostEstimate(flops=80 * 10**9, bytes_accessed=100 * MIB, transcendentals=0),
        name="weights",
    )(wg, wu, wd, *[xs for xs, _ in slots], *[ys for _, ys in slots], *more)


def unpack_kernel(sums_ref, q_ref, k_ref, v_ref, heads_ref, router_ref, gain_ref):
    ways = sums_ref.shape[0]
    d_rows, h_rows, s_rows = q_ref.shape[0] // ways, heads_ref.shape[0] // ways, SMALL_ROWS // ways
    q_width, k_width, half = q_ref.shape[1], k_ref.shape[1], heads_ref.shape[1] // 2
    small = []
    for i in range(ways):
        block = sums_ref[i].astype(F32)
        cut = slice(i * d_rows, (i + 1) * d_rows)
        q_ref[cut, :] = block[:d_rows, :q_width]
        k_ref[cut, :] = block[:d_rows, q_width : q_width + k_width]
        v_ref[cut, :] = block[:d_rows, q_width + k_width :]
        cut = slice(i * h_rows, (i + 1) * h_rows)
        heads_ref[cut, :half] = block[d_rows : d_rows + h_rows]
        heads_ref[cut, half:] = block[d_rows + h_rows : d_rows + 2 * h_rows]
        small.append(block[d_rows + 2 * h_rows :])
    small = jnp.concatenate(small, axis=0)
    router_ref[:, :half] = small[:EXPERTS]
    router_ref[:, half:] = small[EXPERTS : 2 * EXPERTS]
    gain_ref[...] = small[2 * EXPERTS : 2 * EXPERTS + 2]


def unpack_call(sums, q_width, k_width, heads_shape):
    ways = sums.shape[0]
    width = heads_shape[1]
    shape = jax.ShapeDtypeStruct
    return pl.pallas_call(
        unpack_kernel,
        out_shape=(
            shape((width, q_width), F32), shape((width, k_width), F32), shape((width, k_width), F32), shape(heads_shape, F32),
            shape((EXPERTS, width), F32), shape((2, width // 2), F32),
        ),
        in_specs=vmem(1),
        out_specs=tuple(vmem(6)),
        compiler_params=params(32),
        cost_estimate=pl.CostEstimate(flops=MIB, bytes_accessed=5 * MIB, transcendentals=0),
        name="unpack",
    )(sums)


def on_device(
    tokens, cotangent, seq_lengths, deal_order, routes, slot_order, first_gain, w_query, w_key, w_value, w_out,
    second_gain, w_router, w_gate, w_up, w_down,
):
    dp_count = lax.axis_size("dp")
    dp_index = lax.axis_index("dp")
    tensor_count = lax.axis_size("tensor")
    tensor_index = lax.axis_index("tensor")
    expert_count = lax.axis_size("expert")
    expert_index = lax.axis_index("expert")
    rows, width = tokens.shape
    share = rows // tensor_count
    everywhere = ("expert", "dp", "tensor")
    unit_shape = (expert_count, dp_count, rows, width)

    cosine, sine = (jnp.asarray(values) for values in rotary_tables(rows))
    gain1, gain2 = first_gain, second_gain
    router_t = w_router.T
    normed, q, k, v, heads, logsum, hidden, normed_share, tables, far_dy, x_own, dy_own = front(
        seq_lengths, deal_order, tokens, gain1, w_query, w_key, w_value, w_out, cosine, sine, gain2, routes.T, slot_order, cotangent
    )
    never = seq_lengths[0, 0] < 0
    rows_all = ("expert", "dp")

    def after(values, other):
        return jnp.where(never, other.astype(values.dtype), values)

    small_mesh = expert_count == 2
    out_c, out_g, xs_own, ys_own, x_other, dy_other = own_call(
        x_own, dy_own, tables, router_t, w_gate, w_up, w_down, hidden, normed_share, far_dy
    )
    group_count = expert_count
    if not small_mesh:
        out_c = lax.psum_scatter(out_c, "expert", scatter_dimension=0, tiled=True)
        out_g = lax.psum_scatter(out_g, "expert", scatter_dimension=0, tiled=True)
        x_own = lax.dynamic_slice_in_dim(x_own, expert_index, 1, 0)
        group_count = 1
    first, stat, hidden_grad, scale, dense, heads_grad, small, *x_passed = back_call(
        group_count, seq_lengths,
        (cotangent, tokens, gain1, gain2, router_t, hidden, tables, normed, q, k, v, heads, logsum,
         w_query, w_key, w_value, w_out, cosine, sine),
        out_g, x_own, x_other if small_mesh else None,
    )
    local = w_gate.shape[0]
    q_width, k_width = w_query.shape[1], w_key.shape[1]
    half, columns = width // 2, width // tensor_count
    if small_mesh:
        _, xs, ys, sums, input_grad, block_out, gain1_rows = slots_call(
            tuple(range(1, dp_count)), x_passed[0], dy_other, tables, router_t, local,
            (dense, heads_grad, small, first, out_c, hidden_grad, tokens, stat, scale, gain1),
        )
        gain1_sum = gain1_rows[0]
        ways = expert_count * dp_count
        sums = lax.all_gather(sums, rows_all, axis=0)
        gate_grad, up_grad, down_grad = weights_call([(xs_own, ys_own), (xs, ys)], w_gate, w_up, w_down)
        q_sum, k_sum, v_sum, out_sum, router_rows, gain2_rows = unpack_call(sums, q_width, k_width, w_out.shape)
        router_sum, gain2_sum = router_rows.T, gain2_rows.reshape(width)
    else:
        grads = weights_call([(xs_own, ys_own)], w_gate, w_up, w_down)
        for mask in range(1, dp_count):
            moved = (
                lax.all_gather(
                    after(values[mask - 1], grads[2][0, 0, 0]), ("expert", "tensor"), axis=0, tiled=True
                ).reshape(expert_count, rows, width)
                for values in (
                    [lax.ppermute(normed_share, "dp", [(i, i ^ m) for i in range(dp_count)]) for m in range(1, dp_count)],
                    far_dy,
                )
            )
            xs, ys = slots_call((mask,), *moved, tables, router_t, local)
            grads = weights_call([(xs, ys)], w_gate, w_up, w_down, grads)
        gate_grad, up_grad, down_grad = grads
        dense_sum, out_sum, small_sum = (
            values.astype(F32) for values in lax.psum((dense, heads_grad, small), rows_all)
        )
        gain1_sum = lax.psum(stat[0, rows:], everywhere)
        q_sum, k_sum, v_sum = jnp.split(dense_sum, [q_width, q_width + k_width], axis=1)
        router_sum = jnp.concatenate([small_sum[:EXPERTS], small_sum[EXPERTS : 2 * EXPERTS]], axis=1)
        gain2_sum = small_sum[2 * EXPERTS : 2 * EXPERTS + 2].reshape(width)
        router_sum = router_sum.T
        block_out = lax.psum_scatter(out_c[0], "tensor", scatter_dimension=0, tiled=True)[0]
        first_sum = lax.psum_scatter(first, "tensor", scatter_dimension=0, tiled=True)[0].astype(F32)
        mean = lax.psum(stat[0, :rows], "tensor")[:, None] / width

        def cols(values):
            return lax.dynamic_slice_in_dim(values, tensor_index * columns, columns, -1).astype(F32)

        input_grad = (
            cols(hidden_grad) + scale[:, :1] * (first_sum * cols(gain1) - cols(tokens) * scale[:, :1] * mean)
        ).astype(BF)
    return (
        block_out, input_grad, gain1_sum, q_sum, k_sum, v_sum, out_sum, gain2_sum, router_sum,
        gate_grad, up_grad, down_grad,
    )


def solution(mesh):
    rows2 = P(("expert", "dp"), None)
    placed = (
        rows2, rows2, P("expert", None), P("expert", None), rows2, rows2, P(),
        P(None, "tensor"), P(None, "tensor"), P(None, "tensor"), P("tensor", None), P(), P(),
        P("expert", None, "tensor"), P("expert", None, "tensor"), P("expert", "tensor", None),
    )
    return jax.shard_map(
        on_device,
        mesh=mesh,
        in_specs=placed,
        out_specs=(
            P(("expert", "dp"), "tensor"), P(("expert", "dp"), "tensor"), P(),
            P(None, "tensor"), P(None, "tensor"), P(None, "tensor"), P("tensor", None), P(), P(),
            P("expert", None, "tensor"), P("expert", None, "tensor"), P("expert", "tensor", None),
        ),
        check_vma=False,
    )
```

time: 352 us -> 273 us (0.78)
  waiting for transfers between devices: 74.4 us -> 0.02 us
  other arithmetic: 9.77 us -> 0 us
  Pallas kernels: 248 us -> 254 us
    all_gather x2 -> x1, waiting for transfers between devices: 60.4 us -> 0.01 us  [on_device(): sums = lax.all_gather(sums, rows_all, axis=0)]
    pallas_call x2 -> x4, Pallas kernels: 134 us -> 149 us  [the longest x1 49.2 us: weights_call(): pl.pallas_call(functools.partial(weights_kernel, counts, chunks, capacity...]
    psum x1 -> x0, waiting for transfers between devices: 14 us -> none  [on_device(): lax.psum((out_term, q_term, k_term, v_term, small), ('expert', 'dp'))]
    pallas_call x1, Pallas kernels: 64.9 us -> 53.8 us  [back_call(): pl.pallas_call(functools.partial(back_kernel, (group_count, tensor_count,...]
    select_n x4 -> x0, other arithmetic: 9.77 us -> none  [after(): return jnp.where(never, other.astype(values.dtype), values)]
  transfers between devices with their start and end apart: 3 -> 1, of which waited for: 3 -> 0; matrix products, arithmetic and copies ran while one was open for 0% -> 0% of each run, Pallas kernels for 52% -> 18%
where the time goes in v3:
time: 273 us
  Pallas kernels  254 us (93%)
  between operations  14.1 us (5%)
  local copies, waits for them, and re-layouts  4.81 us (2%)
    pallas_call x1, Pallas kernels, back_call(): pl.pallas_call(functools.partial(back_kernel, (group_count, tensor_count,...  53.8 us
    pallas_call x1, Pallas kernels, front(): pl.pallas_call(functools.partial(front_kernel, sizes), out_shape=(shape((...  51.3 us
    pallas_call x1, Pallas kernels, weights_call(): pl.pallas_call(functools.partial(weights_kernel, counts, chunks, capacity...  49.2 us
    pallas_call x1, Pallas kernels, slots_call(): pl.pallas_call(functools.partial(slots_kernel, sizes, masks, capacity, lo...  49.2 us
    pallas_call x1, Pallas kernels, own_call(): pl.pallas_call(functools.partial(own_kernel, sizes, groups, capacity, loc...  48.9 us
  transfers between devices with their start and end apart: 1, of which 0 were waited for; matrix products, arithmetic and copies ran while one was open for 0% of the time, Pallas kernels for 18%

profile of v3, /device:TPU:0, one launch (start us, length us, event | category | flops | bytes accessed | tf_op | source)
XLA Modules:
  0.0 273.1 jit_solution(5988956345562090935)
XLA Ops:
  7.2 0.0 all-gather.3.cloned.1.call-start
  7.2 51.3 %front.1 = (bf16[512,1024]{1,0:T(8,128)(2,1)}, bf16[512,256]{1,0:T(8,128)(2,1)}, bf16[512,128]{1,0:T(8,128)(2,1)}, bf16[512,128]{1,0:T(8,128)(2,1)}, bf16[512,25...) custom-call(s32[1,4]{1,0:T(1,128)} %lengths_ref.3, ...), custom_call_target="tpu_custom_call" | custom-call | flops 1048576 | bytes 1048576 | tf_op jit(solution)/shard_map/front/pallas_call | solution.py:384
  58.5 48.9 %experts_own.1 = (bf16[2,4,512,256]{3,2,1,0:T(8,128)(2,1)}, bf16[2,512,1152]{2,1,0:T(8,128)(2,1)}, bf16[16,2,128,1024]{3,2,1,0:T(8,128)(2,1)}, bf16[16,2,128,102...) custom-call(bf16[2,512,1024]{2,1,0:T(8,128)(2,1)} %get-tuple-element.61.x_ref.xown_ref, ...), custom_call_target="tpu_custom_call" | custom-call | flops 1048576 | bytes 1048576 | tf_op jit(solution)/shard_map/experts_own/pallas_call | solution.py:848
  107.4 53.8 %back.1 = (bf16[4,512,256]{2,1,0:T(8,128)(2,1)}, f32[8,1536]{1,0:T(8,128)}, bf16[512,1024]{1,0:T(8,128)(2,1)}, f32[512,128]{1,0:T(8,128)}, bf16[1024,512]{1,0:T(...) custom-call(s32[1,4]{1,0:T(1,128)} %lengths_ref.3, ...), custom_call_target="tpu_custom_call", output_to_operand_aliasing={{7}: (22, {})} | custom-call | flops 1048576 | bytes 1048576 | tf_op jit(solution)/shard_map/back/pallas_call | solution.py:584
  161.2 49.2 %slots.1 = (bf16[3,2,512,1024]{3,2,1,0:T(8,128)(2,1)}, bf16[16,6,128,1024]{3,2,1,0:T(8,128)(2,1)}, bf16[16,6,128,1024]{3,2,1,0:T(8,128)(2,1)}, bf16[208,512]{1,0...) custom-call(bf16[3,2,512,1024]{3,2,1,0:T(8,128)(2,1)} %get-tuple-ele, ...), custom_call_target="tpu_custom_call", output_to_operand_aliasing={{0}: (0, {})} | custom-call | flops 1048576 | bytes 1048576 | tf_op jit(solution)/shard_map/slots/pallas_call | solution.py:1125
  210.4 0.0 all-gather.3.cloned.1.call-update
  210.4 0.0 copy-start.2
  210.4 0.0 copy-start.1
  210.4 49.2 %weights.1 = (f32[16,1024,128]{2,1,0:T(8,128)}, f32[16,1024,128]{2,1,0:T(8,128)}, f32[16,128,1024]{2,1,0:T(8,128)}) custom-call(bf16[16,1024,128]{2,1,0:T(8,128)(2,1)} %wg_ref.3, bf16[16,1024,128]{2,1,0:T(8,128)(2,1)} %wu_ref.3, bf16[16,128,1024]{2,1,0:T(8,128)(2,1)} %wd_ref.3, bf16[16,2,128,1024]{3,2,1,0:T(8,128)(2,1)} %get-tuple-element.87.rest_0_, ...), custom_call_target="tpu_custom_call" | custom-call | flops 80000000000 | bytes 104857600 | tf_op jit(solution)/shard_map/weights/pallas_call | solution.py:1214
  259.6 1.4 slice.3
  260.9 0.0 all-gather.3.cloned.1.call-done
  260.9 0.0 copy-start
  260.9 1.5 copy-done
  262.4 1.8 unpack.1
  264.2 0.6 copy.32
  264.8 0.0 copy-done.2
  264.8 0.7 copy.37
  265.5 0.0 copy-done.1
  265.5 0.7 copy.38
Async XLA Ops:
  7.2 253.8 %all-gather.3.cloned.1.call-start = ((), (), s32[]{:S(2)}) async-start(), calls=%async_computation | async-start | bytes 1916928 | tf_op jit(solution)/shard_map/all_gather | solution.py:1319
  210.4 54.4 %copy-start.2 = (bf16[512,256]{1,0:T(8,128)(2,1)S(1)}, bf16[512,256]{1,0:T(8,128)(2,1)}, u32[]{:S(2)}) copy-start(bf16[512,256]{1,0:T(8,128)(2,1)} %get-tuple-element.106) | copy-start | bytes 786436
  210.4 55.1 %copy-start.1 = (bf16[512,256]{1,0:T(8,128)(2,1)S(1)}, bf16[512,256]{1,0:T(8,128)(2,1)}, u32[]{:S(2)}) copy-start(bf16[512,256]{1,0:T(8,128)(2,1)} %get-tuple-element.107) | copy-start | bytes 786436
  260.9 1.5 copy-start
Sparse Core Ops, SparseCore 0:
  210.5 43.1 all-gather.2

commit v4 on v3

--- a/solution.py
+++ b/solution.py
@@ -80,16 +80,18 @@
 
     def barrier(self, partners):
         sem = pltpu.get_barrier_semaphore()
-        for axis, mask in partners:
-            pl.semaphore_signal(
-                sem, inc=1, device_id={axis: flip(self.me[axis], mask)}, device_id_type=pl.DeviceIdType.MESH
-            )
+        for partner in partners:
+            pl.semaphore_signal(sem, inc=1, device_id=self.device(partner), device_id_type=pl.DeviceIdType.MESH)
         pl.semaphore_wait(sem, len(partners))
 
-    def send(self, source, target, axis, mask):
+    def device(self, partner):
+        pairs = [partner] if isinstance(partner[0], str) else partner
+        return {axis: flip(self.me[axis], mask) for axis, mask in pairs}
+
+    def send(self, source, target, *partner):
         k = self.used
         self.used += 1
-        copy = Copy(self, k, source, target, axis, mask)
+        copy = Copy(self, k, source, target, partner)
         copy.build().start()
         self.copies.append(copy)
         return copy
@@ -100,8 +102,8 @@
 
 
 class Copy:
-    def __init__(self, net, index, source, target, axis, mask):
-        self.net, self.index, self.source, self.target, self.axis, self.mask = net, index, source, target, axis, mask
+    def __init__(self, net, index, source, target, partner):
+        self.net, self.index, self.source, self.target, self.partner = net, index, source, target, partner
 
     def build(self):
         source = self.source() if callable(self.source) else self.source
@@ -109,7 +111,7 @@
         return pltpu.make_async_remote_copy(
             src_ref=source, dst_ref=target,
             send_sem=self.net.send_sem.at[self.index], recv_sem=self.net.recv_sem.at[self.index],
-            device_id={self.axis: flip(self.net.me[self.axis], self.mask)}, device_id_type=pl.DeviceIdType.MESH,
+            device_id=self.net.device(self.partner), device_id_type=pl.DeviceIdType.MESH,
         )
 
     def wait_recv(self):
@@ -144,45 +146,42 @@
     def start(self):
         axis, mask = self.steps.pop(0)
         side = 0 if axis == "expert" else 1
-        going = [r for r in self.live if r[side] & mask]
-        self.live = [r for r in self.live if not r[side] & mask]
+        going = [r for r in self.live if (r[side] & mask if mask else r[side])]
+        self.live = [r for r in self.live if r not in going]
         for r in going:
-            kept = (r[0] ^ mask, r[1]) if side == 0 else (r[0], r[1] ^ mask)
-            copy = self.net.send(functools.partial(self.at, *r), functools.partial(self.landing, self.used), axis, mask)
+            toward = mask or r[side]
+            kept = (r[0] ^ toward, r[1]) if side == 0 else (r[0], r[1] ^ toward)
+            copy = self.net.send(functools.partial(self.at, *r), functools.partial(self.landing, self.used), axis, toward)
             self.flight.append((kept, copy, self.used))
             self.used += 1
-        if self.steps:
-            axis, mask = self.steps[0]
-            side = 0 if axis == "expert" else 1
-            self.flight.sort(key=lambda item: 0 if item[0][side] & mask else 1)
 
     def finish(self):
-        for kept, copy, slot in self.flight:
+        for place in sorted({kept for kept, _, _ in self.flight}):
+            total = self.at(*place)[...].astype(F32)
+            for kept, copy, slot in self.flight:
+                if kept == place:
+                    copy.wait_recv()
+                    total = total + self.landing(slot)[...].astype(F32)
+            self.at(*place)[...] = total.astype(BF)
+        self.flight = []
+
+
+class Exchange:
+    def __init__(self, net, stages, k, landing, partners):
+        self.net, self.stages, self.k, self.landing, self.partners, self.flight = net, stages, k, landing, partners, []
+
+    def start(self):
+        for index, partner in enumerate(self.partners):
+            self.flight.append(self.net.send(
+                lambda: self.stages.at[self.k], lambda index=index: self.landing.at[index], *partner
+            ))
+
+    def finish(self):
+        total = self.stages[self.k]
+        for index, copy in enumerate(self.flight):
             copy.wait_recv()
-            place = self.at(*kept)
-            place[...] = (place[...].astype(F32) + self.landing(slot)[...].astype(F32)).astype(BF)
-        self.flight = []
-
-
-class AllReduce:
-    def __init__(self, net, stages, landing, steps):
-        self.net, self.stages, self.landing, self.steps, self.flight = net, stages, landing, list(steps), []
-
-    def finish(self):
-        k = len(self.flight)
-        self.flight[-1].wait_recv()
-        self.stages[k] = self.stages[k - 1] + self.landing[k - 1]
-
-    def start(self):
-        k = len(self.flight)
-        axis, mask = self.steps[k]
-        self.flight.append(self.net.send(lambda: self.stages.at[k], lambda: self.landing.at[k], axis, mask))
-
-    def advance(self, k):
-        if 1 <= k <= len(self.steps):
-            self.finish()
-        if k < len(self.steps):
-            self.start()
+            total = total + self.landing[index]
+        self.stages[self.k + 1] = total
 
 
 TABLE_ROWS = 48
@@ -260,11 +259,6 @@
         first=dy_ref.at[pl.ds(half_start, half)],
     )
     dy_half.start()
-    mine_rows = pl.multiple_of(me_t * share, share)
-    far_copies = [
-        net.send(dy_ref.at[pl.ds(mine_rows, share)], far_dy_ref.at[m - 1], "dp", m) for m in range(1, dp_count)
-    ]
-
     length, source, dealt_length = lengths_ref[0, me_d], order_of_ref[0, me_d], 0
     for i in range(dp_count):
         dealt_length = jnp.where(source == i, lengths_ref[0, i], dealt_length)
@@ -318,6 +312,10 @@
     tables_ref[me_e, me_d] = jnp.concatenate([table, source], axis=0).astype(BF)
     mine = tables_ref.at[me_e, me_d]
     table_copies = [net.send(mine, mine, "dp", m) for m in range(1, dp_count)]
+    mine_rows = pl.multiple_of(me_t * share, share)
+    far_copies = [
+        net.send(dy_ref.at[pl.ds(mine_rows, share)], far_dy_ref.at[m - 1], "dp", m) for m in range(1, dp_count)
+    ]
     attn.finish()
     while attn.steps:
         attn.start()
@@ -411,9 +409,9 @@
     grad_in_ref, xown_ref, *rest,
 ):
     if passes:
-        rest = rest[1:]
-        other_ref = rest[7]
-        rest = rest[:7] + rest[8:]
+        out_in_ref, rest = rest[0], rest[1:]
+        out_pass_ref, rest = rest[7], rest[:7] + rest[8:]
+        (out, out_landing), rest = rest[-2:], rest[:-2]
     (
         first_ref, tiny_ref, hidden_grad_ref, scale_ref, dense_ref, out_grad_ref, small_ref,
         grad, grad_landing, normed2, spread, back_ref, picked, send_sem, recv_sem, local_sem,
@@ -430,6 +428,9 @@
     load_x = pltpu.make_async_copy(xown_ref.at[here], normed2, local_sem.at[1])
     load_grad.start()
     load_x.start()
+    if passes:
+        load_out = pltpu.make_async_copy(out_in_ref, out, local_sem.at[2])
+        load_out.start()
     net.barrier(expert_bits + tensor_bits)
     load_grad.wait()
     high_bits = tensor_bits[1:]
@@ -445,11 +446,22 @@
         sums.append(Reduce(
             net, at, lambda i, p=part_index: grad_landing.at[p, i], tensor_bits[:1] + steps, chunks
         ))
+    if passes:
+        out_sum = Reduce(
+            net, lambda re, rt: out.at[flip(me_e, re), flip(me_t, rt)], lambda i: out_landing.at[i],
+            tensor_bits[:1] + expert_bits, chunks,
+        )
     while sums[0].steps:
         for one in sums:
             one.start()
+        if passes and not out_sum.used:
+            load_out.wait()
+            out_sum.start()
         for one in sums:
             one.finish()
+    if passes:
+        out_sum.finish()
+        out_sum.start()
 
     start = pl.multiple_of(me_t * share, share)
     gain2 = gain2_ref[...].astype(F32)[None, :]
@@ -490,15 +502,13 @@
         gather.start()
         gather.finish()
 
-    row_parts = plane_gathers(net, other_ref, share, done=True) if passes else []
-    for one in row_parts:
-        one.start()
     length = lengths_ref[0, me_d]
     inv = HEAD_DIM**-0.5
     live = (sublanes((rows, 1)) < length).astype(F32)
     hidden_grad_all = spread[:, 0:share, :width].reshape(rows, width)
     hidden_grad_ref[...] = hidden_grad_all
     branch = (hidden_grad_all.astype(F32) * live).astype(BF)
+    out_grad_ref[...] = dot(heads_ref[...], branch, 0, 0).astype(BF)
     heads_grad = dot(branch, wo_ref[...], 1, 1).astype(BF)
     cosine, sine = cos_ref[...], -sin_ref[...]
     lane = lanes((rows, 128))
@@ -554,7 +564,6 @@
     tiny_ref[:, 0:rows] = jnp.transpose(jnp.broadcast_to(stat, (rows, 128)))[0:8, :]
     tiny_ref[:, rows:] = jnp.broadcast_to(jnp.sum(along, axis=0, keepdims=True), (8, width))
     dense_ref[...] = dot(normed_ref[...], back, 0, 0).astype(BF)
-    out_grad_ref[...] = dot(heads_ref[...], branch, 0, 0).astype(BF)
     load_x.wait()
     router_rows = dot(spread[:, 0:share, width:].reshape(rows, 128), normed2[...], 0, 0)[0:EXPERTS]
     gain2_sum = jnp.zeros((1, width), F32)
@@ -563,14 +572,15 @@
         gain2_sum = gain2_sum + block[0:1] + block[1:2]
     half = width // 2
     pieces = [router_rows[:, :half], router_rows[:, half:], gain2_sum[:, :half], gain2_sum[:, half:]]
-    for one in row_parts:
-        one.finish()
+    if passes:
+        out_sum.finish()
+        out_pass_ref[...] = out[me_e]
     filled = sum(piece.shape[0] for piece in pieces)
     small_ref[...] = jnp.concatenate(pieces + [jnp.zeros((SMALL_ROWS - filled, half), F32)], axis=0).astype(BF)
     net.close()
 
 
-def back_call(group_count, lengths, vmem_operands, grad, xown, other=None):
+def back_call(group_count, lengths, vmem_operands, grad, xown, out=None):
     dy, x = vmem_operands[0], vmem_operands[1]
     rows, width = x.shape
     wq, wk, wv, wo = vmem_operands[13:17]
@@ -580,17 +590,16 @@
     inner = wq.shape[1] + wk.shape[1] + wv.shape[1]
     shape = jax.ShapeDtypeStruct
     copies = 64
-    passed = [] if other is None else [other]
+    passed = [] if out is None else [out]
     return pl.pallas_call(
-        functools.partial(back_kernel, (group_count, tensor_count, dp_count), other is not None),
+        functools.partial(back_kernel, (group_count, tensor_count, dp_count), out is not None),
         out_shape=(
             shape((tensor_count, rows, columns), BF), shape((8, rows + width), F32), shape((rows, width), BF),
             shape((rows, 128), F32), shape((width, inner), BF), shape(wo.shape, BF), shape((SMALL_ROWS, width // 2), BF),
-            *[shape(one.shape, BF) for one in passed],
+            *[shape(one.shape[1:], BF) for one in passed],
         ),
         in_specs=[pl.BlockSpec(memory_space=pltpu.SMEM)] + vmem(len(vmem_operands)) + [pl.BlockSpec(memory_space=pl.ANY)] * (2 + len(passed)),
-        out_specs=tuple(vmem(7)) + (pl.BlockSpec(memory_space=pl.ANY),) * len(passed),
-        input_output_aliases={len(vmem_operands) + 3: 7} if passed else {},
+        out_specs=tuple(vmem(7)) + tuple(vmem(len(passed))),
         scratch_shapes=[
             pltpu.VMEM(grad.shape, BF),
             pltpu.VMEM((2, chunks - 1, share // 2, width + 128), BF),
@@ -600,8 +609,11 @@
             pltpu.VMEM((EXPERTS, rows), F32),
             pltpu.SemaphoreType.DMA((copies,)),
             pltpu.SemaphoreType.DMA((copies,)),
-            pltpu.SemaphoreType.DMA((2,)),
-        ],
+            pltpu.SemaphoreType.DMA((3,)),
+        ] + ([
+            pltpu.VMEM(out.shape, BF),
+            pltpu.VMEM((chunks, rows, columns), BF),
+        ] if passed else []),
         compiler_params=params(60, collective_id=2, has_side_effects=True),
         cost_estimate=pl.CostEstimate(flops=MIB, bytes_accessed=MIB, transcendentals=0),
         name="back",
@@ -623,7 +635,7 @@
     return expert_bits, tensor_bits, tensor_bits[1:][::-1]
 
 
-def plane_gathers(net, target, share, first=None, done=False):
+def plane_gathers(net, target, share, first=None, done=False, last=None, which=slice(None)):
     counts = lax.axis_size("expert"), lax.axis_size("tensor")
     expert_bits, _, high_bits = bit_steps(*counts)
     size = share // 2
@@ -632,14 +644,14 @@
 
         def at(re, rt, offset=index * size):
             begin = pl.multiple_of(flip(net.me["tensor"], rt) * share + offset, size)
-            return target.at[:, flip(net.me["expert"], re), pl.ds(begin, size)]
+            return target.at[which, flip(net.me["expert"], re), pl.ds(begin, size)]
 
         source = None if first is None else first.at[:, pl.ds(index * size, size)]
         known = [(0, 0)]
         if done:
             axis, mask = steps.pop(0)
             known.append((mask, 0) if axis == "expert" else (0, mask))
-        parts.append(Gather(net, at, steps, known=known, first=source))
+        parts.append(Gather(net, at, steps[:last], known=known, first=source))
     return parts
 
 
@@ -651,14 +663,21 @@
     return Gather(net, whole, [("tensor", 1)], known=known)
 
 
+def slot_numbers(capacity, rows):
+    return sublanes((capacity, rows)).astype(F32).astype(BF)
+
+
+def placed(slot_id, table_row, weight):
+    return jnp.where(slot_id == (table_row - 1.0).astype(BF), weight, jnp.zeros((), BF))
+
+
 def fill_units(table, gate, slot_id, first_expert, count, hits_ref, gated_ref):
     capacity = slot_id.shape[0]
     for j in range(count):
-        rank = table(first_expert + j).astype(jnp.int32) - 1
-        hit = slot_id == rank
+        row = table(first_expert + j)
         cut = slice(j * capacity, (j + 1) * capacity)
-        hits_ref[cut, :] = jnp.where(hit, 1.0, 0.0).astype(BF)
-        gated_ref[cut, :] = jnp.where(hit, gate(first_expert + j), 0.0).astype(BF)
+        hits_ref[cut, :] = placed(slot_id, row, jnp.ones((), BF))
+        gated_ref[cut, :] = placed(slot_id, row, gate(first_expert + j).astype(BF))
 
 
 def middle(both, grad_act, hidden):
@@ -674,8 +693,8 @@
 def own_kernel(
     sizes, groups, capacity, local, batch, gathers,
     x_ref, dy_ref, table_ref, router_ref, wg_ref, wu_ref, wd_ref, hidden_ref, share_ref, far_dy_ref,
-    out_c_ref, out_g_ref, xs_out, ys_out, oth_ref, othy_ref,
-    gates, ranks, hits, gated, xs, ys, made, back, gi_rows, acc_c, acc_g, send_sem, recv_sem, local_sem,
+    out_c_ref, out_g_ref, xs_out, ys_out, oth_ref, othy_ref, gates_out,
+    gates, gates_b, ranks, hits, gated, xs, ys, made, back, gi_rows, acc_c, acc_g, send_sem, recv_sem, local_sem,
 ):
     chunk, pair = pl.program_id(0), pl.program_id(1)
     pairs = local // 2
@@ -686,13 +705,13 @@
     rows, width = x_ref.shape[-2:]
     units = groups
     hidden = wg_ref.shape[2]
-    slot_id = sublanes((capacity, rows))
+    slot_id = slot_numbers(capacity, rows)
     share = rows // tensor_count
 
     if gathers:
         expert_bits, tensor_bits, high_bits = bit_steps(expert_count, tensor_count)
         cotangent_parts = plane_gathers(net, othy_ref, share, first=far_dy_ref)
-        row_parts = plane_gathers(net, oth_ref, share)
+        row_parts = plane_gathers(net, oth_ref, share, last=1)
         mine = pl.ds(pl.multiple_of(me_t * share, share), share)
         keep = pltpu.make_async_copy(far_dy_ref, othy_ref.at[:, me_e, mine], local_sem.at[2])
         flight = []
@@ -719,6 +738,7 @@
             cotangent_parts[-1].start()
             for copy in flight:
                 copy.wait_recv()
+            flight.clear()
             for one in row_parts:
                 one.start()
 
@@ -726,6 +746,8 @@
             cotangent_parts[-1].finish()
             for one in row_parts:
                 one.finish()
+            for copy in flight:
+                copy.wait_recv()
             net.close()
 
         for time, steps in ((0, first_steps), (pairs * 2 // 8, second_steps), (pairs * 6 // 8, third_steps)):
@@ -743,6 +765,15 @@
             table = given_table(table_ref, i, dp_here.astype(F32))
             ranks[i] = table
             gates[i] = gate_rows(router_ref[...], x_ref[i], table)
+            gates_b[i] = gates[i].astype(BF)
+
+    @pl.when(pair == 0)
+    def _():
+        if not gathers:
+            gates_out[...] = gates_b[...]
+            return
+        for m in range(1, dp_count):
+            flight.append(net.send(gates_b, lambda m=m: gates_out.at[m - 1], "dp", m))
 
     place = lax.rem(pair, per_batch)
     half = lax.div(pair, per_batch)
@@ -767,18 +798,17 @@
         for copy in outs:
             copy.start()
 
+    spots = [place * 2 + j for j in range(2)]
+    inner_w = [jnp.concatenate([wg_ref[j], wu_ref[j]], axis=1) for j in range(2)]
+    both = [dot(xs[spots[j]].reshape(units * capacity, width), inner_w[j]) for j in range(2)]
+    grad_act = [dot(ys[spots[j]].reshape(units * capacity, width), wd_ref[j], 1, 1) for j in range(2)]
+    mids = [middle(both[j], grad_act[j], hidden) for j in range(2)]
     for j in range(2):
-        spot = place * 2 + j
-        x_here = xs[spot].reshape(units * capacity, width)
-        y_here = ys[spot].reshape(units * capacity, width)
-        inner_w = jnp.concatenate([wg_ref[j], wu_ref[j]], axis=1)
-        both = dot(x_here, inner_w)
-        grad_act = dot(y_here, wd_ref[j], 1, 1)
-        act, grads = middle(both, grad_act, hidden)
+        act, grads = mids[j]
         result = dot(act.astype(BF), wd_ref[j]).astype(BF)
-        moved = dot(grads, inner_w, 1, 1).astype(BF)
-        inner = jnp.sum(act * grad_act, axis=-1, keepdims=True)
-        at_slot = pl.ds(pl.multiple_of(spot * capacity, capacity), capacity)
+        moved = dot(grads, inner_w[j], 1, 1).astype(BF)
+        inner = jnp.sum(act * grad_act[j], axis=-1, keepdims=True)
+        at_slot = pl.ds(pl.multiple_of(spots[j] * capacity, capacity), capacity)
         for i in range(units):
             cut = slice(i * capacity, (i + 1) * capacity)
             made[i, at_slot, :] = result[cut]
@@ -850,6 +880,7 @@
         out_shape=(
             shape((groups_all, blocks, rows, columns), BF), shape((groups_all, rows, width + 128), BF), slots, slots,
             *[shape((dp_count - 1, groups_all, rows, width) if gathers else (16, 128), BF)] * 2,
+            shape((dp_count - 1, groups_all, EXPERTS, rows) if gathers else (groups_all, EXPERTS, rows), BF),
         ),
         grid=(chunks, pairs),
         in_specs=[
@@ -863,9 +894,11 @@
             pl.BlockSpec((groups, blocks, rows, columns), lambda c, p: (c, 0, 0, 0)),
             pl.BlockSpec((groups, rows, width + 128), lambda c, p: (c, 0, 0)),
             anywhere, anywhere, anywhere, anywhere,
+            anywhere if gathers else pl.BlockSpec((groups, EXPERTS, rows), lambda c, p: (c, 0, 0)),
         ),
         scratch_shapes=[
             pltpu.VMEM((groups, EXPERTS, rows), F32),
+            pltpu.VMEM((groups, EXPERTS, rows), BF),
             pltpu.VMEM((groups, EXPERTS, rows), F32),
             pltpu.VMEM((groups, batch * capacity, rows), BF),
             pltpu.VMEM((groups, batch * capacity, rows), BF),
@@ -889,25 +922,22 @@
     )(x, dy, table, router_t, wg, wu, wd, hidden_share, normed_share, far_dy)
 
 
-def slots_kernel(
-    sizes, masks, capacity, local, batch, reduces, x_hbm, dy_hbm, table_ref, router_ref, *rest,
-):
+def slots_kernel(sizes, masks, capacity, local, batch, reduces, x_hbm, dy_hbm, table_ref, gates_ref, *rest):
     if reduces:
         (
             dense_in, heads_in, small_in, first_in, out_in, old_hbm, x_tok_hbm, stat_in, scale_ref, gain_ref,
             x_hbm, xs_ref, ys_ref, sums_ref, input_ref, block_ref, gain_out_ref,
-            x_buf, y_buf, hits, gated, dense, heads, small, first, out, dense_land, heads_land, small_land, first_land, out_land,
-            stat, stat_land, gains, gains_land, old, x_tok, load_sem, send_sem, recv_sem, local_sem,
+            buf, onehot, ranks, weights, dense, heads, small, first, out, dense_land, heads_land, small_land, first_land, out_land,
+            stat, stat_land, gains, gains_land, gains_far_land, old, x_tok, load_sem, send_sem, recv_sem, local_sem,
         ) = rest
     else:
-        xs_ref, ys_ref, x_buf, y_buf, hits, gated, load_sem = rest
+        xs_ref, ys_ref, buf, onehot, ranks, weights, load_sem = rest
     expert_count, tensor_count, dp_count = sizes
-    unit = pl.program_id(0)
-    units = pl.num_programs(0)
-    rows, width = x_buf.shape[-2:]
+    step = pl.program_id(0)
+    units = expert_count * len(masks)
+    rows, width = buf.shape[-2:]
     me_e, me_d = lax.axis_index("expert"), lax.axis_index("dp")
-    per_mask = expert_count
-    slot_id = sublanes((capacity, rows))
+    slot_id = slot_numbers(capacity, rows)
 
     def far_dp(m):
         value = me_d
@@ -917,29 +947,32 @@
         return value
 
     def place(i):
-        m = masks[0] + lax.div(i, per_mask)
-        return m, lax.rem(i, per_mask), far_dp(m)
-
-    def loads(i):
-        m, group, d = place(i)
-        slot = lax.rem(i, 2)
-        y_source = dy_hbm.at[m - masks[0], group] if len(dy_hbm.shape) == 4 else dy_hbm.at[group]
-        x_source = x_hbm.at[m - masks[0], group] if len(x_hbm.shape) == 4 else x_hbm.at[group]
-        return (
-            pltpu.make_async_copy(x_source, x_buf.at[slot], load_sem.at[slot, 0]),
-            pltpu.make_async_copy(y_source, y_buf.at[slot], load_sem.at[slot, 1]),
-        )
+        m = masks[0] + lax.div(i, expert_count)
+        return m, lax.rem(i, expert_count), far_dp(m)
+
+    def load(source, i, slot):
+        m, group, _ = place(i)
+        return pltpu.make_async_copy(source.at[m - masks[0], group], buf.at[slot], load_sem.at[slot])
+
+    def start_load(s):
+        @pl.when(s < units)
+        def _():
+            load(dy_hbm, s, lax.rem(s, 2)).start()
+
+        @pl.when(s >= units)
+        def _():
+            load(x_hbm, s - units, lax.rem(s, 2)).start()
 
     if reduces:
         net = Net(send_sem, recv_sem)
         me_t = net.me["tensor"]
         ways = expert_count * dp_count
-        expert_bits = [("expert", b) for b in bits_of(expert_count)]
-        tensor_bits = [("tensor", b) for b in bits_of(tensor_count)]
+        expert_bits, tensor_bits, high_bits = bit_steps(expert_count, tensor_count)
         dp_bits = [("dp", b) for b in bits_of(dp_count)][::-1]
         chunks = [(e, d) for e in range(expert_count) for d in range(dp_count)]
         plane = [(e, t) for e in range(expert_count) for t in range(0, tensor_count, 2)]
         share = rows // tensor_count
+        planes = [plane_gathers(net, x_hbm, share, done=True, which=m) for m in range(dp_count - 1)]
         cores = [core_gather(net, x_hbm, share, plane, which) for which in range(dp_count - 1)]
 
         def chunk_of(ref):
@@ -951,105 +984,127 @@
 
             return at
 
-        sums = [
-            Reduce(net, chunk_of(dense), lambda i: dense_land.at[i], expert_bits + dp_bits, chunks),
-            Reduce(net, chunk_of(heads), lambda i: heads_land.at[i], dp_bits + expert_bits, chunks),
-            Reduce(net, chunk_of(small), lambda i: small_land.at[i], dp_bits + expert_bits, chunks),
-            Reduce(
-                net, lambda re, rt: out.at[flip(me_e, re), flip(me_t, rt)], lambda i: out_land.at[i],
-                tensor_bits + expert_bits, [(e, t) for e in range(expert_count) for t in range(tensor_count)],
-            ),
-            Reduce(
-                net, lambda re, rt: first.at[flip(me_t, rt)], lambda i: first_land.at[i], tensor_bits,
-                [(0, t) for t in range(tensor_count)],
-            ),
+        def column_of(ref):
+            return lambda re, rt: ref.at[flip(me_t, rt)]
+
+        dense_sum = Reduce(net, chunk_of(dense), lambda i: dense_land.at[i], [("dp", 0)] + expert_bits, chunks)
+        small_sum = Reduce(net, chunk_of(small), lambda i: small_land.at[i], [("dp", 0)] + expert_bits, chunks)
+        heads_sum = Reduce(net, chunk_of(heads), lambda i: heads_land.at[i], expert_bits + [("dp", 0)], chunks)
+        out_sum = Reduce(net, column_of(out), lambda i: out_land.at[i], high_bits, [(0, t) for t in range(0, tensor_count, 2)])
+        first_sum = Reduce(net, column_of(first), lambda i: first_land.at[i], tensor_bits, [(0, t) for t in range(tensor_count)])
+        last = 2 * units
+        plan = [
+            (dense_sum, [0, units + 2]), (small_sum, [0, units + 2]),
+            (heads_sum, [2, units + 2]), (first_sum, [0, units - 1]), (out_sum, [units - 1]),
         ]
-        chains = [
-            AllReduce(net, stat, stat_land, tensor_bits),
-            AllReduce(net, gains, gains_land, tensor_bits + expert_bits + dp_bits),
-        ]
+        near = [("tensor", m) for m in range(1, tensor_count)]
+        far = [(("expert", e), ("dp", d)) for e, d in chunks if e or d]
+        stat_sum = Exchange(net, stat, 0, stat_land, near)
+        gains_near = Exchange(net, gains, 0, gains_land, near)
+        gains_far = Exchange(net, gains, 1, gains_far_land, far)
         columns = first.shape[2]
         begin = pl.multiple_of(me_t * columns, columns)
 
-        count = len(masks) * expert_count
-        times = [[0, 2, 4], [0, 2, 4], [0, 2, 4], [0, 2, 4], [0, 1]]
-
         def advance(k):
-            for one, when in zip(sums, times):
-                if k in when or k == count:
+            for one, when in plan:
+                if k in when or k == last:
                     if one.flight:
                         one.finish()
                     if one.steps:
                         one.start()
 
-        @pl.when(unit == 0)
-        def _():
+        def moves():
             pairs = (
-                (dense_in, dense), (heads_in, heads), (small_in, small), (first_in, first), (out_in, out),
                 (stat_in.at[:, 0:rows], stat.at[0]), (stat_in.at[:, rows:], gains.at[0]),
+                (dense_in, dense), (small_in, small), (first_in, first),
+                (heads_in, heads), (out_in, out),
                 (old_hbm.at[:, pl.ds(begin, columns)], old), (x_tok_hbm.at[:, pl.ds(begin, columns)], x_tok),
             )
-            moves = [pltpu.make_async_copy(a, b, local_sem.at[i]) for i, (a, b) in enumerate(pairs)]
-            for copy in moves:
+            return [pltpu.make_async_copy(a, b, local_sem.at[i]) for i, (a, b) in enumerate(pairs)]
+
+        @pl.when(step == 0)
+        def _():
+            for copy in moves():
                 copy.start()
-            net.barrier(expert_bits + tensor_bits + dp_bits)
-            for one in cores:
-                one.start()
-            for copy in moves:
+            net.barrier(near + far)
+            for copy in moves()[:2]:
+                copy.wait()
+            stat_sum.start()
+            gains_near.start()
+            for parts in planes:
+                for one in parts:
+                    one.start()
+            for copy in moves()[2:5]:
                 copy.wait()
             advance(0)
-            for chain in chains:
-                chain.advance(0)
-
-        for k in range(1, len(chains[1].steps)):
-
-            @pl.when(unit == k)
-            def _(k=k):
+
+        for k in range(1, last):
+            at_plane = [m for m in range(dp_count - 1) if k == max(units - 4 + m * expert_count, 1)]
+            at_core = [m for m in range(dp_count - 1) if k == units - 1 + m * expert_count]
+            if not (k <= 2 or at_plane or at_core or any(k in when for _, when in plan)):
+                continue
+
+            @pl.when(step == k)
+            def _(k=k, at_plane=at_plane, at_core=at_core):
+                if k == 1:
+                    for copy in moves()[5:]:
+                        copy.wait()
+                for m in at_plane:
+                    for one in planes[m]:
+                        one.finish()
+                    cores[m].start()
                 advance(k)
-                for chain in chains:
-                    chain.advance(k)
-
-        for m in range(dp_count - 1):
-
-            @pl.when(unit == max(m * expert_count - 1, 0))
-            def _(m=m):
-                cores[m].finish()
-
-    @pl.when(unit == 0)
+                if k == 2:
+                    stat_sum.finish()
+                    gains_near.finish()
+                    gains_far.start()
+                for m in at_core:
+                    cores[m].finish()
+
+    @pl.when(step == 0)
     def _():
-        for copy in loads(unit):
-            copy.start()
-
-    @pl.when(unit + 1 < units)
+        start_load(step)
+
+    @pl.when(step + 1 < 2 * units)
     def _():
-        for copy in loads(unit + 1):
-            copy.start()
-
-    for copy in loads(unit):
-        copy.wait()
-    slot = lax.rem(unit, 2)
-    _, group, d = place(unit)
-    table = given_table(table_ref, group, d.astype(F32))
-    gates = gate_rows(router_ref[...], x_buf[slot], table)
-    router_rows = sublanes((EXPERTS, rows))
-
-    def row_of(values):
-        return lambda e: jnp.sum(jnp.where(router_rows == e, values, 0.0), axis=0, keepdims=True)
-
-    for part in range(local // batch):
-        fill_units(
-            row_of(table), row_of(gates), slot_id, me_e * local + part * batch, batch, hits.at[part], gated.at[part]
-        )
-        cut = slice(part * batch, (part + 1) * batch)
-        xs_ref[cut, 0] = dot(hits[part], x_buf[slot]).astype(BF).reshape(batch, capacity, width)
-        ys_ref[cut, 0] = dot(gated[part], y_buf[slot]).astype(BF).reshape(batch, capacity, width)
+        start_load(step + 1)
+
+    slot = lax.rem(step, 2)
+
+    def spread(unit, source, target_ref, gated):
+        m, group, d = place(unit)
+        ranks[...] = given_table(table_ref, group, d.astype(F32))
+        if gated:
+            weights[...] = gates_ref[m - masks[0], group].astype(F32)
+        for part in range(local // batch):
+            for j in range(batch):
+                e = me_e * local + part * batch + j
+                weight = weights[pl.ds(e, 1), :].astype(BF) if gated else jnp.ones((), BF)
+                onehot[part, j * capacity : (j + 1) * capacity, :] = placed(slot_id, ranks[pl.ds(e, 1), :], weight)
+        load(source, unit, slot).wait()
+        for part in range(local // batch):
+            moved = dot(onehot[part], buf[slot]).astype(BF)
+            target_ref[part * batch : (part + 1) * batch, 0] = moved.reshape(batch, capacity, width)
+
+    @pl.when(step < units)
+    def _():
+        spread(step, dy_hbm, ys_ref, True)
+
+    @pl.when(step >= units)
+    def _():
+        spread(step - units, x_hbm, xs_ref, False)
 
     if reduces:
 
-        @pl.when(unit == units - 1)
+        @pl.when(step == last - 1)
         def _():
-            advance(count)
-            chains[1].advance(len(chains[1].steps))
+            for one, _ in plan:
+                while one.flight or one.steps:
+                    if one.flight:
+                        one.finish()
+                    if one.steps:
+                        one.start()
+            gains_far.finish()
             here = me_e * dp_count + me_d
             d_rows, h_rows, s_rows = (ref.shape[0] // ways for ref in (dense, heads, small))
             half = heads.shape[1] // 2
@@ -1068,11 +1123,11 @@
                     - x_tok[...].astype(F32) * scale * mean
                 )
             ).astype(BF)
-            block_ref[...] = out[me_e, me_t]
+            block_ref[...] = out[me_t]
             net.close()
 
 
-def slots_call(masks, x, dy, table, router_t, local, sums=None):
+def slots_call(masks, x, dy, table, gates, local, sums=None):
     sizes = tuple(lax.axis_size(axis) for axis in ("expert", "tensor", "dp"))
     expert_count, _, dp_count = sizes
     rows, width = x.shape[-2:]
@@ -1081,18 +1136,19 @@
     batch = min(8, local)
     shape = jax.ShapeDtypeStruct
     anywhere = pl.BlockSpec(memory_space=pl.ANY)
-    block = pl.BlockSpec((local, 1, capacity, width), lambda i: (0, i, 0, 0))
+    y_block = pl.BlockSpec((local, 1, capacity, width), lambda i: (0, jnp.minimum(i, units - 1), 0, 0))
+    x_block = pl.BlockSpec((local, 1, capacity, width), lambda i: (0, jnp.maximum(i - units, 0), 0, 0))
     whole = pl.BlockSpec(memory_space=pltpu.VMEM)
     out_shape = [shape((local, units, capacity, width), BF)] * 2
-    out_specs = [block, block]
+    out_specs = [x_block, y_block]
     aliases = {}
-    operands = [x, dy, table, router_t]
+    operands = [x, dy, table, gates]
     in_specs = [anywhere, anywhere, whole, whole]
     scratch = [
-        pltpu.VMEM((2, rows, width), BF), pltpu.VMEM((2, rows, width), BF),
-        pltpu.VMEM((local // batch, batch * capacity, rows), BF), pltpu.VMEM((local // batch, batch * capacity, rows), BF),
+        pltpu.VMEM((2, rows, width), BF), pltpu.VMEM((local // batch, batch * capacity, rows), BF),
+        pltpu.VMEM((EXPERTS, rows), F32), pltpu.VMEM((EXPERTS, rows), F32),
     ]
-    tail = [pltpu.SemaphoreType.DMA((2, 2))]
+    tail = [pltpu.SemaphoreType.DMA((2,))]
     more = {}
     if sums is not None:
         dense, heads, small, first, out, old, tokens, stat, scale, gain = sums
@@ -1109,23 +1165,21 @@
         out_shape = [shape(x.shape, BF)] + out_shape
         out_specs = [anywhere] + out_specs
         aliases = {0: 0}
-        steps = len(bits_of(sizes[1]))
-        rounds = steps + len(bits_of(ways))
         scratch += [pltpu.VMEM(values.shape, BF) for values in (dense, heads, small, first, out)]
         scratch += [
             pltpu.VMEM((ways - 1, chunk[0], dense.shape[1]), BF), pltpu.VMEM((ways - 1, chunk[1], heads.shape[1]), BF),
             pltpu.VMEM((ways - 1, chunk[2], small.shape[1]), BF), pltpu.VMEM((first.shape[0] - 1, rows, columns), BF),
-            pltpu.VMEM((expert_count * sizes[1] - 1, rows, columns), BF),
-            pltpu.VMEM((steps + 1, 8, rows), F32), pltpu.VMEM((steps, 8, rows), F32),
-            pltpu.VMEM((rounds + 1, 8, width), F32), pltpu.VMEM((rounds, 8, width), F32),
+            pltpu.VMEM((max(sizes[1] // 2 - 1, 1), rows, columns), BF),
+            pltpu.VMEM((2, 8, rows), F32), pltpu.VMEM((sizes[1] - 1, 8, rows), F32),
+            pltpu.VMEM((3, 8, width), F32), pltpu.VMEM((sizes[1] - 1, 8, width), F32), pltpu.VMEM((ways - 1, 8, width), F32),
             pltpu.VMEM((rows, columns), BF), pltpu.VMEM((rows, columns), BF),
         ]
-        tail += [pltpu.SemaphoreType.DMA((64,)), pltpu.SemaphoreType.DMA((64,)), pltpu.SemaphoreType.DMA((9,))]
+        tail += [pltpu.SemaphoreType.DMA((96,)), pltpu.SemaphoreType.DMA((96,)), pltpu.SemaphoreType.DMA((9,))]
         more = dict(collective_id=4, has_side_effects=True)
     return pl.pallas_call(
         functools.partial(slots_kernel, sizes, masks, capacity, local, batch, sums is not None),
         out_shape=tuple(out_shape),
-        grid=(units,),
+        grid=(2 * units,),
         in_specs=in_specs,
         out_specs=tuple(out_specs),
         input_output_aliases=aliases,
@@ -1154,7 +1208,8 @@
             take = count // chunks
             for which, (refs, buf) in enumerate(((xs_refs, x_buf), (ys_refs, y_buf))):
                 copies.append(pltpu.make_async_copy(
-                    refs[index].at[e, pl.ds(c * take, take)], buf.at[slot, pl.ds(start, take)], sem.at[slot, index, which]
+                    refs[index].at[pl.ds(2 * e, 2), pl.ds(c * take, take)], buf.at[slot, :, pl.ds(start, take)],
+                    sem.at[slot, index, which],
                 ))
             start += take
         return copies
@@ -1173,30 +1228,31 @@
         copy.wait()
     slot = lax.rem(step, 2)
     width, hidden = wg_ref.shape[1:]
-    x_here = x_buf[slot].reshape(-1, width)
-    y_here = y_buf[slot].reshape(-1, width)
-    both = dot(x_here, jnp.concatenate([wg_ref[0], wu_ref[0]], axis=1))
-    grad_act = dot(y_here, wd_ref[0], 1, 1)
-    act, grads = middle(both, grad_act, hidden)
-    inner = dot(x_here, grads, 0, 0)
-    down = dot(act.astype(BF), y_here, 0, 0)
-
-    def put(ref, values, partial):
+    x_here = [x_buf[slot, j].reshape(-1, width) for j in range(2)]
+    y_here = [y_buf[slot, j].reshape(-1, width) for j in range(2)]
+    both = [dot(x_here[j], jnp.concatenate([wg_ref[j], wu_ref[j]], axis=1)) for j in range(2)]
+    grad_act = [dot(y_here[j], wd_ref[j], 1, 1) for j in range(2)]
+    mids = [middle(both[j], grad_act[j], hidden) for j in range(2)]
+
+    def put(j, ref, values, partial):
         if chunks == 1:
-            ref[0] = values + partial[0] if has_partial else values
+            ref[j] = values + partial[j] if has_partial else values
             return
 
         @pl.when(chunk == 0)
         def _():
-            ref[0] = values + partial[0] if has_partial else values
+            ref[j] = values + partial[j] if has_partial else values
 
         @pl.when(chunk != 0)
         def _():
-            ref[0] += values
-
-    put(gg_ref, inner[:, :hidden], in_g if has_partial else None)
-    put(gu_ref, inner[:, hidden:], in_u if has_partial else None)
-    put(gd_ref, down, in_d if has_partial else None)
+            ref[j] += values
+
+    for j in range(2):
+        act, grads = mids[j]
+        inner = dot(x_here[j], grads, 0, 0)
+        put(j, gg_ref, inner[:, :hidden], in_g if has_partial else None)
+        put(j, gu_ref, inner[:, hidden:], in_u if has_partial else None)
+        put(j, gd_ref, dot(act.astype(BF), y_here[j], 0, 0), in_d if has_partial else None)
 
 
 def weights_call(slots, wg, wu, wd, partial=None):
@@ -1206,15 +1262,15 @@
     chunks = max(1, sum(counts) // 8)
     assert len(counts) == 1 or chunks == 1
     shape = jax.ShapeDtypeStruct
-    in_block = pl.BlockSpec((1, width, hidden), lambda e, c: (e, 0, 0))
-    down_block = pl.BlockSpec((1, hidden, width), lambda e, c: (e, 0, 0))
+    in_block = pl.BlockSpec((2, width, hidden), lambda e, c: (e, 0, 0))
+    down_block = pl.BlockSpec((2, hidden, width), lambda e, c: (e, 0, 0))
     specs = (in_block, in_block, down_block)
     more = list(partial) if partial is not None else []
-    buffer = pltpu.VMEM((2, sum(counts) // chunks, capacity, width), BF)
+    buffer = pltpu.VMEM((2, 2, sum(counts) // chunks, capacity, width), BF)
     return pl.pallas_call(
         functools.partial(weights_kernel, counts, chunks, capacity, partial is not None),
         out_shape=(shape(wg.shape, F32), shape(wu.shape, F32), shape(wd.shape, F32)),
-        grid=(local, chunks),
+        grid=(local // 2, chunks),
         in_specs=list(specs) + [pl.BlockSpec(memory_space=pl.ANY)] * (2 * len(slots)) + (list(specs) if more else []),
         out_specs=specs,
         scratch_shapes=[buffer, buffer, pltpu.SemaphoreType.DMA((2, len(counts), 2))],
@@ -1291,7 +1347,7 @@
         return jnp.where(never, other.astype(values.dtype), values)
 
     small_mesh = expert_count == 2
-    out_c, out_g, xs_own, ys_own, x_other, dy_other = own_call(
+    out_c, out_g, xs_own, ys_own, x_other, dy_other, gates = own_call(
         x_own, dy_own, tables, router_t, w_gate, w_up, w_down, hidden, normed_share, far_dy
     )
     group_count = expert_count
@@ -1300,19 +1356,19 @@
         out_g = lax.psum_scatter(out_g, "expert", scatter_dimension=0, tiled=True)
         x_own = lax.dynamic_slice_in_dim(x_own, expert_index, 1, 0)
         group_count = 1
-    first, stat, hidden_grad, scale, dense, heads_grad, small, *x_passed = back_call(
+    first, stat, hidden_grad, scale, dense, heads_grad, small, *out_passed = back_call(
         group_count, seq_lengths,
         (cotangent, tokens, gain1, gain2, router_t, hidden, tables, normed, q, k, v, heads, logsum,
          w_query, w_key, w_value, w_out, cosine, sine),
-        out_g, x_own, x_other if small_mesh else None,
+        out_g, x_own, *((out_c,) if small_mesh else ()),
     )
     local = w_gate.shape[0]
     q_width, k_width = w_query.shape[1], w_key.shape[1]
     half, columns = width // 2, width // tensor_count
     if small_mesh:
         _, xs, ys, sums, input_grad, block_out, gain1_rows = slots_call(
-            tuple(range(1, dp_count)), x_passed[0], dy_other, tables, router_t, local,
-            (dense, heads_grad, small, first, out_c, hidden_grad, tokens, stat, scale, gain1),
+            tuple(range(1, dp_count)), x_other, dy_other, tables, gates, local,
+            (dense, heads_grad, small, first, out_passed[0], hidden_grad, tokens, stat, scale, gain1),
         )
         gain1_sum = gain1_rows[0]
         ways = expert_count * dp_count
@@ -1326,13 +1382,14 @@
             moved = (
                 lax.all_gather(
                     after(values[mask - 1], grads[2][0, 0, 0]), ("expert", "tensor"), axis=0, tiled=True
-                ).reshape(expert_count, rows, width)
+                ).reshape(1, expert_count, rows, width)
                 for values in (
                     [lax.ppermute(normed_share, "dp", [(i, i ^ m) for i in range(dp_count)]) for m in range(1, dp_count)],
                     far_dy,
                 )
             )
-            xs, ys = slots_call((mask,), *moved, tables, router_t, local)
+            far_gates = lax.ppermute(gates, "dp", [(i, i ^ mask) for i in range(dp_count)])[None]
+            xs, ys = slots_call((mask,), *moved, tables, far_gates, local)
             grads = weights_call([(xs, ys)], w_gate, w_up, w_down, grads)
         gate_grad, up_grad, down_grad = grads
         dense_sum, out_sum, small_sum = (

time: 273 us -> 251 us (0.919)
  Pallas kernels: 254 us -> 232 us
    pallas_call x1, Pallas kernels: 53.8 us -> 42.1 us  [back_call(): pl.pallas_call(functools.partial(back_kernel, (group_count, tensor_count,...]
    pallas_call x1, Pallas kernels: 51.3 us -> 44 us  [front(): pl.pallas_call(functools.partial(front_kernel, sizes), out_shape=(shape((...]
    pallas_call x1, Pallas kernels: 49.2 us -> 42.8 us  [weights_call(): pl.pallas_call(functools.partial(weights_kernel, counts, chunks, capacity...]
    pallas_call x1, Pallas kernels: 49.2 us -> 53.9 us  [slots_call(): pl.pallas_call(functools.partial(slots_kernel, sizes, masks, capacity, lo...]
  transfers between devices with their start and end apart: 1 -> 1, of which waited for: 0 -> 0; matrix products, arithmetic and copies ran while one was open for 0% -> 1% of each run, Pallas kernels for 18% -> 17%
where the time goes in v4:
time: 251 us
  Pallas kernels  232 us (92%)
  between operations  14.1 us (6%)
  local copies, waits for them, and re-layouts  4.81 us (2%)
    pallas_call x1, Pallas kernels, slots_call(): pl.pallas_call(functools.partial(slots_kernel, sizes, masks, capacity, lo...  53.9 us
    pallas_call x1, Pallas kernels, own_call(): pl.pallas_call(functools.partial(own_kernel, sizes, groups, capacity, loc...  47.1 us
    pallas_call x1, Pallas kernels, front(): pl.pallas_call(functools.partial(front_kernel, sizes), out_shape=(shape((...  44 us
    pallas_call x1, Pallas kernels, weights_call(): pl.pallas_call(functools.partial(weights_kernel, counts, chunks, capacity...  42.8 us
    pallas_call x1, Pallas kernels, back_call(): pl.pallas_call(functools.partial(back_kernel, (group_count, tensor_count,...  42.1 us
  transfers between devices with their start and end apart: 1, of which 0 were waited for; matrix products, arithmetic and copies ran while one was open for 1% of the time, Pallas kernels for 17%

profile of v4, /device:TPU:0, one launch (start us, length us, event | category | flops | bytes accessed | tf_op | source)
XLA Modules:
  0.0 250.8 jit_solution(8728136696517476460)
XLA Ops:
  7.2 0.0 all-gather.3.cloned.1.call-start
  7.2 44.0 %front.1 = (bf16[512,1024]{1,0:T(8,128)(2,1)}, bf16[512,256]{1,0:T(8,128)(2,1)}, bf16[512,128]{1,0:T(8,128)(2,1)}, bf16[512,128]{1,0:T(8,128)(2,1)}, bf16[512,25...) custom-call(s32[1,4]{1,0:T(1,128)} %lengths_ref.3, ...), custom_call_target="tpu_custom_call" | custom-call | flops 1048576 | bytes 1048576 | tf_op jit(solution)/shard_map/front/pallas_call | solution.py:382
  51.3 47.1 %experts_own.1 = (bf16[2,4,512,256]{3,2,1,0:T(8,128)(2,1)}, bf16[2,512,1152]{2,1,0:T(8,128)(2,1)}, bf16[16,2,128,1024]{3,2,1,0:T(8,128)(2,1)}, bf16[16,2,128,102...) custom-call(bf16[2,512,1024]{2,1,0:T(8,128)(2,1)} %get-tuple-element, ...), custom_call_target="tpu_custom_call" | custom-call | flops 1048576 | bytes 1048576 | tf_op jit(solution)/shard_map/experts_own/pallas_call | solution.py:878
  98.4 42.1 %back.1 = (bf16[4,512,256]{2,1,0:T(8,128)(2,1)}, f32[8,1536]{1,0:T(8,128)}, bf16[512,1024]{1,0:T(8,128)(2,1)}, f32[512,128]{1,0:T(8,128)}, bf16[1024,512]{1,0:T(...) custom-call(s32[1,4]{1,0:T(1,128)} %lengths_ref.3, ...), custom_call_target="tpu_custom_call" | custom-call | flops 1048576 | bytes 1048576 | tf_op jit(solution)/shard_map/back/pallas_call | solution.py:594
  140.5 53.9 %slots.1 = (bf16[3,2,512,1024]{3,2,1,0:T(8,128)(2,1)}, bf16[16,6,128,1024]{3,2,1,0:T(8,128)(2,1)}, bf16[16,6,128,1024]{3,2,1,0:T(8,128)(2,1)}, bf16[208,512]{1,0...) custom-call(bf16[3,2,512,1024]{3,2,1,0:T(8,128)(2,1)} %get-tuple-ele, ...), custom_call_target="tpu_custom_call", output_to_operand_aliasing={{0}: (0, {})} | custom-call | flops 1048576 | bytes 1048576 | tf_op jit(solution)/shard_map/slots/pallas_call | solution.py:1179
  194.4 0.0 all-gather.3.cloned.1.call-update
  194.4 0.0 copy-start.2
  194.5 0.0 copy-start.1
  194.5 42.8 %weights.1 = (f32[16,1024,128]{2,1,0:T(8,128)}, f32[16,1024,128]{2,1,0:T(8,128)}, f32[16,128,1024]{2,1,0:T(8,128)}) custom-call(bf16[16,1024,128]{2,1,0:T(8,128)(2,1)} %wg_ref.3, bf16[16,1024,128]{2,1,0:T(8,128)(2,1)} %wu_ref.3, bf16[16,128,1024]{2,1,0:T(8,128)(2,1)} %wd_ref.3, bf16[16,2,128,1024]{3,2,1,0:T(8,128)(2,1)} %get-tuple-element.89.rest_0_, ...), custom_call_target="tpu_custom_call" | custom-call | flops 80000000000 | bytes 104857600 | tf_op jit(solution)/shard_map/weights/pallas_call | solution.py:1270
  237.3 1.4 slice.3
  238.7 0.0 all-gather.3.cloned.1.call-done
  238.7 0.0 copy-start
  238.7 1.5 copy-done
  240.1 1.8 unpack.1
  241.9 0.6 copy.31
  242.5 0.0 copy-done.2
  242.5 0.7 copy.35
  243.2 0.0 copy-done.1
  243.2 0.7 copy.36
Async XLA Ops:
  7.2 231.5 %all-gather.3.cloned.1.call-start = ((), (), s32[]{:S(2)}) async-start(), calls=%async_computation | async-start | bytes 1916928 | tf_op jit(solution)/shard_map/all_gather | solution.py:1375
  194.4 48.1 %copy-start.2 = (bf16[512,256]{1,0:T(8,128)(2,1)S(1)}, bf16[512,256]{1,0:T(8,128)(2,1)}, u32[]{:S(2)}) copy-start(bf16[512,256]{1,0:T(8,128)(2,1)} %get-tuple-element.108) | copy-start | bytes 786436
  194.5 48.8 %copy-start.1 = (bf16[512,256]{1,0:T(8,128)(2,1)S(1)}, bf16[512,256]{1,0:T(8,128)(2,1)}, u32[]{:S(2)}) copy-start(bf16[512,256]{1,0:T(8,128)(2,1)} %get-tuple-element.109) | copy-start | bytes 786436
  238.7 1.5 copy-start
Sparse Core Ops, SparseCore 0:
  194.6 43.5 all-gather.2

commit v5 on v4

--- a/solution.py
+++ b/solution.py
@@ -408,6 +408,12 @@
     normed_ref, q_ref, k_ref, v_ref, heads_ref, logsum_ref, wq_ref, wk_ref, wv_ref, wo_ref, cos_ref, sin_ref,
     grad_in_ref, xown_ref, *rest,
 ):
+    late_count = 13
+    late_sem, rest = rest[-1], rest[:-1]
+    late_refs, rest = rest[-late_count:], rest[:-late_count]
+    late_hbm = (
+        x_ref, normed_ref, q_ref, k_ref, v_ref, heads_ref, logsum_ref, wq_ref, wk_ref, wv_ref, wo_ref, cos_ref, sin_ref,
+    )
     if passes:
         out_in_ref, rest = rest[0], rest[1:]
         out_pass_ref, rest = rest[7], rest[:7] + rest[8:]
@@ -428,11 +434,14 @@
     load_x = pltpu.make_async_copy(xown_ref.at[here], normed2, local_sem.at[1])
     load_grad.start()
     load_x.start()
+    late = [pltpu.make_async_copy(a, b, late_sem.at[i]) for i, (a, b) in enumerate(zip(late_hbm, late_refs))]
     if passes:
         load_out = pltpu.make_async_copy(out_in_ref, out, local_sem.at[2])
         load_out.start()
     net.barrier(expert_bits + tensor_bits)
     load_grad.wait()
+    for copy in late:
+        copy.start()
     high_bits = tensor_bits[1:]
     chunks = [(e, t) for e in range(group_count) for t in range(tensor_count)]
     sums = []
@@ -502,11 +511,18 @@
         gather.start()
         gather.finish()
 
+    for copy in late:
+        copy.wait()
+    (
+        x_ref, normed_ref, q_ref, k_ref, v_ref, heads_ref, logsum_ref, wq_ref, wk_ref, wv_ref, wo_ref, cos_ref, sin_ref,
+    ) = late_refs
     length = lengths_ref[0, me_d]
     inv = HEAD_DIM**-0.5
     live = (sublanes((rows, 1)) < length).astype(F32)
     hidden_grad_all = spread[:, 0:share, :width].reshape(rows, width)
-    hidden_grad_ref[...] = hidden_grad_all
+    columns = width // tensor_count
+    cut = pl.ds(pl.multiple_of(me_t * columns, columns), columns)
+    hidden_grad_ref[...] = jnp.concatenate([spread[t, 0:share, cut] for t in range(tensor_count)], axis=0)
     branch = (hidden_grad_all.astype(F32) * live).astype(BF)
     out_grad_ref[...] = dot(heads_ref[...], branch, 0, 0).astype(BF)
     heads_grad = dot(branch, wo_ref[...], 1, 1).astype(BF)
@@ -591,14 +607,17 @@
     shape = jax.ShapeDtypeStruct
     copies = 64
     passed = [] if out is None else [out]
+    late = [1] + list(range(7, len(vmem_operands)))
     return pl.pallas_call(
         functools.partial(back_kernel, (group_count, tensor_count, dp_count), out is not None),
         out_shape=(
-            shape((tensor_count, rows, columns), BF), shape((8, rows + width), F32), shape((rows, width), BF),
+            shape((tensor_count, rows, columns), BF), shape((8, rows + width), F32), shape((rows, columns), BF),
             shape((rows, 128), F32), shape((width, inner), BF), shape(wo.shape, BF), shape((SMALL_ROWS, width // 2), BF),
             *[shape(one.shape[1:], BF) for one in passed],
         ),
-        in_specs=[pl.BlockSpec(memory_space=pltpu.SMEM)] + vmem(len(vmem_operands)) + [pl.BlockSpec(memory_space=pl.ANY)] * (2 + len(passed)),
+        in_specs=[pl.BlockSpec(memory_space=pltpu.SMEM)] + [
+            pl.BlockSpec(memory_space=pl.ANY if i in late else pltpu.VMEM) for i in range(len(vmem_operands))
+        ] + [pl.BlockSpec(memory_space=pl.ANY)] * (2 + len(passed)),
         out_specs=tuple(vmem(7)) + tuple(vmem(len(passed))),
         scratch_shapes=[
             pltpu.VMEM(grad.shape, BF),
@@ -613,7 +632,9 @@
         ] + ([
             pltpu.VMEM(out.shape, BF),
             pltpu.VMEM((chunks, rows, columns), BF),
-        ] if passed else []),
+        ] if passed else []) + [pltpu.VMEM(vmem_operands[i].shape, vmem_operands[i].dtype) for i in late] + [
+            pltpu.SemaphoreType.DMA((len(late),))
+        ],
         compiler_params=params(60, collective_id=2, has_side_effects=True),
         cost_estimate=pl.CostEstimate(flops=MIB, bytes_accessed=MIB, transcendentals=0),
         name="back",
@@ -994,8 +1015,8 @@
         first_sum = Reduce(net, column_of(first), lambda i: first_land.at[i], tensor_bits, [(0, t) for t in range(tensor_count)])
         last = 2 * units
         plan = [
-            (dense_sum, [0, units + 2]), (small_sum, [0, units + 2]),
-            (heads_sum, [2, units + 2]), (first_sum, [0, units - 1]), (out_sum, [units - 1]),
+            (dense_sum, [0, units + 4]), (small_sum, [0, units + 4]),
+            (heads_sum, [4, units + 4]), (first_sum, [0, units]), (out_sum, [units]),
         ]
         near = [("tensor", m) for m in range(1, tensor_count)]
         far = [(("expert", e), ("dp", d)) for e, d in chunks if e or d]
@@ -1018,7 +1039,7 @@
                 (stat_in.at[:, 0:rows], stat.at[0]), (stat_in.at[:, rows:], gains.at[0]),
                 (dense_in, dense), (small_in, small), (first_in, first),
                 (heads_in, heads), (out_in, out),
-                (old_hbm.at[:, pl.ds(begin, columns)], old), (x_tok_hbm.at[:, pl.ds(begin, columns)], x_tok),
+                (old_hbm, old), (x_tok_hbm.at[:, pl.ds(begin, columns)], x_tok),
             )
             return [pltpu.make_async_copy(a, b, local_sem.at[i]) for i, (a, b) in enumerate(pairs)]
 
@@ -1039,7 +1060,7 @@
             advance(0)
 
         for k in range(1, last):
-            at_plane = [m for m in range(dp_count - 1) if k == max(units - 4 + m * expert_count, 1)]
+            at_plane = [m for m in range(dp_count - 1) if k == max(units - 3 + m * expert_count, 1)]
             at_core = [m for m in range(dp_count - 1) if k == units - 1 + m * expert_count]
             if not (k <= 2 or at_plane or at_core or any(k in when for _, when in plan)):
                 continue
@@ -1081,8 +1102,8 @@
                 e = me_e * local + part * batch + j
                 weight = weights[pl.ds(e, 1), :].astype(BF) if gated else jnp.ones((), BF)
                 onehot[part, j * capacity : (j + 1) * capacity, :] = placed(slot_id, ranks[pl.ds(e, 1), :], weight)
-        load(source, unit, slot).wait()
-        for part in range(local // batch):
+            if part == 0:
+                load(source, unit, slot).wait()
             moved = dot(onehot[part], buf[slot]).astype(BF)
             target_ref[part * batch : (part + 1) * batch, 0] = moved.reshape(batch, capacity, width)
 
@@ -1280,7 +1301,10 @@
     )(wg, wu, wd, *[xs for xs, _ in slots], *[ys for _, ys in slots], *more)
 
 
-def unpack_kernel(sums_ref, q_ref, k_ref, v_ref, heads_ref, router_ref, gain_ref):
+def unpack_kernel(
+    sums_ref, gain1_rows_ref, block_in, input_in,
+    q_ref, k_ref, v_ref, heads_ref, router_ref, gain_ref, gain1_ref, block_ref, input_ref,
+):
     ways = sums_ref.shape[0]
     d_rows, h_rows, s_rows = q_ref.shape[0] // ways, heads_ref.shape[0] // ways, SMALL_ROWS // ways
     q_width, k_width, half = q_ref.shape[1], k_ref.shape[1], heads_ref.shape[1] // 2
@@ -1298,10 +1322,14 @@
     small = jnp.concatenate(small, axis=0)
     router_ref[:, :half] = small[:EXPERTS]
     router_ref[:, half:] = small[EXPERTS : 2 * EXPERTS]
-    gain_ref[...] = small[2 * EXPERTS : 2 * EXPERTS + 2]
-
-
-def unpack_call(sums, q_width, k_width, heads_shape):
+    gain_ref[0:half] = small[2 * EXPERTS]
+    gain_ref[half:] = small[2 * EXPERTS + 1]
+    gain1_ref[...] = gain1_rows_ref[0]
+    block_ref[...] = block_in[...]
+    input_ref[...] = input_in[...]
+
+
+def unpack_call(sums, gain1_rows, block, grad, q_width, k_width, heads_shape):
     ways = sums.shape[0]
     width = heads_shape[1]
     shape = jax.ShapeDtypeStruct
@@ -1309,14 +1337,14 @@
         unpack_kernel,
         out_shape=(
             shape((width, q_width), F32), shape((width, k_width), F32), shape((width, k_width), F32), shape(heads_shape, F32),
-            shape((EXPERTS, width), F32), shape((2, width // 2), F32),
+            shape((EXPERTS, width), F32), shape((width,), F32), shape((width,), F32), shape(block.shape, BF), shape(grad.shape, BF),
         ),
-        in_specs=vmem(1),
-        out_specs=tuple(vmem(6)),
-        compiler_params=params(32),
+        in_specs=vmem(4),
+        out_specs=tuple(vmem(9)),
+        compiler_params=params(60),
         cost_estimate=pl.CostEstimate(flops=MIB, bytes_accessed=5 * MIB, transcendentals=0),
         name="unpack",
-    )(sums)
+    )(sums, gain1_rows, block, grad)
 
 
 def on_device(
@@ -1370,12 +1398,13 @@
             tuple(range(1, dp_count)), x_other, dy_other, tables, gates, local,
             (dense, heads_grad, small, first, out_passed[0], hidden_grad, tokens, stat, scale, gain1),
         )
-        gain1_sum = gain1_rows[0]
         ways = expert_count * dp_count
         sums = lax.all_gather(sums, rows_all, axis=0)
         gate_grad, up_grad, down_grad = weights_call([(xs_own, ys_own), (xs, ys)], w_gate, w_up, w_down)
-        q_sum, k_sum, v_sum, out_sum, router_rows, gain2_rows = unpack_call(sums, q_width, k_width, w_out.shape)
-        router_sum, gain2_sum = router_rows.T, gain2_rows.reshape(width)
+        q_sum, k_sum, v_sum, out_sum, router_rows, gain2_sum, gain1_sum, block_out, input_grad = unpack_call(
+            sums, gain1_rows, block_out, input_grad, q_width, k_width, w_out.shape
+        )
+        router_sum = router_rows.T
     else:
         grads = weights_call([(xs_own, ys_own)], w_gate, w_up, w_down)
         for mask in range(1, dp_count):
@@ -1408,7 +1437,7 @@
             return lax.dynamic_slice_in_dim(values, tensor_index * columns, columns, -1).astype(F32)
 
         input_grad = (
-            cols(hidden_grad) + scale[:, :1] * (first_sum * cols(gain1) - cols(tokens) * scale[:, :1] * mean)
+            hidden_grad.astype(F32) + scale[:, :1] * (first_sum * cols(gain1) - cols(tokens) * scale[:, :1] * mean)
         ).astype(BF)
     return (
         block_out, input_grad, gain1_sum, q_sum, k_sum, v_sum, out_sum, gain2_sum, router_sum,

time: 251 us -> 244 us (0.972)
  local copies, waits for them, and re-layouts: 4.81 us -> 0 us
  Pallas kernels: 232 us -> 228 us
    pallas_call x1, Pallas kernels: 53.9 us -> 49.9 us  [slots_call(): pl.pallas_call(functools.partial(slots_kernel, sizes, masks, capacity, lo...]
    unnamed x9 -> x0, local copies, waits for them, and re-layouts: 3.46 us -> none
  transfers between devices with their start and end apart: 1 -> 1, of which waited for: 0 -> 1; matrix products, arithmetic and copies ran while one was open for 1% -> 0% of each run, Pallas kernels for 17% -> 18%
where the time goes in v5:
time: 244 us
  Pallas kernels  228 us (93%)
  between operations  14.1 us (6%)
    pallas_call x1, Pallas kernels, slots_call(): pl.pallas_call(functools.partial(slots_kernel, sizes, masks, capacity, lo...  49.9 us
    pallas_call x1, Pallas kernels, own_call(): pl.pallas_call(functools.partial(own_kernel, sizes, groups, capacity, loc...  47.1 us
    pallas_call x1, Pallas kernels, front(): pl.pallas_call(functools.partial(front_kernel, sizes), out_shape=(shape((...  44 us
    pallas_call x1, Pallas kernels, weights_call(): pl.pallas_call(functools.partial(weights_kernel, counts, chunks, capacity...  42.8 us
    pallas_call x1, Pallas kernels, back_call(): pl.pallas_call(functools.partial(back_kernel, (group_count, tensor_count,...  40.5 us
  transfers between devices with their start and end apart: 1, of which 1 were waited for; matrix products, arithmetic and copies ran while one was open for 0% of the time, Pallas kernels for 18%

profile of v5, /device:TPU:0, one launch (start us, length us, event | category | flops | bytes accessed | tf_op | source)
XLA Modules:
  0.0 243.5 jit_solution(10257178953594984880)
XLA Ops:
  7.2 0.0 all-gather.3.cloned.1.call-start
  7.2 44.0 %front.1 = (bf16[512,1024]{1,0:T(8,128)(2,1)}, bf16[512,256]{1,0:T(8,128)(2,1)}, bf16[512,128]{1,0:T(8,128)(2,1)}, bf16[512,128]{1,0:T(8,128)(2,1)}, bf16[512,25...) custom-call(s32[1,4]{1,0:T(1,128)} %lengths_ref.3, ...), custom_call_target="tpu_custom_call" | custom-call | flops 1048576 | bytes 1048576 | tf_op jit(solution)/shard_map/front/pallas_call | solution.py:382
  51.2 47.1 %experts_own.1 = (bf16[2,4,512,256]{3,2,1,0:T(8,128)(2,1)}, bf16[2,512,1152]{2,1,0:T(8,128)(2,1)}, bf16[16,2,128,1024]{3,2,1,0:T(8,128)(2,1)}, bf16[16,2,128,102...) custom-call(bf16[2,512,1024]{2,1,0:T(8,128)(2,1)} %get-tuple-element, ...), custom_call_target="tpu_custom_call" | custom-call | flops 1048576 | bytes 1048576 | tf_op jit(solution)/shard_map/experts_own/pallas_call | solution.py:899
  98.4 40.5 %back.1 = (bf16[4,512,256]{2,1,0:T(8,128)(2,1)}, f32[8,1536]{1,0:T(8,128)}, bf16[512,256]{1,0:T(8,128)(2,1)}, f32[512,128]{1,0:T(8,128)}, bf16[1024,512]{1,0:T(8...) custom-call(s32[1,4]{1,0:T(1,128)} %lengths_ref.3, ...), custom_call_target="tpu_custom_call" | custom-call | flops 1048576 | bytes 1048576 | tf_op jit(solution)/shard_map/back/pallas_call | solution.py:611
  138.9 49.9 %slots.1 = (bf16[3,2,512,1024]{3,2,1,0:T(8,128)(2,1)}, bf16[16,6,128,1024]{3,2,1,0:T(8,128)(2,1)}, bf16[16,6,128,1024]{3,2,1,0:T(8,128)(2,1)}, bf16[208,512]{1,0...) custom-call(bf16[3,2,512,1024]{3,2,1,0:T(8,128)(2,1)} %get-tuple-ele, ...), custom_call_target="tpu_custom_call", output_to_operand_aliasing={{0}: (0, {})} | custom-call | flops 1048576 | bytes 1048576 | tf_op jit(solution)/shard_map/slots/pallas_call | solution.py:1200
  188.8 0.0 all-gather.3.cloned.1.call-update
  188.8 42.8 %weights.1 = (f32[16,1024,128]{2,1,0:T(8,128)}, f32[16,1024,128]{2,1,0:T(8,128)}, f32[16,128,1024]{2,1,0:T(8,128)}) custom-call(bf16[16,1024,128]{2,1,0:T(8,128)(2,1)} %wg_ref.3, bf16[16,1024,128]{2,1,0:T(8,128)(2,1)} %wu_ref.3, bf16[16,128,1024]{2,1,0:T(8,128)(2,1)} %wd_ref.3, bf16[16,2,128,1024]{3,2,1,0:T(8,128)(2,1)} %get-tuple-element.95.rest_0_, ...), custom_call_target="tpu_custom_call" | custom-call | flops 80000000000 | bytes 104857600 | tf_op jit(solution)/shard_map/weights/pallas_call | solution.py:1291
  231.6 1.5 all-gather.3.cloned.1.call-done
  233.2 3.5 %unpack.1 = (f32[1024,256]{1,0:T(8,128)}, f32[1024,128]{1,0:T(8,128)}, f32[1024,128]{1,0:T(8,128)}, f32[256,1024]{1,0:T(8,128)}, f32[32,1024]{1,0:T(8,128)}, /*i...) custom-call(bf16[8,208,512]{2,1,0:T(8,128)(2,1)} %bitcast.4, ...), custom_call_target="tpu_custom_call" | custom-call | flops 1048576 | bytes 5242880 | tf_op jit(solution)/shard_map/unpack/pallas_call | solution.py:1336
Async XLA Ops:
  7.2 226.0 %all-gather.3.cloned.1.call-start = ((), (), s32[]{:S(2)}) async-start(), calls=%async_computation | async-start | bytes 1916928 | tf_op jit(solution)/shard_map/all_gather | solution.py:1402
Sparse Core Ops, SparseCore 0:
  188.9 44.1 all-gather.2

commit v6 on v5

--- a/solution.py
+++ b/solution.py
@@ -238,9 +238,21 @@
 def front_kernel(
     sizes,
     lengths_ref, order_of_ref, x_ref, gain_ref, wq_ref, wk_ref, wv_ref, wo_ref, cos_ref, sin_ref, gain2_ref, routes_ref, order_ref, dy_ref,
-    normed_ref, q_ref, k_ref, v_ref, heads_ref, logsum_ref, hidden_ref, share_ref, tables_ref, far_dy_ref, xown_ref, dyown_ref,
+    normed_out, q_out, k_out, v_out, heads_out, logsum_out, hidden_out, share_out, tables_ref, far_dy_ref, xown_ref, dyown_ref,
     part, landing, send_sem, recv_sem, local_sem,
+    normed_ref, q_ref, k_ref, v_ref, heads_ref, logsum_ref, hidden_ref, share_ref,
+    wq_late, wk_late, wv_late, wo_late, cos_late, sin_late, late_sem, early_sem,
 ):
+    late = [pltpu.make_async_copy(a, b, late_sem.at[i]) for i, (a, b) in enumerate((
+        (wq_ref, wq_late), (wk_ref, wk_late), (wv_ref, wv_late), (wo_ref, wo_late), (cos_ref, cos_late), (sin_ref, sin_late),
+    ))]
+    for copy in late:
+        copy.start()
+    early = [pltpu.make_async_copy(a, b, early_sem.at[i]) for i, (a, b) in enumerate((
+        (normed_ref, normed_out), (q_ref, q_out), (k_ref, k_out), (v_ref, v_out), (heads_ref, heads_out),
+        (logsum_ref, logsum_out), (hidden_ref, hidden_out), (share_ref, share_out),
+    ))]
+    wq_ref, wk_ref, wv_ref, wo_ref, cos_ref, sin_ref = wq_late, wk_late, wv_late, wo_late, cos_late, sin_late
     expert_count, tensor_count, dp_count = sizes
     rows, width = x_ref.shape
     share = rows // tensor_count
@@ -266,6 +278,8 @@
     scale = lax.rsqrt(jnp.mean(x * x, axis=-1, keepdims=True) + EPS)
     normed = (x * scale * gain_ref[...].astype(F32)[None, :]).astype(BF)
     normed_ref[...] = normed
+    for copy in late:
+        copy.wait()
     cosine, sine = cos_ref[...], sin_ref[...]
     lane = lanes((rows, 128))
     low_half = lane % HEAD_DIM < HEAD_DIM // 2
@@ -302,6 +316,8 @@
     live = (sublanes((rows, 1)) < length).astype(F32)
     part[...] = (dot(heads_ref[...], wo_ref[...]) * live).astype(BF).reshape(part.shape)
 
+    for copy in early[:6]:
+        copy.start()
     attn = Reduce(
         net, lambda re, rt: part.at[flip(me_t, rt)], lambda i: landing.at[i], tensor_bits,
         [(0, r) for r in range(tensor_count)],
@@ -336,6 +352,8 @@
     share_ref[...] = (hidden * scale2 * gain2_ref[...].astype(F32)[None, :]).astype(BF)
     keep_x = pltpu.make_async_copy(share_ref, xown_ref.at[me_e, pl.ds(start, share)], local_sem.at[1])
     keep_x.start()
+    for copy in early[6:]:
+        copy.start()
     high_bits = tensor_bits[1:][::-1]
     gathers = []
     for part_index, steps in enumerate((high_bits + expert_bits, expert_bits + high_bits)):
@@ -370,6 +388,8 @@
     net.close()
     keep_dy.wait()
     keep_x.wait()
+    for copy in early:
+        copy.wait()
 
 
 def front(lengths, order_of, x, gain, wq, wk, wv, wo, cosine, sine, gain2, routes, order, dy):
@@ -379,6 +399,7 @@
     share = rows // tensor_count
     shape = jax.ShapeDtypeStruct
     copies = 96
+    anywhere = pl.BlockSpec(memory_space=pl.ANY)
     return pl.pallas_call(
         functools.partial(front_kernel, sizes),
         out_shape=(
@@ -387,14 +408,20 @@
             shape((share, width), F32), shape((share, width), BF), shape((expert_count, dp_count, TABLE_ROWS, rows), BF),
             shape((dp_count - 1, share, width), BF), shape((expert_count, rows, width), BF), shape((expert_count, rows, width), BF),
         ),
-        in_specs=[pl.BlockSpec(memory_space=pltpu.SMEM)] * 2 + vmem(11) + [pl.BlockSpec(memory_space=pl.ANY)],
-        out_specs=tuple(vmem(10)) + (pl.BlockSpec(memory_space=pl.ANY),) * 2,
+        in_specs=[pl.BlockSpec(memory_space=pltpu.SMEM)] * 2 + vmem(2) + [anywhere] * 6 + vmem(3) + [anywhere],
+        out_specs=(anywhere,) * 8 + (vmem()[0],) + (anywhere,) * 3,
         scratch_shapes=[
             pltpu.VMEM((tensor_count, share, width), BF),
             pltpu.VMEM((tensor_count - 1, share, width), BF),
             pltpu.SemaphoreType.DMA((copies,)),
             pltpu.SemaphoreType.DMA((copies,)),
             pltpu.SemaphoreType.DMA((2,)),
+            pltpu.VMEM((rows, width), BF), pltpu.VMEM((rows, wq.shape[1]), BF), pltpu.VMEM((rows, wk.shape[1]), BF),
+            pltpu.VMEM((rows, wv.shape[1]), BF), pltpu.VMEM((rows, wq.shape[1]), BF), pltpu.VMEM((rows, 128), F32),
+            pltpu.VMEM((share, width), F32), pltpu.VMEM((share, width), BF),
+            *[pltpu.VMEM(values.shape, values.dtype) for values in (wq, wk, wv, wo, cosine, sine)],
+            pltpu.SemaphoreType.DMA((6,)),
+            pltpu.SemaphoreType.DMA((8,)),
         ],
         compiler_params=params(56, collective_id=1, has_side_effects=True),
         cost_estimate=pl.CostEstimate(flops=MIB, bytes_accessed=MIB, transcendentals=0),

time: 244 us -> 243 us (level)
  no operation moved by 1% of the time
where the time goes in v6:
time: 243 us; the launch traced here: 242 us
  Pallas kernels  227 us (93%)
  between operations  14.1 us (6%)
    pallas_call x1, Pallas kernels, slots_call(): pl.pallas_call(functools.partial(slots_kernel, sizes, masks, capacity, lo...  49.9 us
    pallas_call x1, Pallas kernels, own_call(): pl.pallas_call(functools.partial(own_kernel, sizes, groups, capacity, loc...  47.1 us
    pallas_call x1, Pallas kernels, front(): pl.pallas_call(functools.partial(front_kernel, sizes), out_shape=(shape((...  42.9 us
    pallas_call x1, Pallas kernels, weights_call(): pl.pallas_call(functools.partial(weights_kernel, counts, chunks, capacity...  42.8 us
    pallas_call x1, Pallas kernels, back_call(): pl.pallas_call(functools.partial(back_kernel, (group_count, tensor_count,...  40.6 us
  transfers between devices with their start and end apart: 1, of which 1 were waited for; matrix products, arithmetic and copies ran while one was open for 0% of the time, Pallas kernels for 18%

profile of v6, /device:TPU:0, one launch (start us, length us, event | category | flops | bytes accessed | tf_op | source)
XLA Modules:
  0.0 242.5 jit_solution(7513979934252767053)
XLA Ops:
  7.2 0.0 all-gather.3.cloned.1.call-start
  7.2 42.9 %front.1 = (bf16[512,1024]{1,0:T(8,128)(2,1)}, bf16[512,256]{1,0:T(8,128)(2,1)}, bf16[512,128]{1,0:T(8,128)(2,1)}, bf16[512,128]{1,0:T(8,128)(2,1)}, bf16[512,25...) custom-call(s32[1,4]{1,0:T(1,128)} %lengths_ref.3, ...), custom_call_target="tpu_custom_call" | custom-call | flops 1048576 | bytes 1048576 | tf_op jit(solution)/shard_map/front/pallas_call | solution.py:403
  50.1 47.1 %experts_own.1 = (bf16[2,4,512,256]{3,2,1,0:T(8,128)(2,1)}, bf16[2,512,1152]{2,1,0:T(8,128)(2,1)}, bf16[16,2,128,1024]{3,2,1,0:T(8,128)(2,1)}, bf16[16,2,128,102...) custom-call(bf16[2,512,1024]{2,1,0:T(8,128)(2,1)} %get-tuple-element, ...), custom_call_target="tpu_custom_call" | custom-call | flops 1048576 | bytes 1048576 | tf_op jit(solution)/shard_map/experts_own/pallas_call | solution.py:926
  97.3 40.6 %back.1 = (bf16[4,512,256]{2,1,0:T(8,128)(2,1)}, f32[8,1536]{1,0:T(8,128)}, bf16[512,256]{1,0:T(8,128)(2,1)}, f32[512,128]{1,0:T(8,128)}, bf16[1024,512]{1,0:T(8...) custom-call(s32[1,4]{1,0:T(1,128)} %lengths_ref.3, ...), custom_call_target="tpu_custom_call" | custom-call | flops 1048576 | bytes 1048576 | tf_op jit(solution)/shard_map/back/pallas_call | solution.py:638
  137.8 49.9 %slots.1 = (bf16[3,2,512,1024]{3,2,1,0:T(8,128)(2,1)}, bf16[16,6,128,1024]{3,2,1,0:T(8,128)(2,1)}, bf16[16,6,128,1024]{3,2,1,0:T(8,128)(2,1)}, bf16[208,512]{1,0...) custom-call(bf16[3,2,512,1024]{3,2,1,0:T(8,128)(2,1)} %get-tuple-ele, ...), custom_call_target="tpu_custom_call", output_to_operand_aliasing={{0}: (0, {})} | custom-call | flops 1048576 | bytes 1048576 | tf_op jit(solution)/shard_map/slots/pallas_call | solution.py:1227
  187.7 0.0 all-gather.3.cloned.1.call-update
  187.8 42.8 %weights.1 = (f32[16,1024,128]{2,1,0:T(8,128)}, f32[16,1024,128]{2,1,0:T(8,128)}, f32[16,128,1024]{2,1,0:T(8,128)}) custom-call(bf16[16,1024,128]{2,1,0:T(8,128)(2,1)} %wg_ref.3, bf16[16,1024,128]{2,1,0:T(8,128)(2,1)} %wu_ref.3, bf16[16,128,1024]{2,1,0:T(8,128)(2,1)} %wd_ref.3, bf16[16,2,128,1024]{3,2,1,0:T(8,128)(2,1)} %get-tuple-element.95.rest_0_, ...), custom_call_target="tpu_custom_call" | custom-call | flops 80000000000 | bytes 104857600 | tf_op jit(solution)/shard_map/weights/pallas_call | solution.py:1318
  230.6 1.5 all-gather.3.cloned.1.call-done
  232.1 3.5 %unpack.1 = (f32[1024,256]{1,0:T(8,128)}, f32[1024,128]{1,0:T(8,128)}, f32[1024,128]{1,0:T(8,128)}, f32[256,1024]{1,0:T(8,128)}, f32[32,1024]{1,0:T(8,128)}, /*i...) custom-call(bf16[8,208,512]{2,1,0:T(8,128)(2,1)} %bitcast.4, ...), custom_call_target="tpu_custom_call" | custom-call | flops 1048576 | bytes 5242880 | tf_op jit(solution)/shard_map/unpack/pallas_call | solution.py:1363
Async XLA Ops:
  7.2 224.9 %all-gather.3.cloned.1.call-start = ((), (), s32[]{:S(2)}) async-start(), calls=%async_computation | async-start | bytes 1916928 | tf_op jit(solution)/shard_map/all_gather | solution.py:1429
Sparse Core Ops, SparseCore 0:
  187.9 44.1 all-gather.2

commit v7 on v6

--- a/solution.py
+++ b/solution.py
@@ -1330,8 +1330,13 @@
 
 def unpack_kernel(
     sums_ref, gain1_rows_ref, block_in, input_in,
-    q_ref, k_ref, v_ref, heads_ref, router_ref, gain_ref, gain1_ref, block_ref, input_ref,
+    q_ref, k_ref, v_ref, heads_ref, router_ref, gain_ref, gain1_ref, block_ref, input_ref, sem,
 ):
+    moves = [
+        pltpu.make_async_copy(block_in, block_ref, sem.at[0]), pltpu.make_async_copy(input_in, input_ref, sem.at[1]),
+    ]
+    for copy in moves:
+        copy.start()
     ways = sums_ref.shape[0]
     d_rows, h_rows, s_rows = q_ref.shape[0] // ways, heads_ref.shape[0] // ways, SMALL_ROWS // ways
     q_width, k_width, half = q_ref.shape[1], k_ref.shape[1], heads_ref.shape[1] // 2
@@ -1352,8 +1357,8 @@
     gain_ref[0:half] = small[2 * EXPERTS]
     gain_ref[half:] = small[2 * EXPERTS + 1]
     gain1_ref[...] = gain1_rows_ref[0]
-    block_ref[...] = block_in[...]
-    input_ref[...] = input_in[...]
+    for copy in moves:
+        copy.wait()
 
 
 def unpack_call(sums, gain1_rows, block, grad, q_width, k_width, heads_shape):
@@ -1366,8 +1371,9 @@
             shape((width, q_width), F32), shape((width, k_width), F32), shape((width, k_width), F32), shape(heads_shape, F32),
             shape((EXPERTS, width), F32), shape((width,), F32), shape((width,), F32), shape(block.shape, BF), shape(grad.shape, BF),
         ),
-        in_specs=vmem(4),
-        out_specs=tuple(vmem(9)),
+        in_specs=vmem(2) + [pl.BlockSpec(memory_space=pl.ANY)] * 2,
+        out_specs=tuple(vmem(7)) + (pl.BlockSpec(memory_space=pl.ANY),) * 2,
+        scratch_shapes=[pltpu.SemaphoreType.DMA((2,))],
         compiler_params=params(60),
         cost_estimate=pl.CostEstimate(flops=MIB, bytes_accessed=5 * MIB, transcendentals=0),
         name="unpack",

time: 243 us -> 259 us (1.066)
  Pallas kernels: 227 us -> 243 us
    pallas_call x1, Pallas kernels: 3.53 us -> 20.2 us  [unpack_call(): pl.pallas_call(unpack_kernel, out_shape=(shape((width, q_width), F32), sh...]
  transfers between devices with their start and end apart: 1 -> 1, of which waited for: 1 -> 1; matrix products, arithmetic and copies ran while one was open for 0% -> 0% of each run, Pallas kernels for 18% -> 17%
where the time goes in v7:
time: 259 us
  Pallas kernels  243 us (94%)
  between operations  14.1 us (5%)
    pallas_call x1, Pallas kernels, slots_call(): pl.pallas_call(functools.partial(slots_kernel, sizes, masks, capacity, lo...  49.9 us
    pallas_call x1, Pallas kernels, own_call(): pl.pallas_call(functools.partial(own_kernel, sizes, groups, capacity, loc...  47.1 us
    pallas_call x1, Pallas kernels, front(): pl.pallas_call(functools.partial(front_kernel, sizes), out_shape=(shape((...  42.9 us
    pallas_call x1, Pallas kernels, weights_call(): pl.pallas_call(functools.partial(weights_kernel, counts, chunks, capacity...  42.8 us
    pallas_call x1, Pallas kernels, back_call(): pl.pallas_call(functools.partial(back_kernel, (group_count, tensor_count,...  40.6 us
    pallas_call x1, Pallas kernels, unpack_call(): pl.pallas_call(unpack_kernel, out_shape=(shape((width, q_width), F32), sh...  20.2 us
  transfers between devices with their start and end apart: 1, of which 1 were waited for; matrix products, arithmetic and copies ran while one was open for 0% of the time, Pallas kernels for 17%

profile of v7, /device:TPU:0, one launch (start us, length us, event | category | flops | bytes accessed | tf_op | source)
XLA Modules:
  0.0 259.1 jit_solution(13270867283271008982)
XLA Ops:
  7.2 0.0 all-gather.3.cloned.1.call-start
  7.2 42.9 %front.1 = (bf16[512,1024]{1,0:T(8,128)(2,1)}, bf16[512,256]{1,0:T(8,128)(2,1)}, bf16[512,128]{1,0:T(8,128)(2,1)}, bf16[512,128]{1,0:T(8,128)(2,1)}, bf16[512,25...) custom-call(s32[1,4]{1,0:T(1,128)} %lengths_ref.3, ...), custom_call_target="tpu_custom_call" | custom-call | flops 1048576 | bytes 1048576 | tf_op jit(solution)/shard_map/front/pallas_call | solution.py:403
  50.1 47.1 %experts_own.1 = (bf16[2,4,512,256]{3,2,1,0:T(8,128)(2,1)}, bf16[2,512,1152]{2,1,0:T(8,128)(2,1)}, bf16[16,2,128,1024]{3,2,1,0:T(8,128)(2,1)}, bf16[16,2,128,102...) custom-call(bf16[2,512,1024]{2,1,0:T(8,128)(2,1)} %get-tuple-element, ...), custom_call_target="tpu_custom_call" | custom-call | flops 1048576 | bytes 1048576 | tf_op jit(solution)/shard_map/experts_own/pallas_call | solution.py:926
  97.3 40.6 %back.1 = (bf16[4,512,256]{2,1,0:T(8,128)(2,1)}, f32[8,1536]{1,0:T(8,128)}, bf16[512,256]{1,0:T(8,128)(2,1)}, f32[512,128]{1,0:T(8,128)}, bf16[1024,512]{1,0:T(8...) custom-call(s32[1,4]{1,0:T(1,128)} %lengths_ref.3, ...), custom_call_target="tpu_custom_call" | custom-call | flops 1048576 | bytes 1048576 | tf_op jit(solution)/shard_map/back/pallas_call | solution.py:638
  137.8 49.9 %slots.1 = (bf16[3,2,512,1024]{3,2,1,0:T(8,128)(2,1)}, bf16[16,6,128,1024]{3,2,1,0:T(8,128)(2,1)}, bf16[16,6,128,1024]{3,2,1,0:T(8,128)(2,1)}, bf16[208,512]{1,0...) custom-call(bf16[3,2,512,1024]{3,2,1,0:T(8,128)(2,1)} %get-tuple-ele, ...), custom_call_target="tpu_custom_call", output_to_operand_aliasing={{0}: (0, {})} | custom-call | flops 1048576 | bytes 1048576 | tf_op jit(solution)/shard_map/slots/pallas_call | solution.py:1227
  187.7 0.0 all-gather.3.cloned.1.call-update
  187.8 42.8 %weights.1 = (f32[16,1024,128]{2,1,0:T(8,128)}, f32[16,1024,128]{2,1,0:T(8,128)}, f32[16,128,1024]{2,1,0:T(8,128)}) custom-call(bf16[16,1024,128]{2,1,0:T(8,128)(2,1)} %wg_ref.3, bf16[16,1024,128]{2,1,0:T(8,128)(2,1)} %wu_ref.3, bf16[16,128,1024]{2,1,0:T(8,128)(2,1)} %wd_ref.3, bf16[16,2,128,1024]{3,2,1,0:T(8,128)(2,1)} %get-tuple-element.95.rest_0_, ...), custom_call_target="tpu_custom_call" | custom-call | flops 80000000000 | bytes 104857600 | tf_op jit(solution)/shard_map/weights/pallas_call | solution.py:1318
  230.6 1.5 all-gather.3.cloned.1.call-done
  232.1 20.2 %unpack.1 = (f32[1024,256]{1,0:T(8,128)}, f32[1024,128]{1,0:T(8,128)}, f32[1024,128]{1,0:T(8,128)}, f32[256,1024]{1,0:T(8,128)}, f32[32,1024]{1,0:T(8,128)}, /*i...) custom-call(bf16[8,208,512]{2,1,0:T(8,128)(2,1)} %bitcast.4, ...), custom_call_target="tpu_custom_call" | custom-call | flops 1048576 | bytes 5242880 | tf_op jit(solution)/shard_map/unpack/pallas_call | solution.py:1368
Async XLA Ops:
  7.2 224.9 %all-gather.3.cloned.1.call-start = ((), (), s32[]{:S(2)}) async-start(), calls=%async_computation | async-start | bytes 1916928 | tf_op jit(solution)/shard_map/all_gather | solution.py:1435
Sparse Core Ops, SparseCore 0:
  187.9 44.1 all-gather.2
